TPU v7x, 32 devices: a whole 2x2x4 slice. The times are simulated.
32 devices in a mesh: ep: 8 (over z, y), tp: 4 (over x, core).
Axes of the slice: x: 2, y: 2, z: 4, core: 2. Of those that a mesh axis runs over, the one named last changes fastest.
Arguments:
- tokens: bfloat16 [2048, 3584], P('ep', 'tp'), may hold values from -6 to 6
- expert_ids: int32 [2048, 8], P('ep'), may hold values from 0 to 255, as said below
- gate_weight: bfloat16 [8, 3584, 2048], P('ep', None, 'tp'), may hold values from -0.09375 to 0.09375
- up_weight: bfloat16 [8, 3584, 2048], P('ep', None, 'tp'), may hold values from -0.09375 to 0.09375
Outputs:
- hidden: bfloat16 [8, 128, 2048], P('ep', None, 'tp')
- hessian: float32 [8, 2048, 2048], P('ep', 'tp')
Inputs may be any that keep to these rules, and one draw needn't show every extreme that they name: `expert_ids`: each row names 8 different experts. In the rows of one source block (one index of ep) every expert id appears 0, 8 or 16 times, and some expert id below 8 appears exactly 16 times in every source block.
All inputs are finite; a program needn't handle non-finite values.
Results may differ from a plain program's by a relative error of at most 0.0045.
Values may be sent and summed in bfloat16 or wider, within the bound.
No kernel may reach another device: no remote copies, remote signals or barrier semaphores. Data moves between devices by JAX's collectives and lax.ppermute only.
A program may use at most 64 MiB of HBM per device.

v0:
```python
import jax
import jax.numpy as jnp
from jax import lax
from jax.sharding import PartitionSpec as P

EXPERTS = 256
TOP = 8


def on_device(tokens, expert_ids, gate_weight, up_weight):
    groups = lax.axis_size("ep")
    tok_rows = tokens.shape[0]
    capacity = 2 * tok_rows * TOP // EXPERTS
    slot_count = groups * capacity
    targets = jnp.arange(groups, dtype=jnp.int32)
    member = jnp.any(expert_ids[:, :, None] == targets[None, None, :], axis=1).astype(jnp.int32)
    ranking = jnp.cumsum(member, axis=0) - 1
    slot_ids = jnp.arange(capacity, dtype=jnp.int32)
    chosen = (member.T[:, None, :] > 0) & (ranking.T[:, None, :] == slot_ids[None, :, None])
    selector = jnp.where(chosen, 1.0, 0.0).astype(jnp.bfloat16)
    outgoing = jnp.einsum(
        "gcj,jf->gcf", selector, tokens, preferred_element_type=jnp.float32
    ).astype(jnp.bfloat16)
    arrived = lax.all_to_all(outgoing, "ep", split_axis=0, concat_axis=0, tiled=True)
    arrived = arrived.reshape(slot_count, arrived.shape[2])
    local_gate = gate_weight[0]
    local_up = up_weight[0]
    routed = lax.all_gather(arrived, "tp", axis=1, tiled=True)
    gate_proj = jnp.dot(routed, local_gate, preferred_element_type=jnp.float32)
    up_proj = jnp.dot(routed, local_up, preferred_element_type=jnp.float32)
    hidden = (jax.nn.silu(gate_proj) * up_proj).astype(jnp.bfloat16)
    factor = 2.0 / slot_count
    hessian = (
        lax.dot_general(
            hidden,
            lax.all_gather(hidden, "tp", axis=1, tiled=True),
            (((0,), (0,)), ((), ())),
            preferred_element_type=jnp.float32,
        )
        * factor
    )
    return (hidden[None], hessian[None])


def solution(mesh):
    return jax.shard_map(
        on_device,
        mesh=mesh,
        in_specs=(P("ep", "tp"), P("ep", None), P("ep", None, "tp"), P("ep", None, "tp")),
        out_specs=(P("ep", None, "tp"), P("ep", "tp", None)),
        check_vma=False,
    )
```

profile of v0, /device:TPU:0, one launch (start us, length us, event | category | flops | bytes accessed | tf_op | source)
XLA Modules:
  0.0 41.1 jit_solution(13798919349103435407)
XLA Ops:
  0.6 0.0 copy-start
  0.6 0.8 %fusion.15 = pred[256,8]{0,1:T(8,128)(4,1)S(1)} fusion(s32[256,8]{0,1:T(8,128)} %param.5), kind=kLoop, calls=%fused_computation.16 | loop fusion | flops 30720 | bytes 10240 | tf_op jit(solution)/shard_map/reduce_or | solution.py:16
  1.4 0.6 %reduce-window.6 = s32[8,2,128]{2,0,1:T(8,128)S(1)} reduce-window(s32[8,2,128]{2,0,1:T(8,128)S(1)} %convert_bitcast_fusion, s32[]{:T(128)} %constant.4.clone.1), window={size=1x1x128 pad=0_0x0_0x127_0}, to_apply=%region_1.0 | reduce-window | flops 260096 | bytes 16388 | tf_op jit(solution)/shard_map/reduce-window
  2.0 0.2 slice_reduce_fusion
  2.3 0.0 copy-start.2
  2.3 0.1 add_bitcast_fusion
  2.4 0.0 copy-done
  2.4 0.2 convolution_convert_fusion
  2.6 15.8 %all_to_all.5 = bf16[8,16,896]{2,1,0:T(8,128)(2,1)S(1)} all-to-all(bf16[8,16,896]{2,1,0:T(8,128)(2,1)S(1)} %convolution_convert_fusion), channel_id=1, replica_groups=mesh['ep'=8,'tp'=4] {'ep'}, dimensions={0} | all-to-all | bytes 458752 | tf_op jit(solution)/shard_map/all_to_all | solution.py:24
  18.4 9.3 %all_gather.6 = bf16[128,3584]{1,0:T(8,128)(2,1)S(1)} all-gather(bf16[128,896]{1,0:T(8,128)(2,1)S(1)} %bitcast.30), channel_id=1, replica_groups=mesh['ep'=8,'tp'=4] {'tp'}, dimensions={1}, use_global_device_ids=true | all-gather | bytes 1146880 | tf_op jit(solution)/shard_map/all_gather | solution.py:28
  27.7 2.7 %fusion.2 = f32[128,512]{1,0:T(8,128)S(1)} fusion(bf16[128,3584]{1,0:T(8,128)(2,1)S(1)} %all_gather.6, bf16[1,3584,512]{2,1,0:T(8,128)(2,1)} %param.6), kind=kOutput, calls=%fused_computation.3 | convolution fusion | flops 469762048 | bytes 4849664 | tf_op jit(solution)/shard_map/dot_general | solution.py:29
  30.4 0.0 copy-done.2
  30.4 0.7 %fusion.7 = bf16[128,512]{1,0:T(8,128)(2,1)S(1)} fusion(bf16[128,3584]{1,0:T(8,128)(2,1)S(1)} %all_gather.6, bf16[1,3584,512]{2,1,0:T(8,128)(2,1)S(1)} %copy-done.2, f32[128,512]{1,0:T(8,128)S(1)} %fusion.2), kind=kOutput, calls=%fused_computation.7 | convolution fusion | flops 470155264 | bytes 4980736 | tf_op jit(solution)/shard_map/dot_general | solution.py:30
  31.0 0.0 copy-start.1
  31.0 7.3 %all_gather.7 = bf16[128,2048]{1,0:T(8,128)(2,1)S(1)} all-gather(bf16[128,512]{1,0:T(8,128)(2,1)S(1)} %fusion.7), channel_id=1, replica_groups=mesh['ep'=8,'tp'=4] {'tp'}, dimensions={1}, use_global_device_ids=true | all-gather | bytes 655360 | tf_op jit(solution)/shard_map/all_gather | solution.py:36
  38.3 2.7 %multiply_bitcast_fusion = f32[1,512,2048]{2,1,0:T(8,128)} fusion(bf16[128,512]{1,0:T(8,128)(2,1)S(1)} %fusion.7, bf16[128,2048]{1,0:T(8,128)(2,1)S(1)} %all_gather.7), kind=kOutput, calls=%fused_computation | convolution fusion | flops 269484032 | bytes 4849664 | tf_op jit(solution)/shard_map/dot_general | solution.py:34
  41.1 0.0 copy-done.1
  (4 shorter events, 0.1 us)
Async XLA Ops:
  0.6 1.7 %copy-start = (bf16[256,896]{1,0:T(8,128)(2,1)S(1)}, bf16[256,896]{1,0:T(8,128)(2,1)}, u32[]{:S(2)}) copy-start(bf16[256,896]{1,0:T(8,128)(2,1)} %param.4) | copy-start | bytes 1376260
  2.3 28.1 %copy-start.2 = (bf16[1,3584,512]{2,1,0:T(8,128)(2,1)S(1)}, bf16[1,3584,512]{2,1,0:T(8,128)(2,1)}, u32[]{:S(2)}) copy-start(bf16[1,3584,512]{2,1,0:T(8,128)(2,1)} %param.7) | copy-start | bytes 11010052
  31.0 10.1 %copy-start.1 = (bf16[128,512]{1,0:T(8,128)(2,1)}, bf16[128,512]{1,0:T(8,128)(2,1)S(1)}, u32[]{:S(2)}) copy-start(bf16[128,512]{1,0:T(8,128)(2,1)S(1)} %fusion.7) | copy-start | bytes 393220
where the time goes:
time: 41.3 us; the launch traced here: 41.1 us
  blocking collectives  32.4 us (78%)
  matrix products  6.31 us (15%)
  other arithmetic  1.47 us (4%)
  between operations  0.7 us (2%)
    all_to_all x1, blocking collectives, on_device(): lax.all_to_all(outgoing, 'ep', split_axis=0, concat_axis=0, tiled=True)  15.8 us
    all_gather x1, blocking collectives, on_device(): routed = lax.all_gather(arrived, 'tp', axis=1, tiled=True)  9.3 us
    all_gather x1, blocking collectives, on_device(): lax.all_gather(hidden, 'tp', axis=1, tiled=True)  7.3 us
    dot_general x1, matrix products, on_device(): lax.dot_general(hidden, lax.all_gather(hidden, 'tp', axis=1, tiled=True),...  2.75 us
    dot_general x1, matrix products, on_device(): gate_proj = jnp.dot(routed, local_gate, preferred_element_type=jnp.float32)  2.67 us

commit v1 on v0

v1 whole, which is shorter than its diff:
```python
import functools

import jax
import jax.numpy as jnp
from jax import lax
from jax.experimental import pallas as pl
from jax.experimental.pallas import tpu as pltpu
from jax.sharding import PartitionSpec as P

EXPERTS = 256
TOP = 8
BF16 = jnp.bfloat16
F32 = jnp.float32
VMEM = pl.BlockSpec(memory_space=pltpu.VMEM)
ANY = pl.BlockSpec(memory_space=pl.ANY)
HBM = pl.BlockSpec(memory_space=pltpu.HBM)
LIMIT = 48 * 1024 * 1024


def dot(a, b):
    return lax.dot_general(a, b, (((1,), (0,)), ((), ())), preferred_element_type=F32)


def select_kernel(groups, capacity, ids_hbm, tok_hbm, out_ref, ids_ref, tok_ref, sems):
    get_ids = pltpu.make_async_copy(ids_hbm, ids_ref, sems.at[0])
    get_tok = pltpu.make_async_copy(tok_hbm, tok_ref, sems.at[1])
    get_ids.start()
    get_tok.start()
    rows = ids_ref.shape[1]
    before = lax.broadcasted_iota(jnp.int32, (rows, rows), 0)
    after = lax.broadcasted_iota(jnp.int32, (rows, rows), 1)
    upto = jnp.where(before <= after, 1.0, 0.0).astype(BF16)
    want = lax.broadcasted_iota(jnp.int32, (8, capacity, rows), 1).astype(F32)
    get_ids.wait()
    ids = ids_ref[...]
    for base in range(0, groups, 8):
        expert = base + lax.broadcasted_iota(jnp.int32, (8, rows), 0)
        hit = ids[0:1, :] == expert
        for k in range(1, ids.shape[0]):
            hit = hit | (ids[k : k + 1, :] == expert)
        count = dot(jnp.where(hit, 1.0, 0.0).astype(BF16), upto)
        slot = jnp.where(hit, count - 1.0, -1.0)
        chosen = jnp.where(slot[:, None, :] == want, 1.0, 0.0)
        chosen = chosen.reshape(8 * capacity, rows).astype(BF16)
        if base == 0:
            get_tok.wait()
        out_ref[pl.ds(base * capacity, 8 * capacity), :] = dot(chosen, tok_ref[...]).astype(BF16)


def first_kernel(own_ref, sib_ref, gate_hbm, up_hbm, g_ref, u_ref, rest_ref, wbuf, sems):
    t = lax.axis_index("tp")
    depth = own_ref.shape[1]
    copies = []
    for n, slice_index in enumerate((t, t ^ 1, t ^ 2, t ^ 3)):
        at = pl.ds(pl.multiple_of(slice_index * depth, depth), depth)
        for m, w in enumerate((gate_hbm, up_hbm)):
            target = wbuf.at[n, m] if n < 2 else rest_ref.at[n - 2, m]
            copies.append(pltpu.make_async_copy(w.at[0, at, :], target, sems.at[n * 2 + m]))
    for c in copies:
        c.start()
    for n, block in enumerate((own_ref, sib_ref)):
        for m, total in enumerate((g_ref, u_ref)):
            copies[n * 2 + m].wait()
            part = dot(block[...], wbuf[n, m])
            if n == 0:
                total[...] = part
            else:
                total[...] += part
    for c in copies[4:]:
        c.wait()


def more_kernel(first, x_ref, rest_ref, g_in, u_in, g_ref, u_ref):
    at = pl.ds(first, x_ref.shape[0])
    g_ref[...] = g_in[at, :] + dot(x_ref[...], rest_ref[0, 0])
    u_ref[...] = u_in[at, :] + dot(x_ref[...], rest_ref[0, 1])


def last_kernel(d_ref, rest_ref, g_in, u_in, h_ref):
    gate = g_in[...] + dot(d_ref[...], rest_ref[1, 0])
    up = u_in[...] + dot(d_ref[...], rest_ref[1, 1])
    h_ref[...] = (gate / (1.0 + jnp.exp(-gate)) * up).astype(BF16)


def write_block(flip, h_ref, factor, index, hess_hbm, buf, sems):
    wide = h_ref.shape[1]
    part = wide // 4
    at = pl.ds(pl.multiple_of(index * wide, wide), wide)
    copies = []
    for i in range(4):
        rows = pl.ds(i * part, part)
        buf[rows, :] = dot(flip[rows, :], h_ref[...]) * factor
        copies.append(pltpu.make_async_copy(buf.at[rows, :], hess_hbm.at[0, rows, at], sems.at[i]))
        copies[-1].start()
    return copies


def near_kernel(factor, h_ref, sib_ref, flip_ref, hid_hbm, hess_hbm, buf, sems):
    t = lax.axis_index("tp")
    out = pltpu.make_async_copy(h_ref, hid_hbm.at[0], sems.at[2, 0])
    out.start()
    flip_ref[...] = h_ref[...].astype(F32).T.astype(BF16)
    copies = write_block(flip_ref, h_ref, factor, t, hess_hbm, buf.at[0], sems.at[0])
    copies += write_block(flip_ref, sib_ref, factor, t ^ 1, hess_hbm, buf.at[1], sems.at[1])
    out.wait()
    for c in copies:
        c.wait()


def other_kernel(factor, which, flip_ref, h_ref, hess_in, hess_hbm, buf, sems):
    t = lax.axis_index("tp")
    for c in write_block(flip_ref, h_ref, factor, t ^ which, hess_hbm, buf, sems):
        c.wait()


def call(kernel, out_shape, in_specs, out_specs, scratch=(), name=None, aliases={}, flops=0, moved=0):
    return pl.pallas_call(
        kernel,
        out_shape=out_shape,
        in_specs=in_specs,
        out_specs=out_specs,
        scratch_shapes=list(scratch),
        input_output_aliases=aliases,
        name=name,
        cost_estimate=pl.CostEstimate(flops=flops, bytes_accessed=moved, transcendentals=0),
        compiler_params=pltpu.CompilerParams(vmem_limit_bytes=LIMIT),
    )


def on_device(tokens, expert_ids, gate_weight, up_weight):
    groups = lax.axis_size("ep")
    tok_rows, depth = tokens.shape
    capacity = 2 * tok_rows * TOP // EXPERTS
    slots = groups * capacity
    wide = gate_weight.shape[2]
    full = wide * lax.axis_size("tp")
    S = jax.ShapeDtypeStruct
    D = pltpu.SemaphoreType.DMA
    outgoing = call(
        functools.partial(select_kernel, groups, capacity),
        S((slots, depth), BF16), [HBM, HBM], VMEM,
        (pltpu.VMEM(expert_ids.T.shape, jnp.int32), pltpu.VMEM(tokens.shape, BF16), D((2,))), name="select",
    )(expert_ids.T, tokens)
    own = lax.all_to_all(outgoing, "ep", split_axis=0, concat_axis=0, tiled=True)
    cores = [(i, i ^ 1) for i in range(4)]
    chips = [(i, i ^ 2) for i in range(4)]
    parts = 2
    size = slots // parts
    far = [lax.ppermute(own[i * size : (i + 1) * size], "tp", chips) for i in range(parts)]
    sib = lax.ppermute(own, "tp", cores)
    part = S((slots, wide), F32)
    weights = 4 * depth * wide * 2 * 2
    gate, up, rest = call(
        first_kernel,
        (part, part, pltpu.VMEM((2, 2, depth, wide), BF16)),
        [VMEM, VMEM, HBM, HBM], (VMEM, VMEM, VMEM),
        (pltpu.VMEM((2, 2, depth, wide), BF16), D((8,))), name="first",
        flops=8 * slots * depth * wide, moved=weights,
    )(own, sib, gate_weight, up_weight)
    *far, gate = lax.optimization_barrier((*far, gate))
    hidden = []
    some = S((size, wide), F32)
    for i in range(parts):
        diag = lax.ppermute(far[i], "tp", cores)
        g, u = call(
            functools.partial(more_kernel, i * size), (some, some), [VMEM] * 4, (VMEM, VMEM), name="more",
            flops=4 * slots * depth * wide, moved=weights // 16,
        )(far[i], rest, gate, up)
        hidden.append(call(
            last_kernel, S((size, wide), BF16), [VMEM] * 4, VMEM, name="last",
            flops=4 * slots * depth * wide, moved=weights // 16,
        )(diag, rest, g, u))
    hidden = jnp.concatenate(hidden)
    factor = 2.0 / slots
    hess_shape = S((1, wide, full), F32)
    far_h = lax.ppermute(hidden, "tp", chips)
    sib_h = lax.ppermute(hidden, "tp", cores)
    block = wide * wide * 4
    flip, hidden, hess = call(
        functools.partial(near_kernel, factor), (S((wide, slots), BF16), S((1, slots, wide), BF16), hess_shape),
        [VMEM, VMEM], (VMEM, ANY, ANY), (pltpu.VMEM((2, wide, wide), F32), D((3, 4))), name="near",
        flops=4 * slots * wide * wide, moved=2 * block,
    )(hidden, sib_h)

    def other(which, h, hess):
        return call(
            functools.partial(other_kernel, factor, which), hess_shape,
            [VMEM, VMEM, ANY], ANY, (pltpu.VMEM((wide, wide), F32), D((4,))), name="block_%d" % which, aliases={2: 0},
            flops=2 * slots * wide * wide, moved=block,
        )(flip, h, hess)

    far_h, flip = lax.optimization_barrier((far_h, flip))
    diag_h = lax.ppermute(far_h, "tp", cores)
    hess = other(2, far_h, hess)
    hess = other(3, diag_h, hess)
    return hidden, hess


def solution(mesh):
    return jax.shard_map(
        on_device,
        mesh=mesh,
        in_specs=(P("ep", "tp"), P("ep", None), P("ep", None, "tp"), P("ep", None, "tp")),
        out_specs=(P("ep", None, "tp"), P("ep", "tp", None)),
        check_vma=False,
    )
```

time: 41.3 us -> 37.8 us (0.915)
  blocking collectives: 32.4 us -> 15.5 us
  Pallas kernels: 0 us -> 9.65 us
  matrix products: 6.31 us -> 0 us
  waiting for transfers between devices: 0 us -> 5.67 us
  starting transfers between devices: 0 us -> 4.24 us
  local copies, waits for them, and re-layouts: 0.23 us -> 1.73 us
  other arithmetic: 1.47 us -> 0.01 us
    all_gather x2 -> x0, blocking collectives: 16.6 us -> none  [the longest x1 9.3 us: on_device(): routed = lax.all_gather(arrived, 'tp', axis=1, tiled=True)]
    pallas_call x0 -> x9, Pallas kernels: none -> 9.65 us  [the longest x1 3.17 us: on_device(): call(first_kernel, (part, part, pltpu.VMEM((2, 2, depth, wide), BF16)), [...]
    dot_general x4 -> x0, matrix products: 6.31 us -> none  [the longest x1 2.75 us: on_device(): lax.dot_general(hidden, lax.all_gather(hidden, 'tp', axis=1, tiled=True),...]
    ppermute x0 -> x8, waiting for transfers between devices: none -> 5.67 us  [the longest x2 2.81 us: on_device(): lax.ppermute(own[i * size:(i + 1) * size], 'tp', chips)]
    ppermute x0 -> x8, starting transfers between devices: none -> 4.24 us  [the longest x2 2.09 us: on_device(): lax.ppermute(own[i * size:(i + 1) * size], 'tp', chips)]
    unnamed x6 -> x4, local copies, waits for them, and re-layouts: 0.02 us -> 1.71 us
    reduce_or x1 -> x0, other arithmetic: 0.76 us -> none  [on_device(): jnp.any(expert_ids[:, :, None] == targets[None, None, :], axis=1)]
    another operation x2 -> x0, other arithmetic: 0.62 us -> none
  transfers between devices with their start and end apart: 0 -> 8, of which waited for: 0 -> 4; matrix products, arithmetic and copies ran while one was open for 0% -> 0% of each run, Pallas kernels for 0% -> 20%
where the time goes in v1:
time: 37.8 us; the launch traced here: 37.5 us
  blocking collectives  15.5 us (41%)
  Pallas kernels  9.65 us (26%)
  waiting for transfers between devices  5.67 us (15%)
  starting transfers between devices  4.24 us (11%)
  local copies, waits for them, and re-layouts  1.73 us (5%)
  between operations  0.74 us (2%)
    all_to_all x1, blocking collectives, on_device(): lax.all_to_all(outgoing, 'ep', split_axis=0, concat_axis=0, tiled=True)  15.5 us
    pallas_call x1, Pallas kernels, on_device(): call(first_kernel, (part, part, pltpu.VMEM((2, 2, depth, wide), BF16)), [...  3.17 us
    ppermute x2, waiting for transfers between devices, on_device(): lax.ppermute(own[i * size:(i + 1) * size], 'tp', chips)  2.81 us
    ppermute x1, waiting for transfers between devices, on_device(): far_h = lax.ppermute(hidden, 'tp', chips)  2.69 us
    pallas_call x2, Pallas kernels, other(): call(functools.partial(other_kernel, factor, which), hess_shape, [VMEM, V...  2.35 us
    ppermute x2, starting transfers between devices, on_device(): lax.ppermute(own[i * size:(i + 1) * size], 'tp', chips)  2.09 us
    unnamed x4, local copies, waits for them, and re-layouts  1.71 us
    pallas_call x1, Pallas kernels, on_device(): call(functools.partial(near_kernel, factor), (S((wide, slots), BF16), S((...  1.66 us
  transfers between devices with their start and end apart: 8, of which 4 were waited for; matrix products, arithmetic and copies ran while one was open for 0% of the time, Pallas kernels for 20%

profile of v1, /device:TPU:0, one launch (start us, length us, event | category | flops | bytes accessed | tf_op | source)
XLA Modules:
  0.0 37.5 jit_solution(13926863560549007732)
XLA Ops:
  0.6 0.0 copy-start
  0.6 1.0 %copy-done = bf16[256,896]{1,0:T(8,128)(2,1)S(1)} copy-done((bf16[256,896]{1,0:T(8,128)(2,1)S(1)}, bf16[256,896]{1,0:T(8,128)(2,1)}, u32[]{:S(2)}) %copy-start) | copy-done | bytes 458776
  1.6 0.0 copy-start.1
  1.7 0.7 %copy-done.1 = s32[256,8]{0,1:T(8,128)S(1)} copy-done((s32[256,8]{0,1:T(8,128)S(1)}, s32[256,8]{0,1:T(8,128)}, u32[]{:S(2)}) %copy-start.1) | copy-done | bytes 8216
  2.3 0.7 %select.1 = bf16[128,896]{1,0:T(8,128)(2,1)S(1)} custom-call(s32[8,256]{1,0:T(8,128)S(1)} %bitcast.8, bf16[256,896]{1,0:T(8,128)(2,1)S(1)} %copy-done), custom_call_target="tpu_custom_call" | custom-call | tf_op jit(solution)/shard_map/select/pallas_call | solution.py:139
  3.1 15.5 %all_to_all.11 = bf16[8,16,896]{2,1,0:T(8,128)(2,1)S(1)} all-to-all(bf16[8,16,896]{2,1,0:T(8,128)(2,1)S(1)} %bitcast.7), channel_id=1, replica_groups=mesh['ep'=8,'tp'=4] {'ep'}, dimensions={0} | all-to-all | bytes 458752 | tf_op jit(solution)/shard_map/all_to_all | solution.py:144
  18.6 0.0 collective-permute-start.2
  18.6 1.6 %collective-permute-start = (bf16[64,896]{1,0:T(8,128)(2,1)S(1)}, bf16[64,896]{1,0:T(8,128)(2,1)S(1)}, u32[]{:S(2)}, u32[]{:S(2)}) collective-permute-start(bf16[64,896]{1,0:T(8,128)(2,1)S(1)} %bitcast.10), channel_id=1, source_target_pairs={{0,2},{1,3},{2,0},{3,1},{4,6},{5,7},{6,4},{7,5},{8,10},{9,11},{10,... | collective-permute-start | bytes 344072 | tf_op jit(solution)/shard_map/ppermute | solution.py:149
  20.2 0.5 %collective-permute-start.1 = (bf16[64,896]{1,0:T(8,128)(2,1)S(1)}, bf16[64,896]{1,0:T(8,128)(2,1)S(1)}, u32[]{:S(2)}, u32[]{:S(2)}) collective-permute-start(bf16[64,896]{1,0:T(8,128)(2,1)S(1)} %bitcast.9), channel_id=1, source_target_pairs={{0,2},{1,3},{2,0},{3,1},{4,6},{5,7},{6,4},{7,5},{8,10},{9,11},{10,... | collective-permute-start | bytes 344072 | tf_op jit(solution)/shard_map/ppermute | solution.py:149
  20.7 0.0 collective-permute-done.2.sib_ref
  20.7 3.2 %first.1 = (f32[128,512]{1,0:T(8,128)S(1)}, f32[128,512]{1,0:T(8,128)S(1)}, bf16[2,2,896,512]{3,2,1,0:T(8,128)(2,1)S(1)}) custom-call(bf16[128,896]{1,0:T(8,128)(2,1)S(1)} %bitcast.6, bf16[128,896]{1,0:T(8,128)(2,1)S(1)} %collective-permute-done.2.sib_ref, bf16[1,3584,512]{2,1,0:T(8,128)(2,1)} %gate_hbm.1, bf16[1,3584,512]{2,1,0:T(8,128)(2,1)} %up_hbm.1), custom_call_target="tpu_custom_call" | custom-call | flops 469762048 | bytes 7340032 | tf_op jit(solution)/shard_map/first/pallas_call | solution.py:153
  23.9 0.7 %collective-permute-done.x_ref = bf16[64,896]{1,0:T(8,128)(2,1)S(1)} collective-permute-done((bf16[64,896]{1,0:T(8,128)(2,1)S(1)}, bf16[64,896]{1,0:T(8,128)(2,1)S(1)}, u32[]{:S(2)}, u32[]{:S(2)}) %collective-permute-start) | collective-permute-done | bytes 114720 | tf_op jit(solution)/shard_map/ppermute | solution.py:149
  24.6 2.1 %collective-permute-done.1.x_ref = bf16[64,896]{1,0:T(8,128)(2,1)S(1)} collective-permute-done((bf16[64,896]{1,0:T(8,128)(2,1)S(1)}, bf16[64,896]{1,0:T(8,128)(2,1)S(1)}, u32[]{:S(2)}, u32[]{:S(2)}) %collective-permute-start.1) | collective-permute-done | bytes 114720 | tf_op jit(solution)/shard_map/ppermute | solution.py:149
  26.7 0.0 collective-permute-start.4
  26.7 0.5 %collective-permute-start.3 = (bf16[64,896]{1,0:T(8,128)(2,1)S(1)}, bf16[64,896]{1,0:T(8,128)(2,1)S(1)}, u32[]{:S(2)}, u32[]{:S(2)}) collective-permute-start(bf16[64,896]{1,0:T(8,128)(2,1)S(1)} %collective-permute-done.x_ref), channel_id=1, source_target_pairs={{0,1},{1,0},{2,3},{3,2},{4,5},{5,4},{6,7},{7,6},{8,9},{9,8},{10,11... | collective-permute-start | bytes 344072 | tf_op jit(solution)/shard_map/ppermute | solution.py:164
  27.2 0.4 %more.2 = (f32[64,512]{1,0:T(8,128)S(1)}, f32[64,512]{1,0:T(8,128)S(1)}) custom-call(bf16[64,896]{1,0:T(8,128)(2,1)S(1)} %collective-permute-done.x_ref, bf16[2,2,896,512]{3,2,1,0:T(8,128)(2,1)S(1)} %get-tuple-element.19.rest_ref, f32[128,512]{1,0:T(8,128)S(1)} %get-tuple-element.20.g_in, f32[128,512]{1,0:T(8,128)S(1)} %get-tuple-element.21.u_in), custom_call_target="tpu_custom_call" | custom-call | flops 234881024 | bytes 458752 | tf_op jit(solution)/shard_map/more/pallas_call | solution.py:165
  27.6 0.4 %more.3 = (f32[64,512]{1,0:T(8,128)S(1)}, f32[64,512]{1,0:T(8,128)S(1)}) custom-call(bf16[64,896]{1,0:T(8,128)(2,1)S(1)} %collective-permute-done.1.x_ref, bf16[2,2,896,512]{3,2,1,0:T(8,128)(2,1)S(1)} %get-tuple-element.19.rest_ref, f32[128,512]{1,0:T(8,128)S(1)} %get-tuple-element.20.g_in, f32[128,512]{1,0:T(8,128)S(1)} %get-tuple-element.21.u_in), custom_call_target="tpu_custom_call" | custom-call | flops 234881024 | bytes 458752 | tf_op jit(solution)/shard_map/more/pallas_call | solution.py:165
  28.1 0.0 collective-permute-done.4.d_ref
  28.1 0.4 %last.3 = bf16[64,512]{1,0:T(8,128)(2,1)S(1)} custom-call(bf16[64,896]{1,0:T(8,128)(2,1)S(1)} %collective-permute-done.4.d_ref, bf16[2,2,896,512]{3,2,1,0:T(8,128)(2,1)S(1)} %get-tuple-element.19.rest_ref, f32[64,512]{1,0:T(8,128)S(1)} %get-tuple-element.25.g_in, f32[64,512]{1,0:T(8,128)S(1)} %get-tuple-element.26.u_in), custom_call_target="tpu_custom_call" | custom-call | flops 234881024 | bytes 458752 | tf_op jit(solution)/shard_map/last/pallas_call | solution.py:169
  28.6 0.0 collective-permute-done.3.d_ref
  28.6 0.4 %last.2 = bf16[64,512]{1,0:T(8,128)(2,1)S(1)} custom-call(bf16[64,896]{1,0:T(8,128)(2,1)S(1)} %collective-permute-done.3.d_ref, bf16[2,2,896,512]{3,2,1,0:T(8,128)(2,1)S(1)} %get-tuple-element.19.rest_ref, f32[64,512]{1,0:T(8,128)S(1)} %get-tuple-element.22.g_in, f32[64,512]{1,0:T(8,128)S(1)} %get-tuple-element.23.u_in), custom_call_target="tpu_custom_call" | custom-call | flops 234881024 | bytes 458752 | tf_op jit(solution)/shard_map/last/pallas_call | solution.py:169
  29.0 0.1 collective-permute-start.5
  29.2 1.5 %collective-permute-start.6 = (bf16[128,512]{1,0:T(8,128)(2,1)S(1)}, bf16[128,512]{1,0:T(8,128)(2,1)S(1)}, u32[]{:S(2)}, u32[]{:S(2)}) collective-permute-start(bf16[128,512]{1,0:T(8,128)(2,1)S(1)} %pad_maximum_fusion.h_ref), channel_id=1, source_target_pairs={{0,2},{1,3},{2,0},{3,1},{4,6},{5,7},{6,4},{7,5},{8,10},{9,11},{10,... | collective-permute-start | bytes 393224 | tf_op jit(solution)/shard_map/ppermute | solution.py:176
  30.7 0.0 collective-permute-done.5.sib_ref
  30.7 1.7 %near.1 = (bf16[512,128]{1,0:T(8,128)(2,1)S(1)}, bf16[1,128,512]{2,1,0:T(8,128)(2,1)}, f32[1,512,2048]{2,1,0:T(8,128)}) custom-call(bf16[128,512]{1,0:T(8,128)(2,1)S(1)} %pad_maximum_fusion.h_ref, bf16[128,512]{1,0:T(8,128)(2,1)S(1)} %collective-permute-done.5.sib_ref), custom_call_target="tpu_custom_call" | custom-call | flops 134217728 | bytes 2097152 | tf_op jit(solution)/shard_map/near/pallas_call | solution.py:179
  32.3 2.7 %collective-permute-done.6.h_ref = bf16[128,512]{1,0:T(8,128)(2,1)S(1)} collective-permute-done((bf16[128,512]{1,0:T(8,128)(2,1)S(1)}, bf16[128,512]{1,0:T(8,128)(2,1)S(1)}, u32[]{:S(2)}, u32[]{:S(2)}) %collective-permute-start.6) | collective-permute-done | bytes 131104 | tf_op jit(solution)/shard_map/ppermute | solution.py:176
  35.0 0.0 collective-permute-start.7
  35.0 1.2 %block_2.1.hess_in = f32[1,512,2048]{2,1,0:T(8,128)} custom-call(bf16[512,128]{1,0:T(8,128)(2,1)S(1)} %get-tuple-element.29.flip_ref, bf16[128,512]{1,0:T(8,128)(2,1)S(1)} %collective-permute-done.6.h_ref, f32[1,512,2048]{2,1,0:T(8,128)} %get-tuple-element.31.hess_in), custom_call_target="tpu_custom_call", output_to_operand_aliasing={{}: (2, {})} | custom-call | flops 67108864 | bytes 1048576 | tf_op jit(solution)/shard_map/block_2/pallas_call | solution.py:186
  36.2 0.2 collective-permute-done.7.h_ref
  36.4 1.2 %block_3.1 = f32[1,512,2048]{2,1,0:T(8,128)} custom-call(bf16[512,128]{1,0:T(8,128)(2,1)S(1)} %get-tuple-element.29.flip_ref, bf16[128,512]{1,0:T(8,128)(2,1)S(1)} %collective-permute-done.7.h_ref, f32[1,512,2048]{2,1,0:T(8,128)} %block_2.1.hess_in), custom_call_target="tpu_custom_call", output_to_operand_aliasing={{}: (2, {})} | custom-call | flops 67108864 | bytes 1048576 | tf_op jit(solution)/shard_map/block_3/pallas_call | solution.py:186
  (2 shorter events, 0.0 us)
Async XLA Ops:
  0.6 1.0 %copy-start = (bf16[256,896]{1,0:T(8,128)(2,1)S(1)}, bf16[256,896]{1,0:T(8,128)(2,1)}, u32[]{:S(2)}) copy-start(bf16[256,896]{1,0:T(8,128)(2,1)} %tok_hbm.1) | copy-start | bytes 1376260
  1.6 0.7 %copy-start.1 = (s32[256,8]{0,1:T(8,128)S(1)}, s32[256,8]{0,1:T(8,128)}, u32[]{:S(2)}) copy-start(s32[256,8]{0,1:T(8,128)} %param.5) | copy-start | bytes 24580
  18.6 2.1 %collective-permute-start.2 = (bf16[128,896]{1,0:T(8,128)(2,1)S(1)}, bf16[128,896]{1,0:T(8,128)(2,1)S(1)}, u32[]{:S(2)}, u32[]{:S(2)}) collective-permute-start(bf16[128,896]{1,0:T(8,128)(2,1)S(1)} %bitcast.5), channel_id=1, source_target_pairs={{0,1},{1,0},{2,3},{3,2},{4,5},{5,4},{6,7},{7,6},{8,9},{9,8},{10,11... | collective-permute-start | bytes 688136 | tf_op jit(solution)/shard_map/ppermute | solution.py:150
  18.6 6.0 %collective-permute-start = (bf16[64,896]{1,0:T(8,128)(2,1)S(1)}, bf16[64,896]{1,0:T(8,128)(2,1)S(1)}, u32[]{:S(2)}, u32[]{:S(2)}) collective-permute-start(bf16[64,896]{1,0:T(8,128)(2,1)S(1)} %bitcast.10), channel_id=1, source_target_pairs={{0,2},{1,3},{2,0},{3,1},{4,6},{5,7},{6,4},{7,5},{8,10},{9,11},{10,... | collective-permute-start | bytes 344072 | tf_op jit(solution)/shard_map/ppermute | solution.py:149
  20.2 6.5 %collective-permute-start.1 = (bf16[64,896]{1,0:T(8,128)(2,1)S(1)}, bf16[64,896]{1,0:T(8,128)(2,1)S(1)}, u32[]{:S(2)}, u32[]{:S(2)}) collective-permute-start(bf16[64,896]{1,0:T(8,128)(2,1)S(1)} %bitcast.9), channel_id=1, source_target_pairs={{0,2},{1,3},{2,0},{3,1},{4,6},{5,7},{6,4},{7,5},{8,10},{9,11},{10,... | collective-permute-start | bytes 344072 | tf_op jit(solution)/shard_map/ppermute | solution.py:149
  26.7 1.4 %collective-permute-start.4 = (bf16[64,896]{1,0:T(8,128)(2,1)S(1)}, bf16[64,896]{1,0:T(8,128)(2,1)S(1)}, u32[]{:S(2)}, u32[]{:S(2)}) collective-permute-start(bf16[64,896]{1,0:T(8,128)(2,1)S(1)} %collective-permute-done.1.x_ref), channel_id=1, source_target_pairs={{0,1},{1,0},{2,3},{3,2},{4,5},{5,4},{6,7},{7,6},{8,9},{9,8},{10,11... | collective-permute-start | bytes 344072 | tf_op jit(solution)/shard_map/ppermute | solution.py:164
  26.7 1.9 %collective-permute-start.3 = (bf16[64,896]{1,0:T(8,128)(2,1)S(1)}, bf16[64,896]{1,0:T(8,128)(2,1)S(1)}, u32[]{:S(2)}, u32[]{:S(2)}) collective-permute-start(bf16[64,896]{1,0:T(8,128)(2,1)S(1)} %collective-permute-done.x_ref), channel_id=1, source_target_pairs={{0,1},{1,0},{2,3},{3,2},{4,5},{5,4},{6,7},{7,6},{8,9},{9,8},{10,11... | collective-permute-start | bytes 344072 | tf_op jit(solution)/shard_map/ppermute | solution.py:164
  29.0 1.6 %collective-permute-start.5 = (bf16[128,512]{1,0:T(8,128)(2,1)S(1)}, bf16[128,512]{1,0:T(8,128)(2,1)S(1)}, u32[]{:S(2)}, u32[]{:S(2)}) collective-permute-start(bf16[128,512]{1,0:T(8,128)(2,1)S(1)} %pad_maximum_fusion.h_ref), channel_id=1, source_target_pairs={{0,1},{1,0},{2,3},{3,2},{4,5},{5,4},{6,7},{7,6},{8,9},{9,8},{10,11... | collective-permute-start | bytes 393224 | tf_op jit(solution)/shard_map/ppermute | solution.py:177
  29.2 5.9 %collective-permute-start.6 = (bf16[128,512]{1,0:T(8,128)(2,1)S(1)}, bf16[128,512]{1,0:T(8,128)(2,1)S(1)}, u32[]{:S(2)}, u32[]{:S(2)}) collective-permute-start(bf16[128,512]{1,0:T(8,128)(2,1)S(1)} %pad_maximum_fusion.h_ref), channel_id=1, source_target_pairs={{0,2},{1,3},{2,0},{3,1},{4,6},{5,7},{6,4},{7,5},{8,10},{9,11},{10,... | collective-permute-start | bytes 393224 | tf_op jit(solution)/shard_map/ppermute | solution.py:176
  35.0 1.3 %collective-permute-start.7 = (bf16[128,512]{1,0:T(8,128)(2,1)S(1)}, bf16[128,512]{1,0:T(8,128)(2,1)S(1)}, u32[]{:S(2)}, u32[]{:S(2)}) collective-permute-start(bf16[128,512]{1,0:T(8,128)(2,1)S(1)} %collective-permute-done.6.h_ref), channel_id=1, source_target_pairs={{0,1},{1,0},{2,3},{3,2},{4,5},{5,4},{6,7},{7,6},{8,9},{9,8},{10,11... | collective-permute-start | bytes 393224 | tf_op jit(solution)/shard_map/ppermute | solution.py:193

commit v2 on v0

v2 whole, which is shorter than its diff:
```python
import functools

import jax
import jax.numpy as jnp
from jax import lax
from jax.experimental import pallas as pl
from jax.experimental.pallas import tpu as pltpu
from jax.sharding import PartitionSpec as P

EXPERTS = 256
TOP = 8
BF16 = jnp.bfloat16
F32 = jnp.float32
VMEM = pl.BlockSpec(memory_space=pltpu.VMEM)
ANY = pl.BlockSpec(memory_space=pl.ANY)
HBM = pl.BlockSpec(memory_space=pltpu.HBM)
LIMIT = 40 * 1024 * 1024


def dot(a, b):
    return lax.dot_general(a, b, (((1,), (0,)), ((), ())), preferred_element_type=F32)


def weight_copies(gate_hbm, up_hbm, w_ref, sems, chip):
    depth = w_ref.shape[1]
    at = pl.ds(pl.multiple_of(((lax.axis_index("tp") >> 1) ^ chip) * depth, depth), depth)
    return [pltpu.make_async_copy(w.at[0, at, :], w_ref.at[i], sems.at[2 + i]) for i, w in enumerate((gate_hbm, up_hbm))]


def prepare_kernel(capacity, ids_hbm, tok_hbm, gate_hbm, up_hbm, pick_ref, mine_ref, w_ref, ids_ref, tok_ref, sems):
    get = [
        pltpu.make_async_copy(ids_hbm, ids_ref, sems.at[0]),
        pltpu.make_async_copy(tok_hbm, tok_ref, sems.at[1]),
    ] + weight_copies(gate_hbm, up_hbm, w_ref, sems, 0)
    for g in get:
        g.start()
    rows = ids_ref.shape[1]
    before = lax.broadcasted_iota(jnp.int32, (rows, rows), 0)
    after = lax.broadcasted_iota(jnp.int32, (rows, rows), 1)
    upto = jnp.where(before <= after, 1.0, 0.0).astype(BF16)
    want = lax.broadcasted_iota(jnp.int32, (4, capacity, rows), 1).astype(F32)
    core = lax.axis_index("tp") & 1
    step = lax.broadcasted_iota(jnp.int32, (8, rows), 0)
    offset = 2 * step + (core ^ (step & 1))
    expert = lax.axis_index("ep") ^ offset
    get[0].wait()
    ids = ids_ref[...]
    hit = ids[0:1, :] == expert
    for k in range(1, ids.shape[0]):
        hit = hit | (ids[k : k + 1, :] == expert)
    count = dot(jnp.where(hit, 1.0, 0.0).astype(BF16), upto)
    slot = jnp.where(hit, count - 1.0, -1.0)[:4]
    pick = jnp.where(slot[:, None, :] == want, 1.0, 0.0)
    pick = pick.reshape(4 * capacity, rows).astype(BF16)
    pick_ref[...] = pick
    get[1].wait()
    mine_ref[...] = dot(pick, tok_ref[...]).astype(BF16)
    get[2].wait()
    get[3].wait()


def select_kernel(capacity, pick_ref, mine_ref, sib_ref, *outs):
    core = lax.axis_index("tp") & 1
    depth = sib_ref.shape[1]
    here = pl.ds(pl.multiple_of(core * depth, depth), depth)
    there = pl.ds(pl.multiple_of((1 - core) * depth, depth), depth)
    other = dot(pick_ref[...], sib_ref[...]).astype(BF16)
    for k, out in enumerate(outs):
        rows = slice(k * capacity, (k + 1) * capacity)
        out[:, here] = mine_ref[rows, :]
        out[:, there] = other[rows]


def both(a_ref, b_ref):
    return jnp.concatenate([a_ref[...], b_ref[...]], axis=0)


def near_kernel(own_ref, sib_ref, w_ref, g_ref, u_ref):
    x = both(own_ref, sib_ref)
    g_ref[...] = dot(x, w_ref[0])
    u_ref[...] = dot(x, w_ref[1])


def first_near_kernel(own_ref, sib_ref, w_ref, gate_hbm, up_hbm, g_ref, u_ref, far_w_ref, sems):
    get = weight_copies(gate_hbm, up_hbm, far_w_ref, sems, 1)
    for g in get:
        g.start()
    near_kernel(own_ref, sib_ref, w_ref, g_ref, u_ref)
    for g in get:
        g.wait()


def far_kernel(capacity, far_ref, diag_ref, w_ref, g_ref, u_ref, h_ref):
    x = both(far_ref, diag_ref)
    gate = g_ref[...] + dot(x, w_ref[0])
    up = u_ref[...] + dot(x, w_ref[1])
    h = (gate / (1.0 + jnp.exp(-gate)) * up).astype(BF16)
    core = lax.axis_index("tp") & 1
    for i in range(4):
        k = i % 2
        block = 2 * k + (core ^ k ^ (i // 2))
        h_ref[pl.ds(pl.multiple_of(block * capacity, capacity), capacity), :] = h[i * capacity : (i + 1) * capacity]


def write_block(flip, h, factor, index, hess_hbm, buf, sems):
    wide = h.shape[1]
    part = wide // 4
    at = pl.ds(pl.multiple_of(index * wide, wide), wide)
    copies = []
    for i in range(4):
        rows = pl.ds(i * part, part)
        buf[rows, :] = dot(flip[rows, :], h) * factor
        copies.append(pltpu.make_async_copy(buf.at[rows, :], hess_hbm.at[0, rows, at], sems.at[i]))
        copies[-1].start()
    return copies


def hess_near_kernel(factor, capacity, ha, hb, sa, sb, flip_ref, hid_hbm, hess_hbm, buf, sems, out_sems):
    t = lax.axis_index("tp")
    e = lax.axis_index("ep")
    copies = []
    for o in range(8):
        src = (ha, hb)[o // 4].at[pl.ds((o % 4) * capacity, capacity), :]
        at = pl.ds(pl.multiple_of((e ^ o) * capacity, capacity), capacity)
        copies.append(pltpu.make_async_copy(src, hid_hbm.at[0, at, :], out_sems.at[o]))
        copies[-1].start()
    h = both(ha, hb)
    flip_ref[...] = h.astype(F32).T.astype(BF16)
    copies += write_block(flip_ref, h, factor, t, hess_hbm, buf.at[0], sems.at[0])
    copies += write_block(flip_ref, both(sa, sb), factor, t ^ 1, hess_hbm, buf.at[1], sems.at[1])
    for c in copies:
        c.wait()


def hess_far_kernel(factor, which, flip_ref, ha, hb, hess_in, hess_hbm, buf, sems):
    t = lax.axis_index("tp")
    for c in write_block(flip_ref, both(ha, hb), factor, t ^ which, hess_hbm, buf, sems):
        c.wait()


def call(kernel, out_shape, in_specs, out_specs, scratch=(), name=None, aliases={}, flops=0, moved=0, limit=LIMIT):
    return pl.pallas_call(
        kernel,
        out_shape=out_shape,
        in_specs=in_specs,
        out_specs=out_specs,
        scratch_shapes=list(scratch),
        input_output_aliases=aliases,
        name=name,
        cost_estimate=pl.CostEstimate(flops=flops, bytes_accessed=moved, transcendentals=0),
        compiler_params=pltpu.CompilerParams(vmem_limit_bytes=limit),
    )


def tie(x, after):
    return lax.optimization_barrier((x, after))[0]


def paired(tokens, expert_ids, gate_weight, up_weight):
    groups = 8
    tok_rows, depth = tokens.shape
    capacity = 2 * tok_rows * TOP // EXPERTS
    slots = groups * capacity
    wide = gate_weight.shape[2]
    full = wide * 4
    S = jax.ShapeDtypeStruct
    D = pltpu.SemaphoreType.DMA
    V = pltpu.VMEM

    def chips(x):
        return lax.ppermute(x, "tp", [(i, i ^ 2) for i in range(4)])

    def cores(x):
        return lax.ppermute(x, "tp", [(i, i ^ 1) for i in range(4)])

    def spread(k, x):
        pairs = [(e * 4 + t, (e ^ (2 * k + ((t ^ k) & 1))) * 4 + t) for e in range(8) for t in range(4)]
        return lax.ppermute(x, ("ep", "tp"), pairs)

    sib_tokens = cores(tokens)
    half = slots // 2
    weights = 4 * 2 * depth * 2 * wide
    ids, toks, gate_w, up_w = (
        pltpu.with_memory_space_constraint(a, pltpu.HBM) for a in (expert_ids.T, tokens, gate_weight, up_weight)
    )
    half_w = V((2, 2 * depth, wide), BF16)
    pick, mine, near_w = call(
        functools.partial(prepare_kernel, capacity),
        (S((half, tok_rows), BF16), S((half, depth), BF16), half_w),
        [HBM] * 4, (VMEM, VMEM, VMEM),
        (V(ids.shape, jnp.int32), V(tokens.shape, BF16), D((4,))), name="prepare",
        flops=2 * half * tok_rows * depth, moved=weights // 2,
    )(ids, toks, gate_w, up_w)
    out = call(
        functools.partial(select_kernel, capacity),
        (S((capacity, 2 * depth), BF16),) * 4, [VMEM] * 3, (VMEM,) * 4, name="select",
        flops=2 * half * tok_rows * depth,
    )(pick, mine, sib_tokens)
    got = [spread(k, out[k]) for k in range(4)]
    part = S((half, wide), F32)
    work = 4 * half * depth * 2 * wide

    def near(own, sib):
        return call(
            near_kernel, (part, part), [VMEM] * 3, (VMEM,) * 2, name="near", flops=work, moved=weights // 2,
        )(own, sib, near_w)

    def finish(far, diag, gate, up):
        return call(
            functools.partial(far_kernel, capacity), S((half, wide), BF16), [VMEM] * 5, VMEM, name="far",
            flops=work, moved=weights // 2,
        )(far, diag, far_w, gate, up)

    own1 = jnp.concatenate(got[:2])
    own2 = jnp.concatenate(got[2:])
    far1 = chips(own1)
    far2 = chips(own2)
    sib1 = cores(own1)
    sib2 = cores(own2)
    diag1 = cores(far1)
    gate1, up1, far_w = call(
        first_near_kernel, (part, part, half_w), [VMEM] * 3 + [HBM] * 2, (VMEM,) * 3, (D((4,)),), name="first_near",
        flops=work, moved=weights // 2,
    )(own1, tie(sib1, far1), near_w, gate_w, up_w)
    ha = finish(far1, diag1, gate1, up1)
    far_a = chips(ha)
    sib_a = cores(ha)
    far2 = tie(far2, ha)
    diag2 = cores(far2)
    gate2, up2 = near(own2, tie(sib2, far2))
    hb = finish(far2, diag2, gate2, up2)
    far_b = chips(hb)
    sib_b = cores(hb)
    diag_a = cores(far_a)

    factor = 2.0 / slots
    hess_shape = S((1, wide, full), F32)
    block = wide * wide * 4
    flip, hidden, hess = call(
        functools.partial(hess_near_kernel, factor, capacity),
        (S((wide, slots), BF16), S((1, slots, wide), BF16), hess_shape),
        [VMEM] * 4, (VMEM, ANY, ANY), (V((2, wide, wide), F32), D((2, 4)), D((8,))), name="hess_near",
        flops=4 * slots * wide * wide, moved=2 * block,
    )(ha, hb, sib_a, sib_b)

    def other(which, a, b, hess):
        return call(
            functools.partial(hess_far_kernel, factor, which), hess_shape,
            [VMEM, VMEM, VMEM, ANY], ANY, (V((wide, wide), F32), D((4,))), name="hess_%d" % which, aliases={3: 0},
            flops=2 * slots * wide * wide, moved=block,
        )(flip, a, b, hess)

    far_b = tie(far_b, flip)
    diag_b = cores(far_b)
    hess = other(2, far_a, far_b, hess)
    hess = other(3, diag_a, diag_b, hess)
    return hidden, hess


def general(tokens, expert_ids, gate_weight, up_weight):
    groups = lax.axis_size("ep")
    capacity = 2 * tokens.shape[0] * TOP // EXPERTS
    slots = groups * capacity
    member = jnp.any(expert_ids[:, :, None] == jnp.arange(groups, dtype=jnp.int32), axis=1).astype(jnp.int32)
    rank = jnp.cumsum(member, axis=0) - 1
    chosen = (member.T[:, None, :] > 0) & (rank.T[:, None, :] == jnp.arange(capacity, dtype=jnp.int32)[None, :, None])
    outgoing = jnp.einsum("gcj,jf->gcf", chosen.astype(BF16), tokens, preferred_element_type=F32).astype(BF16)
    arrived = lax.all_to_all(outgoing, "ep", split_axis=0, concat_axis=0, tiled=True)
    routed = lax.all_gather(arrived.reshape(slots, arrived.shape[2]), "tp", axis=1, tiled=True)
    gate = dot(routed, gate_weight[0])
    hidden = (jax.nn.silu(gate) * dot(routed, up_weight[0])).astype(BF16)
    whole = lax.all_gather(hidden, "tp", axis=1, tiled=True)
    hess = lax.dot_general(hidden, whole, (((0,), (0,)), ((), ())), preferred_element_type=F32) * (2.0 / slots)
    return hidden[None], hess[None]


def solution(mesh):
    body = paired if (mesh.shape["ep"], mesh.shape["tp"]) == (8, 4) else general
    return jax.shard_map(
        body,
        mesh=mesh,
        in_specs=(P("ep", "tp"), P("ep", None), P("ep", None, "tp"), P("ep", None, "tp")),
        out_specs=(P("ep", None, "tp"), P("ep", "tp", None)),
        check_vma=False,
    )
```

time: 41.3 us -> 33.1 us (0.80)
  blocking collectives: 32.4 us -> 0 us
  starting transfers between devices: 0 us -> 14.9 us
  Pallas kernels: 0 us -> 11.5 us
  matrix products: 6.31 us -> 0 us
  waiting for transfers between devices: 0 us -> 5.71 us
  other arithmetic: 1.47 us -> 0 us
    all_gather x2 -> x0, blocking collectives: 16.6 us -> none  [the longest x1 9.3 us: on_device(): routed = lax.all_gather(arrived, 'tp', axis=1, tiled=True)]
    all_to_all x1 -> x0, blocking collectives: 15.8 us -> none  [on_device(): lax.all_to_all(outgoing, 'ep', split_axis=0, concat_axis=0, tiled=True)]
    ppermute x0 -> x17, starting transfers between devices: none -> 14.9 us  [the longest x4 6.86 us: spread(): return lax.ppermute(x, ('ep', 'tp'), pairs)]
    pallas_call x0 -> x9, Pallas kernels: none -> 11.5 us  [the longest x1 2.67 us: paired(): call(first_near_kernel, (part, part, half_w), [VMEM] * 3 + [HBM] * 2, (VM...]
    dot_general x4 -> x0, matrix products: 6.31 us -> none  [the longest x1 2.75 us: on_device(): lax.dot_general(hidden, lax.all_gather(hidden, 'tp', axis=1, tiled=True),...]
    ppermute x0 -> x17, waiting for transfers between devices: none -> 5.71 us  [the longest x4 3.46 us: chips(): return lax.ppermute(x, 'tp', [(i, i ^ 2) for i in range(4)])]
    reduce_or x1 -> x0, other arithmetic: 0.76 us -> none  [on_device(): jnp.any(expert_ids[:, :, None] == targets[None, None, :], axis=1)]
    another operation x2 -> x0, other arithmetic: 0.62 us -> none
  transfers between devices with their start and end apart: 0 -> 17, of which waited for: 0 -> 6; matrix products, arithmetic and copies ran while one was open for 0% -> 0% of each run, Pallas kernels for 0% -> 31%
where the time goes in v2:
time: 33.1 us; the launch traced here: 32.9 us
  starting transfers between devices  14.9 us (45%)
  Pallas kernels  11.5 us (35%)
  waiting for transfers between devices  5.71 us (17%)
  between operations  0.78 us (2%)
    ppermute x4, starting transfers between devices, spread(): return lax.ppermute(x, ('ep', 'tp'), pairs)  6.86 us
    ppermute x4, starting transfers between devices, chips(): return lax.ppermute(x, 'tp', [(i, i ^ 2) for i in range(4)])  5.39 us
    ppermute x4, waiting for transfers between devices, chips(): return lax.ppermute(x, 'tp', [(i, i ^ 2) for i in range(4)])  3.46 us
    ppermute x9, starting transfers between devices, cores(): return lax.ppermute(x, 'tp', [(i, i ^ 1) for i in range(4)])  2.68 us
    pallas_call x1, Pallas kernels, paired(): call(first_near_kernel, (part, part, half_w), [VMEM] * 3 + [HBM] * 2, (VM...  2.67 us
    pallas_call x2, Pallas kernels, other(): call(functools.partial(hess_far_kernel, factor, which), hess_shape, [VMEM...  2.35 us
    pallas_call x1, Pallas kernels, paired(): call(functools.partial(prepare_kernel, capacity), (S((half, tok_rows), BF...  2.26 us
    ppermute x4, waiting for transfers between devices, spread(): return lax.ppermute(x, ('ep', 'tp'), pairs)  2.17 us
  transfers between devices with their start and end apart: 17, of which 6 were waited for; matrix products, arithmetic and copies ran while one was open for 0% of the time, Pallas kernels for 31%

profile of v2, /device:TPU:0, one launch (start us, length us, event | category | flops | bytes accessed | tf_op | source)
XLA Modules:
  0.0 32.9 jit_solution(12184344181178058268)
XLA Ops:
  0.6 0.5 %collective-permute-start = (bf16[256,896]{1,0:T(8,128)(2,1)}, bf16[256,896]{1,0:T(8,128)(2,1)S(1)}, u32[]{:S(2)}, u32[]{:S(2)}) collective-permute-start(bf16[256,896]{1,0:T(8,128)(2,1)} %tok_hbm.1), channel_id=1, source_target_pairs={{0,1},{1,0},{2,3},{3,2},{4,5},{5,4},{6,7},{7,6},{8,9},{9,8},{10,11... | collective-permute-start | bytes 1376264 | tf_op jit(solution)/shard_map/ppermute | solution.py:174
  1.1 2.3 %prepare.1 = (bf16[64,256]{1,0:T(8,128)(2,1)S(1)}, bf16[64,896]{1,0:T(8,128)(2,1)S(1)}, bf16[2,1792,512]{2,1,0:T(8,128)(2,1)S(1)}) custom-call(s32[8,256]{1,0:T(8,128)} %bitcast.1, bf16[256,896]{1,0:T(8,128)(2,1)} %tok_hbm.1, bf16[1,3584,512]{2,1,0:T(8,128)(2,1)} %gate_hbm.3, bf16[1,3584,512]{2,1,0:T(8,128)(2,1)} %up_hbm.3), custom_call_target="tpu_custom_call" | custom-call | flops 29360128 | bytes 3670016 | tf_op jit(solution)/shard_map/prepare/pallas_call | solution.py:187
  3.4 0.2 select.1
  3.6 0.7 %collective-permute-start.1 = (bf16[16,1792]{1,0:T(8,128)(2,1)S(1)}, bf16[16,1792]{1,0:T(8,128)(2,1)S(1)}, u32[]{:S(2)}, u32[]{:S(2)}) collective-permute-start(bf16[16,1792]{1,0:T(8,128)(2,1)S(1)} %get-tuple-element.23), channel_id=1, source_target_pairs={{0,0},{1,5},{2,2},{3,7},{4,4},{5,1},{6,6},{7,3},{8,8},{9,13},{10,1... | collective-permute-start | bytes 172040 | tf_op jit(solution)/shard_map/ppermute | solution.py:178
  4.3 3.6 %collective-permute-start.2 = (bf16[16,1792]{1,0:T(8,128)(2,1)S(1)}, bf16[16,1792]{1,0:T(8,128)(2,1)S(1)}, u32[]{:S(2)}, u32[]{:S(2)}) collective-permute-start(bf16[16,1792]{1,0:T(8,128)(2,1)S(1)} %get-tuple-element.24), channel_id=1, source_target_pairs={{0,12},{1,9},{2,14},{3,11},{4,8},{5,13},{6,10},{7,15},{8,4},{9,1},... | collective-permute-start | bytes 172040 | tf_op jit(solution)/shard_map/ppermute | solution.py:178
  7.9 2.6 %collective-permute-start.6 = (bf16[16,1792]{1,0:T(8,128)(2,1)S(1)}, bf16[16,1792]{1,0:T(8,128)(2,1)S(1)}, u32[]{:S(2)}, u32[]{:S(2)}) collective-permute-start(bf16[16,1792]{1,0:T(8,128)(2,1)S(1)} %get-tuple-element.30), channel_id=1, source_target_pairs={{0,16},{1,21},{2,18},{3,23},{4,20},{5,17},{6,22},{7,19},{8,24},{9,... | collective-permute-start | bytes 172040 | tf_op jit(solution)/shard_map/ppermute | solution.py:178
  10.5 0.0 collective-permute-start.7
  10.5 0.0 collective-permute-done.1
  10.5 0.0 collective-permute-done.2
  10.5 1.7 %collective-permute-start.3 = (bf16[32,1792]{1,0:T(8,128)(2,1)S(1)}, bf16[32,1792]{1,0:T(8,128)(2,1)S(1)}, u32[]{:S(2)}, u32[]{:S(2)}) collective-permute-start(bf16[32,1792]{1,0:T(8,128)(2,1)S(1)} %constant_dynamic-update-slice_fusion.own_ref), channel_id=1, source_target_pairs={{0,2},{1,3},{2,0},{3,1},{4,6},{5,7},{6,4},{7,5},{8,10},{9,11},{10,... | collective-permute-start | bytes 344072 | tf_op jit(solution)/shard_map/ppermute | solution.py:171
  12.3 1.0 %collective-permute-start.5 = (bf16[32,1792]{1,0:T(8,128)(2,1)S(1)}, bf16[32,1792]{1,0:T(8,128)(2,1)S(1)}, u32[]{:S(2)}, u32[]{:S(2)}) collective-permute-start(bf16[32,1792]{1,0:T(8,128)(2,1)S(1)} %constant_dynamic-update-slice_fusion.own_ref), channel_id=1, source_target_pairs={{0,1},{1,0},{2,3},{3,2},{4,5},{5,4},{6,7},{7,6},{8,9},{9,8},{10,11... | collective-permute-start | bytes 344072 | tf_op jit(solution)/shard_map/ppermute | solution.py:174
  13.2 1.3 %collective-permute-done.6 = bf16[16,1792]{1,0:T(8,128)(2,1)S(1)} collective-permute-done((bf16[16,1792]{1,0:T(8,128)(2,1)S(1)}, bf16[16,1792]{1,0:T(8,128)(2,1)S(1)}, u32[]{:S(2)}, u32[]{:S(2)}) %collective-permute-start.6) | collective-permute-done | bytes 57376 | tf_op jit(solution)/shard_map/ppermute | solution.py:178
  14.6 1.7 %collective-permute-done.3.far_ref = bf16[32,1792]{1,0:T(8,128)(2,1)S(1)} collective-permute-done((bf16[32,1792]{1,0:T(8,128)(2,1)S(1)}, bf16[32,1792]{1,0:T(8,128)(2,1)S(1)}, u32[]{:S(2)}, u32[]{:S(2)}) %collective-permute-start.3) | collective-permute-done | bytes 114720 | tf_op jit(solution)/shard_map/ppermute | solution.py:171
  16.3 0.5 %collective-permute-start.4 = (bf16[32,1792]{1,0:T(8,128)(2,1)S(1)}, bf16[32,1792]{1,0:T(8,128)(2,1)S(1)}, u32[]{:S(2)}, u32[]{:S(2)}) collective-permute-start(bf16[32,1792]{1,0:T(8,128)(2,1)S(1)} %collective-permute-done.3.far_ref), channel_id=1, source_target_pairs={{0,1},{1,0},{2,3},{3,2},{4,5},{5,4},{6,7},{7,6},{8,9},{9,8},{10,11... | collective-permute-start | bytes 344072 | tf_op jit(solution)/shard_map/ppermute | solution.py:174
  16.7 0.8 %collective-permute-done.7 = bf16[16,1792]{1,0:T(8,128)(2,1)S(1)} collective-permute-done((bf16[16,1792]{1,0:T(8,128)(2,1)S(1)}, bf16[16,1792]{1,0:T(8,128)(2,1)S(1)}, u32[]{:S(2)}, u32[]{:S(2)}) %collective-permute-start.7) | collective-permute-done | bytes 57376 | tf_op jit(solution)/shard_map/ppermute | solution.py:178
  17.6 1.5 %collective-permute-start.8 = (bf16[32,1792]{1,0:T(8,128)(2,1)S(1)}, bf16[32,1792]{1,0:T(8,128)(2,1)S(1)}, u32[]{:S(2)}, u32[]{:S(2)}) collective-permute-start(bf16[32,1792]{1,0:T(8,128)(2,1)S(1)} %constant_dynamic-update-slice_fusion.2.own_ref), channel_id=1, source_target_pairs={{0,2},{1,3},{2,0},{3,1},{4,6},{5,7},{6,4},{7,5},{8,10},{9,11},{10,... | collective-permute-start | bytes 344072 | tf_op jit(solution)/shard_map/ppermute | solution.py:171
  19.1 0.0 collective-permute-start.10
  19.1 2.7 %first_near.1 = (f32[64,512]{1,0:T(8,128)S(1)}, f32[64,512]{1,0:T(8,128)S(1)}, bf16[2,1792,512]{2,1,0:T(8,128)(2,1)S(1)}) custom-call(bf16[32,1792]{1,0:T(8,128)(2,1)S(1)} %constant_dynamic-update-slice_fusion.own_ref, bf16[32,1792]{1,0:T(8,128)(2,1)S(1)} %collective-permute-done.5.sib_ref, bf16[2,1792,512]{2,1,0:T(8,128)(2,1)S(1)} %get-tuple-element.26.w_ref, ...), custom_call_target="tpu_custom_call" | custom-call | flops 234881024 | bytes 3670016 | tf_op jit(solution)/shard_map/first_near/pallas_call | solution.py:221
  21.8 0.7 %far.2.ha = bf16[64,512]{1,0:T(8,128)(2,1)S(1)} custom-call(bf16[32,1792]{1,0:T(8,128)(2,1)S(1)} %collective-permute-done.3.far_ref, bf16[32,1792]{1,0:T(8,128)(2,1)S(1)} %collective-permute-done.4.diag_ref, bf16[2,1792,512]{2,1,0:T(8,128)(2,1)S(1)} %get-tuple-element.27.w_ref, f32[64,512]{1,0:T(8,128)S(1)} %get-tuple-element.28.g_ref, ...), custom_call_target="tpu_custom_call" | custom-call | flops 234881024 | bytes 3670016 | tf_op jit(solution)/shard_map/far/pallas_call | solution.py:209
  22.5 0.6 %collective-permute-start.9 = (bf16[32,1792]{1,0:T(8,128)(2,1)S(1)}, bf16[32,1792]{1,0:T(8,128)(2,1)S(1)}, u32[]{:S(2)}, u32[]{:S(2)}) collective-permute-start(bf16[32,1792]{1,0:T(8,128)(2,1)S(1)} %collective-permute-done.8.far_ref), channel_id=1, source_target_pairs={{0,1},{1,0},{2,3},{3,2},{4,5},{5,4},{6,7},{7,6},{8,9},{9,8},{10,11... | collective-permute-start | bytes 344072 | tf_op jit(solution)/shard_map/ppermute | solution.py:174
  23.1 0.1 collective-permute-start.11
  23.2 1.2 %collective-permute-start.13 = (bf16[64,512]{1,0:T(8,128)(2,1)S(1)}, bf16[64,512]{1,0:T(8,128)(2,1)S(1)}, u32[]{:S(2)}, u32[]{:S(2)}) collective-permute-start(bf16[64,512]{1,0:T(8,128)(2,1)S(1)} %far.2.ha), channel_id=1, source_target_pairs={{0,2},{1,3},{2,0},{3,1},{4,6},{5,7},{6,4},{7,5},{8,10},{9,11},{10,... | collective-permute-start | bytes 196616 | tf_op jit(solution)/shard_map/ppermute | solution.py:171
  24.4 0.7 %near.1 = (f32[64,512]{1,0:T(8,128)S(1)}, f32[64,512]{1,0:T(8,128)S(1)}) custom-call(bf16[32,1792]{1,0:T(8,128)(2,1)S(1)} %constant_dynamic-update-slice_fusion.2.own_ref, bf16[32,1792]{1,0:T(8,128)(2,1)S(1)} %collective-permute-done.10.sib_ref, bf16[2,1792,512]{2,1,0:T(8,128)(2,1)S(1)} %get-tuple-element.26.w_ref), custom_call_target="tpu_custom_call" | custom-call | flops 234881024 | bytes 3670016 | tf_op jit(solution)/shard_map/near/pallas_call | solution.py:204
  25.1 0.7 %far.3.hb = bf16[64,512]{1,0:T(8,128)(2,1)S(1)} custom-call(bf16[32,1792]{1,0:T(8,128)(2,1)S(1)} %collective-permute-done.8.far_ref, bf16[32,1792]{1,0:T(8,128)(2,1)S(1)} %collective-permute-done.9.diag_ref, bf16[2,1792,512]{2,1,0:T(8,128)(2,1)S(1)} %get-tuple-element.27.w_ref, f32[64,512]{1,0:T(8,128)S(1)} %get-tuple-element.34.g_ref, ...), custom_call_target="tpu_custom_call" | custom-call | flops 234881024 | bytes 3670016 | tf_op jit(solution)/shard_map/far/pallas_call | solution.py:209
  25.9 0.1 collective-permute-start.12
  26.0 1.0 %collective-permute-start.15 = (bf16[64,512]{1,0:T(8,128)(2,1)S(1)}, bf16[64,512]{1,0:T(8,128)(2,1)S(1)}, u32[]{:S(2)}, u32[]{:S(2)}) collective-permute-start(bf16[64,512]{1,0:T(8,128)(2,1)S(1)} %far.3.hb), channel_id=1, source_target_pairs={{0,2},{1,3},{2,0},{3,1},{4,6},{5,7},{6,4},{7,5},{8,10},{9,11},{10,... | collective-permute-start | bytes 196616 | tf_op jit(solution)/shard_map/ppermute | solution.py:171
  26.9 0.7 %collective-permute-done.13.ha = bf16[64,512]{1,0:T(8,128)(2,1)S(1)} collective-permute-done((bf16[64,512]{1,0:T(8,128)(2,1)S(1)}, bf16[64,512]{1,0:T(8,128)(2,1)S(1)}, u32[]{:S(2)}, u32[]{:S(2)}) %collective-permute-start.13) | collective-permute-done | bytes 65568 | tf_op jit(solution)/shard_map/ppermute | solution.py:171
  27.6 1.7 %hess_near.1 = (bf16[512,128]{1,0:T(8,128)(2,1)S(1)}, bf16[1,128,512]{2,1,0:T(8,128)(2,1)}, f32[1,512,2048]{2,1,0:T(8,128)}) custom-call(bf16[64,512]{1,0:T(8,128)(2,1)S(1)} %far.2.ha, bf16[64,512]{1,0:T(8,128)(2,1)S(1)} %far.3.hb, bf16[64,512]{1,0:T(8,128)(2,1)S(1)} %collective-permute-done.11.sa, bf16[64,512]{1,0:T(8,128)(2,1)S(1)} %collective-permute-done.12.sb), custom_call_target="tpu_custom_call" | custom-call | flops 134217728 | bytes 2097152 | tf_op jit(solution)/shard_map/hess_near/pallas_call | solution.py:239
  29.4 1.1 %collective-permute-done.15.hb = bf16[64,512]{1,0:T(8,128)(2,1)S(1)} collective-permute-done((bf16[64,512]{1,0:T(8,128)(2,1)S(1)}, bf16[64,512]{1,0:T(8,128)(2,1)S(1)}, u32[]{:S(2)}, u32[]{:S(2)}) %collective-permute-start.15) | collective-permute-done | bytes 65568 | tf_op jit(solution)/shard_map/ppermute | solution.py:171
  30.5 1.2 %hess_2.1.hess_in = f32[1,512,2048]{2,1,0:T(8,128)} custom-call(bf16[512,128]{1,0:T(8,128)(2,1)S(1)} %get-tuple-element.37.flip_ref, bf16[64,512]{1,0:T(8,128)(2,1)S(1)} %collective-permute-done.13.ha, bf16[64,512]{1,0:T(8,128)(2,1)S(1)} %collective-permute-done.15.hb, f32[1,512,2048]{2,1,0:T(8,128)} %get-tuple-element.39.hess_in), custom_call_target="tpu_custom_call", output_to_operand_aliasing={{}: (3, {})} | custom-call | flops 67108864 | bytes 1048576 | tf_op jit(solution)/shard_map/hess_2/pallas_call | solution.py:247
  31.7 0.1 collective-permute-done.16.hb
  31.7 1.2 %hess_3.1 = f32[1,512,2048]{2,1,0:T(8,128)} custom-call(bf16[512,128]{1,0:T(8,128)(2,1)S(1)} %get-tuple-element.37.flip_ref, bf16[64,512]{1,0:T(8,128)(2,1)S(1)} %collective-permute-done.14.ha, bf16[64,512]{1,0:T(8,128)(2,1)S(1)} %collective-permute-done.16.hb, f32[1,512,2048]{2,1,0:T(8,128)} %hess_2.1.hess_in), custom_call_target="tpu_custom_call", output_to_operand_aliasing={{}: (3, {})} | custom-call | flops 67108864 | bytes 1048576 | tf_op jit(solution)/shard_map/hess_3/pallas_call | solution.py:247
  (15 shorter events, 0.0 us)
Async XLA Ops:
  0.6 2.8 %collective-permute-start = (bf16[256,896]{1,0:T(8,128)(2,1)}, bf16[256,896]{1,0:T(8,128)(2,1)S(1)}, u32[]{:S(2)}, u32[]{:S(2)}) collective-permute-start(bf16[256,896]{1,0:T(8,128)(2,1)} %tok_hbm.1), channel_id=1, source_target_pairs={{0,1},{1,0},{2,3},{3,2},{4,5},{5,4},{6,7},{7,6},{8,9},{9,8},{10,11... | collective-permute-start | bytes 1376264 | tf_op jit(solution)/shard_map/ppermute | solution.py:174
  3.6 6.9 %collective-permute-start.1 = (bf16[16,1792]{1,0:T(8,128)(2,1)S(1)}, bf16[16,1792]{1,0:T(8,128)(2,1)S(1)}, u32[]{:S(2)}, u32[]{:S(2)}) collective-permute-start(bf16[16,1792]{1,0:T(8,128)(2,1)S(1)} %get-tuple-element.23), channel_id=1, source_target_pairs={{0,0},{1,5},{2,2},{3,7},{4,4},{5,1},{6,6},{7,3},{8,8},{9,13},{10,1... | collective-permute-start | bytes 172040 | tf_op jit(solution)/shard_map/ppermute | solution.py:178
  4.3 6.2 %collective-permute-start.2 = (bf16[16,1792]{1,0:T(8,128)(2,1)S(1)}, bf16[16,1792]{1,0:T(8,128)(2,1)S(1)}, u32[]{:S(2)}, u32[]{:S(2)}) collective-permute-start(bf16[16,1792]{1,0:T(8,128)(2,1)S(1)} %get-tuple-element.24), channel_id=1, source_target_pairs={{0,12},{1,9},{2,14},{3,11},{4,8},{5,13},{6,10},{7,15},{8,4},{9,1},... | collective-permute-start | bytes 172040 | tf_op jit(solution)/shard_map/ppermute | solution.py:178
  7.9 6.7 %collective-permute-start.6 = (bf16[16,1792]{1,0:T(8,128)(2,1)S(1)}, bf16[16,1792]{1,0:T(8,128)(2,1)S(1)}, u32[]{:S(2)}, u32[]{:S(2)}) collective-permute-start(bf16[16,1792]{1,0:T(8,128)(2,1)S(1)} %get-tuple-element.30), channel_id=1, source_target_pairs={{0,16},{1,21},{2,18},{3,23},{4,20},{5,17},{6,22},{7,19},{8,24},{9,... | collective-permute-start | bytes 172040 | tf_op jit(solution)/shard_map/ppermute | solution.py:178
  10.5 7.1 %collective-permute-start.7 = (bf16[16,1792]{1,0:T(8,128)(2,1)S(1)}, bf16[16,1792]{1,0:T(8,128)(2,1)S(1)}, u32[]{:S(2)}, u32[]{:S(2)}) collective-permute-start(bf16[16,1792]{1,0:T(8,128)(2,1)S(1)} %get-tuple-element.31), channel_id=1, source_target_pairs={{0,28},{1,25},{2,30},{3,27},{4,24},{5,29},{6,26},{7,31},{8,20},{9,... | collective-permute-start | bytes 172040 | tf_op jit(solution)/shard_map/ppermute | solution.py:178
  10.5 5.7 %collective-permute-start.3 = (bf16[32,1792]{1,0:T(8,128)(2,1)S(1)}, bf16[32,1792]{1,0:T(8,128)(2,1)S(1)}, u32[]{:S(2)}, u32[]{:S(2)}) collective-permute-start(bf16[32,1792]{1,0:T(8,128)(2,1)S(1)} %constant_dynamic-update-slice_fusion.own_ref), channel_id=1, source_target_pairs={{0,2},{1,3},{2,0},{3,1},{4,6},{5,7},{6,4},{7,5},{8,10},{9,11},{10,... | collective-permute-start | bytes 344072 | tf_op jit(solution)/shard_map/ppermute | solution.py:171
  12.3 6.8 %collective-permute-start.5 = (bf16[32,1792]{1,0:T(8,128)(2,1)S(1)}, bf16[32,1792]{1,0:T(8,128)(2,1)S(1)}, u32[]{:S(2)}, u32[]{:S(2)}) collective-permute-start(bf16[32,1792]{1,0:T(8,128)(2,1)S(1)} %constant_dynamic-update-slice_fusion.own_ref), channel_id=1, source_target_pairs={{0,1},{1,0},{2,3},{3,2},{4,5},{5,4},{6,7},{7,6},{8,9},{9,8},{10,11... | collective-permute-start | bytes 344072 | tf_op jit(solution)/shard_map/ppermute | solution.py:174
  16.3 5.5 %collective-permute-start.4 = (bf16[32,1792]{1,0:T(8,128)(2,1)S(1)}, bf16[32,1792]{1,0:T(8,128)(2,1)S(1)}, u32[]{:S(2)}, u32[]{:S(2)}) collective-permute-start(bf16[32,1792]{1,0:T(8,128)(2,1)S(1)} %collective-permute-done.3.far_ref), channel_id=1, source_target_pairs={{0,1},{1,0},{2,3},{3,2},{4,5},{5,4},{6,7},{7,6},{8,9},{9,8},{10,11... | collective-permute-start | bytes 344072 | tf_op jit(solution)/shard_map/ppermute | solution.py:174
  17.6 4.9 %collective-permute-start.8 = (bf16[32,1792]{1,0:T(8,128)(2,1)S(1)}, bf16[32,1792]{1,0:T(8,128)(2,1)S(1)}, u32[]{:S(2)}, u32[]{:S(2)}) collective-permute-start(bf16[32,1792]{1,0:T(8,128)(2,1)S(1)} %constant_dynamic-update-slice_fusion.2.own_ref), channel_id=1, source_target_pairs={{0,2},{1,3},{2,0},{3,1},{4,6},{5,7},{6,4},{7,5},{8,10},{9,11},{10,... | collective-permute-start | bytes 344072 | tf_op jit(solution)/shard_map/ppermute | solution.py:171
  19.1 5.3 %collective-permute-start.10 = (bf16[32,1792]{1,0:T(8,128)(2,1)S(1)}, bf16[32,1792]{1,0:T(8,128)(2,1)S(1)}, u32[]{:S(2)}, u32[]{:S(2)}) collective-permute-start(bf16[32,1792]{1,0:T(8,128)(2,1)S(1)} %constant_dynamic-update-slice_fusion.2.own_ref), channel_id=1, source_target_pairs={{0,1},{1,0},{2,3},{3,2},{4,5},{5,4},{6,7},{7,6},{8,9},{9,8},{10,11... | collective-permute-start | bytes 344072 | tf_op jit(solution)/shard_map/ppermute | solution.py:174
  22.5 2.6 %collective-permute-start.9 = (bf16[32,1792]{1,0:T(8,128)(2,1)S(1)}, bf16[32,1792]{1,0:T(8,128)(2,1)S(1)}, u32[]{:S(2)}, u32[]{:S(2)}) collective-permute-start(bf16[32,1792]{1,0:T(8,128)(2,1)S(1)} %collective-permute-done.8.far_ref), channel_id=1, source_target_pairs={{0,1},{1,0},{2,3},{3,2},{4,5},{5,4},{6,7},{7,6},{8,9},{9,8},{10,11... | collective-permute-start | bytes 344072 | tf_op jit(solution)/shard_map/ppermute | solution.py:174
  23.1 4.5 %collective-permute-start.11 = (bf16[64,512]{1,0:T(8,128)(2,1)S(1)}, bf16[64,512]{1,0:T(8,128)(2,1)S(1)}, u32[]{:S(2)}, u32[]{:S(2)}) collective-permute-start(bf16[64,512]{1,0:T(8,128)(2,1)S(1)} %far.2.ha), channel_id=1, source_target_pairs={{0,1},{1,0},{2,3},{3,2},{4,5},{5,4},{6,7},{7,6},{8,9},{9,8},{10,11... | collective-permute-start | bytes 196616 | tf_op jit(solution)/shard_map/ppermute | solution.py:174
  23.2 4.4 %collective-permute-start.13 = (bf16[64,512]{1,0:T(8,128)(2,1)S(1)}, bf16[64,512]{1,0:T(8,128)(2,1)S(1)}, u32[]{:S(2)}, u32[]{:S(2)}) collective-permute-start(bf16[64,512]{1,0:T(8,128)(2,1)S(1)} %far.2.ha), channel_id=1, source_target_pairs={{0,2},{1,3},{2,0},{3,1},{4,6},{5,7},{6,4},{7,5},{8,10},{9,11},{10,... | collective-permute-start | bytes 196616 | tf_op jit(solution)/shard_map/ppermute | solution.py:171
  25.9 1.7 %collective-permute-start.12 = (bf16[64,512]{1,0:T(8,128)(2,1)S(1)}, bf16[64,512]{1,0:T(8,128)(2,1)S(1)}, u32[]{:S(2)}, u32[]{:S(2)}) collective-permute-start(bf16[64,512]{1,0:T(8,128)(2,1)S(1)} %far.3.hb), channel_id=1, source_target_pairs={{0,1},{1,0},{2,3},{3,2},{4,5},{5,4},{6,7},{7,6},{8,9},{9,8},{10,11... | collective-permute-start | bytes 196616 | tf_op jit(solution)/shard_map/ppermute | solution.py:174
  26.0 4.5 %collective-permute-start.15 = (bf16[64,512]{1,0:T(8,128)(2,1)S(1)}, bf16[64,512]{1,0:T(8,128)(2,1)S(1)}, u32[]{:S(2)}, u32[]{:S(2)}) collective-permute-start(bf16[64,512]{1,0:T(8,128)(2,1)S(1)} %far.3.hb), channel_id=1, source_target_pairs={{0,2},{1,3},{2,0},{3,1},{4,6},{5,7},{6,4},{7,5},{8,10},{9,11},{10,... | collective-permute-start | bytes 196616 | tf_op jit(solution)/shard_map/ppermute | solution.py:171
  27.6 4.0 %collective-permute-start.14 = (bf16[64,512]{1,0:T(8,128)(2,1)S(1)}, bf16[64,512]{1,0:T(8,128)(2,1)S(1)}, u32[]{:S(2)}, u32[]{:S(2)}) collective-permute-start(bf16[64,512]{1,0:T(8,128)(2,1)S(1)} %collective-permute-done.13.ha), channel_id=1, source_target_pairs={{0,1},{1,0},{2,3},{3,2},{4,5},{5,4},{6,7},{7,6},{8,9},{9,8},{10,11... | collective-permute-start | bytes 196616 | tf_op jit(solution)/shard_map/ppermute | solution.py:174
  30.5 1.3 %collective-permute-start.16 = (bf16[64,512]{1,0:T(8,128)(2,1)S(1)}, bf16[64,512]{1,0:T(8,128)(2,1)S(1)}, u32[]{:S(2)}, u32[]{:S(2)}) collective-permute-start(bf16[64,512]{1,0:T(8,128)(2,1)S(1)} %collective-permute-done.15.hb), channel_id=1, source_target_pairs={{0,1},{1,0},{2,3},{3,2},{4,5},{5,4},{6,7},{7,6},{8,9},{9,8},{10,11... | collective-permute-start | bytes 196616 | tf_op jit(solution)/shard_map/ppermute | solution.py:174

commit v3 on v2

v3 whole, which is shorter than its diff:
```python
import functools

import jax
import jax.numpy as jnp
from jax import lax
from jax.experimental import pallas as pl
from jax.experimental.pallas import tpu as pltpu
from jax.sharding import PartitionSpec as P

EXPERTS = 256
TOP = 8
BF16 = jnp.bfloat16
F32 = jnp.float32
VMEM = pl.BlockSpec(memory_space=pltpu.VMEM)
ANY = pl.BlockSpec(memory_space=pl.ANY)
HBM = pl.BlockSpec(memory_space=pltpu.HBM)
LIMIT = 40 * 1024 * 1024


DISTANCE = ((6, 2, 4), (7, 3, 5))
PARTS = ((0,), (1, 2), (3,))
ORDER = sum(PARTS, ())


def distance(core, k):
    return jnp.where(core == 0, DISTANCE[0][k], DISTANCE[1][k])


def dot(a, b):
    return lax.dot_general(a, b, (((1,), (0,)), ((), ())), preferred_element_type=F32)


def weight_copies(gate_hbm, up_hbm, w_ref, sems, chip):
    depth = w_ref.shape[1]
    at = pl.ds(pl.multiple_of(((lax.axis_index("tp") >> 1) ^ chip) * depth, depth), depth)
    return [pltpu.make_async_copy(w.at[0, at, :], w_ref.at[i], sems.at[i]) for i, w in enumerate((gate_hbm, up_hbm))]


def prepare_kernel(capacity, ids_hbm, tok_hbm, pick_ref, mine_ref, stay_ref, side_ref, ids_ref, tok_ref, sems):
    get = [
        pltpu.make_async_copy(ids_hbm, ids_ref, sems.at[0]),
        pltpu.make_async_copy(tok_hbm, tok_ref, sems.at[1]),
    ]
    for g in get:
        g.start()
    rows = ids_ref.shape[1]
    before = lax.broadcasted_iota(jnp.int32, (rows, rows), 0)
    after = lax.broadcasted_iota(jnp.int32, (rows, rows), 1)
    upto = jnp.where(before <= after, 1.0, 0.0).astype(BF16)
    want = lax.broadcasted_iota(jnp.int32, (5, capacity, rows), 1).astype(F32)
    core = lax.axis_index("tp") & 1
    step = lax.broadcasted_iota(jnp.int32, (8, rows), 0)
    offset = sum(jnp.where(step == k + 2, distance(core, k), 0) for k in range(3)) + jnp.where(step == 1, 1, 0)
    expert = lax.axis_index("ep") ^ offset
    get[0].wait()
    ids = ids_ref[...]
    hit = ids[0:1, :] == expert
    for k in range(1, ids.shape[0]):
        hit = hit | (ids[k : k + 1, :] == expert)
    count = dot(jnp.where(hit, 1.0, 0.0).astype(BF16), upto)
    slot = jnp.where(hit, count - 1.0, -1.0)[:5]
    pick = jnp.where(slot[:, None, :] == want, 1.0, 0.0)
    pick = pick.reshape(5 * capacity, rows).astype(BF16)
    pick_ref[...] = pick[2 * capacity :]
    get[1].wait()
    taken = dot(pick, tok_ref[...]).astype(BF16)
    stay_ref[...] = taken[:capacity]
    side_ref[...] = taken[capacity : 2 * capacity]
    mine_ref[...] = taken[2 * capacity :]


def select_kernel(capacity, pick_ref, mine_ref, sib_ref, *outs):
    core = lax.axis_index("tp") & 1
    depth = sib_ref.shape[1]
    here = pl.ds(pl.multiple_of(core * depth, depth), depth)
    there = pl.ds(pl.multiple_of((1 - core) * depth, depth), depth)
    other = dot(pick_ref[...], sib_ref[...]).astype(BF16)
    for k, out in enumerate(outs):
        rows = slice(k * capacity, (k + 1) * capacity)
        out[:, here] = mine_ref[rows, :]
        out[:, there] = other[rows]


def load_kernel(after_ref, gate_hbm, up_hbm, near_ref, far_ref, near_sems, far_sems):
    get = weight_copies(gate_hbm, up_hbm, near_ref, near_sems, 0) + weight_copies(gate_hbm, up_hbm, far_ref, far_sems, 1)
    for g in get:
        g.start()
    for g in get:
        g.wait()


def assemble(capacity, one_ref, other_ref, x_ref):
    core = lax.axis_index("tp") & 1
    depth = x_ref.shape[1] // 2
    for c, ref in ((core, one_ref), (1 - core, other_ref)):
        lanes = pl.ds(pl.multiple_of(c * depth, depth), depth)
        for at, k in enumerate(ORDER):
            block = ref[pl.ds(at * capacity, capacity), :]
            if k == 0:
                x_ref[pl.ds(0, capacity), lanes] = block[:, :depth]
                x_ref[pl.ds(capacity, capacity), lanes] = block[:, depth:]
            else:
                x_ref[pl.ds(pl.multiple_of(distance(c, k - 1) * capacity, capacity), capacity), :] = block


def near_kernel(capacity, own_ref, sib_ref, w_ref, g_ref, u_ref, x_ref):
    assemble(capacity, own_ref, sib_ref, x_ref)
    g_ref[...] = dot(x_ref[...], w_ref[0])
    u_ref[...] = dot(x_ref[...], w_ref[1])


def far_kernel(capacity, far_ref, diag_ref, w_ref, g_ref, u_ref, h_ref, x_ref):
    assemble(capacity, far_ref, diag_ref, x_ref)
    gate = g_ref[...] + dot(x_ref[...], w_ref[0])
    up = u_ref[...] + dot(x_ref[...], w_ref[1])
    h_ref[...] = (gate / (1.0 + jnp.exp(-gate)) * up).astype(BF16)


def write_block(flip, h, factor, index, hess_hbm, buf, sems):
    wide = h.shape[1]
    part = wide // 4
    at = pl.ds(pl.multiple_of(index * wide, wide), wide)
    copies = []
    for i in range(4):
        rows = pl.ds(i * part, part)
        buf[rows, :] = dot(flip[rows, :], h) * factor
        copies.append(pltpu.make_async_copy(buf.at[rows, :], hess_hbm.at[0, rows, at], sems.at[i]))
        copies[-1].start()
    return copies


def hess_near_kernel(factor, capacity, h_ref, sib_ref, flip_ref, hid_hbm, hess_hbm, buf, sems, out_sems):
    t = lax.axis_index("tp")
    e = lax.axis_index("ep")
    copies = []
    for o in range(8):
        src = h_ref.at[pl.ds(o * capacity, capacity), :]
        at = pl.ds(pl.multiple_of((e ^ o) * capacity, capacity), capacity)
        copies.append(pltpu.make_async_copy(src, hid_hbm.at[0, at, :], out_sems.at[o]))
        copies[-1].start()
    flip_ref[...] = h_ref[...].astype(F32).T.astype(BF16)
    copies += write_block(flip_ref, h_ref[...], factor, t, hess_hbm, buf.at[0], sems.at[0])
    copies += write_block(flip_ref, sib_ref[...], factor, t ^ 1, hess_hbm, buf.at[1], sems.at[1])
    for c in copies:
        c.wait()


def hess_far_kernel(factor, which, flip_ref, h_ref, hess_in, hess_hbm, buf, sems):
    t = lax.axis_index("tp")
    for c in write_block(flip_ref, h_ref[...], factor, t ^ which, hess_hbm, buf, sems):
        c.wait()


def call(kernel, out_shape, in_specs, out_specs, scratch=(), name=None, aliases={}, flops=0, moved=0, limit=LIMIT):
    return pl.pallas_call(
        kernel,
        out_shape=out_shape,
        in_specs=in_specs,
        out_specs=out_specs,
        scratch_shapes=list(scratch),
        input_output_aliases=aliases,
        name=name,
        cost_estimate=pl.CostEstimate(flops=flops, bytes_accessed=moved, transcendentals=0),
        compiler_params=pltpu.CompilerParams(vmem_limit_bytes=limit),
    )


def tie(x, after):
    return lax.optimization_barrier((x, after))[0]


def paired(tokens, expert_ids, gate_weight, up_weight):
    groups = 8
    tok_rows, depth = tokens.shape
    capacity = 2 * tok_rows * TOP // EXPERTS
    slots = groups * capacity
    wide = gate_weight.shape[2]
    full = wide * 4
    S = jax.ShapeDtypeStruct
    D = pltpu.SemaphoreType.DMA
    V = pltpu.VMEM

    def chips(x):
        return lax.ppermute(x, "tp", [(i, i ^ 2) for i in range(4)])

    def cores(x):
        return lax.ppermute(x, "tp", [(i, i ^ 1) for i in range(4)])

    def spread(k, x):
        pairs = [(e * 4 + t, (e ^ DISTANCE[t & 1][k]) * 4 + t) for e in range(8) for t in range(4)]
        return lax.ppermute(x, ("ep", "tp"), pairs)

    sib_tokens = cores(tokens)
    weights = 4 * 2 * depth * 2 * wide
    ids, toks, gate_w, up_w = (
        pltpu.with_memory_space_constraint(a, pltpu.HBM) for a in (expert_ids.T, tokens, gate_weight, up_weight)
    )
    single = S((capacity, depth), BF16)
    pick, mine, stay, side = call(
        functools.partial(prepare_kernel, capacity),
        (S((3 * capacity, tok_rows), BF16), S((3 * capacity, depth), BF16), single, single),
        [HBM] * 2, (VMEM,) * 4,
        (V(ids.shape, jnp.int32), V(tokens.shape, BF16), D((2,))), name="prepare",
        flops=10 * capacity * tok_rows * depth, moved=tokens.size * 2,
    )(ids, toks)
    side = lax.ppermute(side, "ep", [(e, e ^ 1) for e in range(8)])
    out = call(
        functools.partial(select_kernel, capacity),
        (S((capacity, 2 * depth), BF16),) * 3, [VMEM] * 3, (VMEM,) * 3, name="select",
        flops=6 * capacity * tok_rows * depth,
    )(pick, mine, sib_tokens)
    got = [jnp.concatenate([stay, side], axis=1)] + [spread(k, out[k]) for k in range(3)]
    half_w = V((2, 2 * depth, wide), BF16)
    part = S((slots, wide), F32)
    work = 4 * slots * depth * 2 * wide
    parts = [jnp.concatenate([got[k] for k in part]) for part in PARTS]
    far = jnp.concatenate([chips(part) for part in parts])
    own = jnp.concatenate(parts)
    sib = cores(own)
    near_w, far_w = call(
        load_kernel, (half_w, half_w), [VMEM] + [HBM] * 2, (VMEM,) * 2, (D((2,)), D((2,))), name="load", moved=weights,
    )(own, gate_w, up_w)
    far = tie(far, far_w)
    diag = cores(far)
    x = V((slots, 2 * depth), BF16)
    gate, up = call(
        functools.partial(near_kernel, capacity), (part, part), [VMEM] * 3, (VMEM,) * 2, (x,), name="near",
        flops=work, moved=weights // 2,
    )(own, tie(sib, far), near_w)
    hidden = call(
        functools.partial(far_kernel, capacity), S((slots, wide), BF16), [VMEM] * 5, VMEM, (x,), name="far",
        flops=work, moved=weights // 2,
    )(far, diag, far_w, gate, up)

    factor = 2.0 / slots
    hess_shape = S((1, wide, full), F32)
    block = wide * wide * 4
    far_h = chips(hidden)
    sib_h = cores(hidden)
    flip, hidden, hess = call(
        functools.partial(hess_near_kernel, factor, capacity),
        (S((wide, slots), BF16), S((1, slots, wide), BF16), hess_shape),
        [VMEM] * 2, (VMEM, ANY, ANY), (V((2, wide, wide), F32), D((2, 4)), D((8,))), name="hess_near",
        flops=4 * slots * wide * wide, moved=2 * block,
    )(hidden, sib_h)

    def other(which, h, hess):
        return call(
            functools.partial(hess_far_kernel, factor, which), hess_shape,
            [VMEM, VMEM, ANY], ANY, (V((wide, wide), F32), D((4,))), name="hess_%d" % which, aliases={2: 0},
            flops=2 * slots * wide * wide, moved=block,
        )(flip, h, hess)

    far_h = tie(far_h, flip)
    diag_h = cores(far_h)
    hess = other(2, far_h, hess)
    hess = other(3, diag_h, hess)
    return hidden, hess


def general(tokens, expert_ids, gate_weight, up_weight):
    groups = lax.axis_size("ep")
    capacity = 2 * tokens.shape[0] * TOP // EXPERTS
    slots = groups * capacity
    member = jnp.any(expert_ids[:, :, None] == jnp.arange(groups, dtype=jnp.int32), axis=1).astype(jnp.int32)
    rank = jnp.cumsum(member, axis=0) - 1
    chosen = (member.T[:, None, :] > 0) & (rank.T[:, None, :] == jnp.arange(capacity, dtype=jnp.int32)[None, :, None])
    outgoing = jnp.einsum("gcj,jf->gcf", chosen.astype(BF16), tokens, preferred_element_type=F32).astype(BF16)
    arrived = lax.all_to_all(outgoing, "ep", split_axis=0, concat_axis=0, tiled=True)
    routed = lax.all_gather(arrived.reshape(slots, arrived.shape[2]), "tp", axis=1, tiled=True)
    gate = dot(routed, gate_weight[0])
    hidden = (jax.nn.silu(gate) * dot(routed, up_weight[0])).astype(BF16)
    whole = lax.all_gather(hidden, "tp", axis=1, tiled=True)
    hess = lax.dot_general(hidden, whole, (((0,), (0,)), ((), ())), preferred_element_type=F32) * (2.0 / slots)
    return hidden[None], hess[None]


def solution(mesh):
    body = paired if (mesh.shape["ep"], mesh.shape["tp"]) == (8, 4) else general
    return jax.shard_map(
        body,
        mesh=mesh,
        in_specs=(P("ep", "tp"), P("ep", None), P("ep", None, "tp"), P("ep", None, "tp")),
        out_specs=(P("ep", None, "tp"), P("ep", "tp", None)),
        check_vma=False,
    )
```

time: 33.1 us -> 30.9 us (0.934)
  Pallas kernels: 11.5 us -> 10.1 us
  starting transfers between devices: 14.9 us -> 13.5 us
  waiting for transfers between devices: 5.71 us -> 6.39 us
    ppermute x0 -> x1, starting transfers between devices: none -> 2.59 us  [paired(): side = lax.ppermute(side, 'ep', [(e, e ^ 1) for e in range(8)])]
    ppermute x4 -> x3, starting transfers between devices: 6.86 us -> 4.66 us  [spread(): return lax.ppermute(x, ('ep', 'tp'), pairs)]
    ppermute x9 -> x5, starting transfers between devices: 2.68 us -> 1.08 us  [cores(): return lax.ppermute(x, 'tp', [(i, i ^ 1) for i in range(4)])]
    pallas_call x5 -> x4, Pallas kernels: 7.16 us -> 5.78 us  [the longest x1 3.2 us: paired(): call(load_kernel, (half_w, half_w), [VMEM] + [HBM] * 2, (VMEM,) * 2, (D((...]
    ppermute x9 -> x5, waiting for transfers between devices: 0.08 us -> 0.82 us  [cores(): return lax.ppermute(x, 'tp', [(i, i ^ 1) for i in range(4)])]
    ppermute x4, waiting for transfers between devices: 3.46 us -> 2.83 us  [chips(): return lax.ppermute(x, 'tp', [(i, i ^ 2) for i in range(4)])]
    ppermute x4 -> x3, waiting for transfers between devices: 2.17 us -> 2.73 us  [spread(): return lax.ppermute(x, ('ep', 'tp'), pairs)]
  transfers between devices with their start and end apart: 17 -> 13, of which waited for: 6 -> 6; matrix products, arithmetic and copies ran while one was open for 0% -> 0% of each run, Pallas kernels for 31% -> 27%
where the time goes in v3:
time: 30.9 us; the launch traced here: 30.7 us
  starting transfers between devices  13.5 us (44%)
  Pallas kernels  10.1 us (33%)
  waiting for transfers between devices  6.39 us (21%)
  between operations  0.72 us (2%)
    ppermute x4, starting transfers between devices, chips(): return lax.ppermute(x, 'tp', [(i, i ^ 2) for i in range(4)])  5.13 us
    ppermute x3, starting transfers between devices, spread(): return lax.ppermute(x, ('ep', 'tp'), pairs)  4.66 us
    pallas_call x1, Pallas kernels, paired(): call(load_kernel, (half_w, half_w), [VMEM] + [HBM] * 2, (VMEM,) * 2, (D((...  3.2 us
    ppermute x4, waiting for transfers between devices, chips(): return lax.ppermute(x, 'tp', [(i, i ^ 2) for i in range(4)])  2.83 us
    ppermute x3, waiting for transfers between devices, spread(): return lax.ppermute(x, ('ep', 'tp'), pairs)  2.73 us
    ppermute x1, starting transfers between devices, paired(): side = lax.ppermute(side, 'ep', [(e, e ^ 1) for e in range(8)])  2.59 us
    pallas_call x2, Pallas kernels, other(): call(functools.partial(hess_far_kernel, factor, which), hess_shape, [VMEM...  2.35 us
    pallas_call x1, Pallas kernels, paired(): call(functools.partial(hess_near_kernel, factor, capacity), (S((wide, slo...  1.74 us
  transfers between devices with their start and end apart: 13, of which 6 were waited for; matrix products, arithmetic and copies ran while one was open for 0% of the time, Pallas kernels for 27%

profile of v3, /device:TPU:0, one launch (start us, length us, event | category | flops | bytes accessed | tf_op | source)
XLA Modules:
  0.0 30.7 jit_solution(17353598530263130963)
XLA Ops:
  0.6 0.5 %collective-permute-start.2 = (bf16[256,896]{1,0:T(8,128)(2,1)}, bf16[256,896]{1,0:T(8,128)(2,1)S(1)}, u32[]{:S(2)}, u32[]{:S(2)}) collective-permute-start(bf16[256,896]{1,0:T(8,128)(2,1)} %tok_hbm.1), channel_id=1, source_target_pairs={{0,1},{1,0},{2,3},{3,2},{4,5},{5,4},{6,7},{7,6},{8,9},{9,8},{10,11... | collective-permute-start | bytes 1376264 | tf_op jit(solution)/shard_map/ppermute | solution.py:187
  1.1 1.3 %prepare.1 = (bf16[48,256]{1,0:T(8,128)(2,1)S(1)}, bf16[48,896]{1,0:T(8,128)(2,1)S(1)}, bf16[16,896]{1,0:T(8,128)(2,1)S(1)}, bf16[16,896]{1,0:T(8,128)(2,1)S(1)}) custom-call(s32[8,256]{1,0:T(8,128)} %bitcast.1, bf16[256,896]{1,0:T(8,128)(2,1)} %tok_hbm.1), custom_call_target="tpu_custom_call" | custom-call | flops 36700160 | bytes 458752 | tf_op jit(solution)/shard_map/prepare/pallas_call | solution.py:199
  2.4 2.6 %collective-permute-start = (bf16[16,896]{1,0:T(8,128)(2,1)S(1)}, bf16[16,896]{1,0:T(8,128)(2,1)S(1)}, u32[]{:S(2)}, u32[]{:S(2)}) collective-permute-start(bf16[16,896]{1,0:T(8,128)(2,1)S(1)} %get-tuple-element.20), channel_id=1, source_target_pairs={{0,4},{4,0},{8,12},{12,8},{16,20},{20,16},{24,28},{28,24},{1,5},{5... | collective-permute-start | bytes 86024 | tf_op jit(solution)/shard_map/ppermute | solution.py:206
  5.0 0.0 collective-permute-done.2.sib_ref
  5.0 0.2 select.1
  5.2 3.7 %collective-permute-start.3 = (bf16[16,1792]{1,0:T(8,128)(2,1)S(1)}, bf16[16,1792]{1,0:T(8,128)(2,1)S(1)}, u32[]{:S(2)}, u32[]{:S(2)}) collective-permute-start(bf16[16,1792]{1,0:T(8,128)(2,1)S(1)} %get-tuple-element.23), channel_id=1, source_target_pairs={{0,24},{1,29},{2,26},{3,31},{4,28},{5,25},{6,30},{7,27},{8,16},{9,... | collective-permute-start | bytes 172040 | tf_op jit(solution)/shard_map/ppermute | solution.py:191
  8.9 0.0 collective-permute-start.4
  8.9 0.0 collective-permute-done
  8.9 1.6 %collective-permute-start.1 = (bf16[16,1792]{1,0:T(8,128)(2,1)S(1)}, bf16[16,1792]{1,0:T(8,128)(2,1)S(1)}, u32[]{:S(2)}, u32[]{:S(2)}) collective-permute-start(bf16[16,1792]{1,0:T(8,128)(2,1)S(1)} %constant_dynamic-update-slice_fusion), channel_id=1, source_target_pairs={{0,2},{1,3},{2,0},{3,1},{4,6},{5,7},{6,4},{7,5},{8,10},{9,11},{10,... | collective-permute-start | bytes 172040 | tf_op jit(solution)/shard_map/ppermute | solution.py:184
  10.5 1.0 %collective-permute-start.6 = (bf16[16,1792]{1,0:T(8,128)(2,1)S(1)}, bf16[16,1792]{1,0:T(8,128)(2,1)S(1)}, u32[]{:S(2)}, u32[]{:S(2)}) collective-permute-start(bf16[16,1792]{1,0:T(8,128)(2,1)S(1)} %get-tuple-element.25), channel_id=1, source_target_pairs={{0,16},{1,21},{2,18},{3,23},{4,20},{5,17},{6,22},{7,19},{8,24},{9,... | collective-permute-start | bytes 172040 | tf_op jit(solution)/shard_map/ppermute | solution.py:191
  11.5 0.0 collective-permute-done.3
  11.5 2.1 %collective-permute-done.4 = bf16[16,1792]{1,0:T(8,128)(2,1)S(1)} collective-permute-done((bf16[16,1792]{1,0:T(8,128)(2,1)S(1)}, bf16[16,1792]{1,0:T(8,128)(2,1)S(1)}, u32[]{:S(2)}, u32[]{:S(2)}) %collective-permute-start.4) | collective-permute-done | bytes 57376 | tf_op jit(solution)/shard_map/ppermute | solution.py:191
  13.6 1.6 %collective-permute-start.5 = (bf16[32,1792]{1,0:T(8,128)(2,1)S(1)}, bf16[32,1792]{1,0:T(8,128)(2,1)S(1)}, u32[]{:S(2)}, u32[]{:S(2)}) collective-permute-start(bf16[32,1792]{1,0:T(8,128)(2,1)S(1)} %pad_maximum_fusion.2), channel_id=1, source_target_pairs={{0,2},{1,3},{2,0},{3,1},{4,6},{5,7},{6,4},{7,5},{8,10},{9,11},{10,... | collective-permute-start | bytes 344072 | tf_op jit(solution)/shard_map/ppermute | solution.py:184
  15.1 0.6 %collective-permute-done.6 = bf16[16,1792]{1,0:T(8,128)(2,1)S(1)} collective-permute-done((bf16[16,1792]{1,0:T(8,128)(2,1)S(1)}, bf16[16,1792]{1,0:T(8,128)(2,1)S(1)}, u32[]{:S(2)}, u32[]{:S(2)}) %collective-permute-start.6) | collective-permute-done | bytes 57376 | tf_op jit(solution)/shard_map/ppermute | solution.py:191
  15.8 0.5 %collective-permute-start.7 = (bf16[16,1792]{1,0:T(8,128)(2,1)S(1)}, bf16[16,1792]{1,0:T(8,128)(2,1)S(1)}, u32[]{:S(2)}, u32[]{:S(2)}) collective-permute-start(bf16[16,1792]{1,0:T(8,128)(2,1)S(1)} %collective-permute-done.6), channel_id=1, source_target_pairs={{0,2},{1,3},{2,0},{3,1},{4,6},{5,7},{6,4},{7,5},{8,10},{9,11},{10,... | collective-permute-start | bytes 172040 | tf_op jit(solution)/shard_map/ppermute | solution.py:184
  16.3 0.1 collective-permute-start.9
  16.4 3.2 %load.1 = (bf16[2,1792,512]{2,1,0:T(8,128)(2,1)S(1)}, bf16[2,1792,512]{2,1,0:T(8,128)(2,1)S(1)}) custom-call(bf16[64,1792]{1,0:T(8,128)(2,1)S(1)} %pad_maximum_fusion.1.after_ref.own_ref, bf16[1,3584,512]{2,1,0:T(8,128)(2,1)} %gate_hbm.1, bf16[1,3584,512]{2,1,0:T(8,128)(2,1)} %up_hbm.1), custom_call_target="tpu_custom_call" | custom-call | bytes 7340032 | tf_op jit(solution)/shard_map/load/pallas_call | solution.py:220
  19.6 0.0 collective-permute-done.1
  19.6 0.3 %collective-permute-done.7 = bf16[16,1792]{1,0:T(8,128)(2,1)S(1)} collective-permute-done((bf16[16,1792]{1,0:T(8,128)(2,1)S(1)}, bf16[16,1792]{1,0:T(8,128)(2,1)S(1)}, u32[]{:S(2)}, u32[]{:S(2)}) %collective-permute-start.7) | collective-permute-done | bytes 57376 | tf_op jit(solution)/shard_map/ppermute | solution.py:184
  20.0 0.2 collective-permute-start.8
  20.2 0.0 collective-permute-done.9.sib_ref
  20.2 0.6 %near.1 = (f32[128,512]{1,0:T(8,128)S(1)}, f32[128,512]{1,0:T(8,128)S(1)}) custom-call(bf16[64,1792]{1,0:T(8,128)(2,1)S(1)} %pad_maximum_fusion.1.after_ref.own_ref, bf16[64,1792]{1,0:T(8,128)(2,1)S(1)} %collective-permute-done.9.sib_ref, bf16[2,1792,512]{2,1,0:T(8,128)(2,1)S(1)} %get-tuple-element.29.w_ref), custom_call_target="tpu_custom_call" | custom-call | flops 469762048 | bytes 3670016 | tf_op jit(solution)/shard_map/near/pallas_call | solution.py:226
  20.9 0.7 %collective-permute-done.8.diag_ref = bf16[64,1792]{1,0:T(8,128)(2,1)S(1)} collective-permute-done((bf16[64,1792]{1,0:T(8,128)(2,1)S(1)}, bf16[64,1792]{1,0:T(8,128)(2,1)S(1)}, u32[]{:S(2)}, u32[]{:S(2)}) %collective-permute-start.8) | collective-permute-done | bytes 229408 | tf_op jit(solution)/shard_map/ppermute | solution.py:187
  21.5 0.7 %far.1.h_ref = bf16[128,512]{1,0:T(8,128)(2,1)S(1)} custom-call(bf16[64,1792]{1,0:T(8,128)(2,1)S(1)} %pad_maximum_fusion.far_ref, bf16[64,1792]{1,0:T(8,128)(2,1)S(1)} %collective-permute-done.8.diag_ref, bf16[2,1792,512]{2,1,0:T(8,128)(2,1)S(1)} %get-tuple-element.26.w_ref, f32[128,512]{1,0:T(8,128)S(1)} %get-tuple-element.30.g_ref, ...), custom_call_target="tpu_custom_call" | custom-call | flops 469762048 | bytes 3670016 | tf_op jit(solution)/shard_map/far/pallas_call | solution.py:230
  22.2 0.2 collective-permute-start.10
  22.4 1.5 %collective-permute-start.11 = (bf16[128,512]{1,0:T(8,128)(2,1)S(1)}, bf16[128,512]{1,0:T(8,128)(2,1)S(1)}, u32[]{:S(2)}, u32[]{:S(2)}) collective-permute-start(bf16[128,512]{1,0:T(8,128)(2,1)S(1)} %far.1.h_ref), channel_id=1, source_target_pairs={{0,2},{1,3},{2,0},{3,1},{4,6},{5,7},{6,4},{7,5},{8,10},{9,11},{10,... | collective-permute-start | bytes 393224 | tf_op jit(solution)/shard_map/ppermute | solution.py:184
  23.9 0.0 collective-permute-done.10.sib_ref
  23.9 1.7 %hess_near.1 = (bf16[512,128]{1,0:T(8,128)(2,1)S(1)}, bf16[1,128,512]{2,1,0:T(8,128)(2,1)}, f32[1,512,2048]{2,1,0:T(8,128)}) custom-call(bf16[128,512]{1,0:T(8,128)(2,1)S(1)} %far.1.h_ref, bf16[128,512]{1,0:T(8,128)(2,1)S(1)} %collective-permute-done.10.sib_ref), custom_call_target="tpu_custom_call" | custom-call | flops 134217728 | bytes 2097152 | tf_op jit(solution)/shard_map/hess_near/pallas_call | solution.py:240
  25.7 2.5 %collective-permute-done.11.h_ref = bf16[128,512]{1,0:T(8,128)(2,1)S(1)} collective-permute-done((bf16[128,512]{1,0:T(8,128)(2,1)S(1)}, bf16[128,512]{1,0:T(8,128)(2,1)S(1)}, u32[]{:S(2)}, u32[]{:S(2)}) %collective-permute-start.11) | collective-permute-done | bytes 131104 | tf_op jit(solution)/shard_map/ppermute | solution.py:184
  28.2 1.2 %hess_2.1.hess_in = f32[1,512,2048]{2,1,0:T(8,128)} custom-call(bf16[512,128]{1,0:T(8,128)(2,1)S(1)} %get-tuple-element.33.flip_ref, bf16[128,512]{1,0:T(8,128)(2,1)S(1)} %collective-permute-done.11.h_ref, f32[1,512,2048]{2,1,0:T(8,128)} %get-tuple-element.35.hess_in), custom_call_target="tpu_custom_call", output_to_operand_aliasing={{}: (2, {})} | custom-call | flops 67108864 | bytes 1048576 | tf_op jit(solution)/shard_map/hess_2/pallas_call | solution.py:248
  29.4 0.2 collective-permute-done.12.h_ref
  29.5 1.2 %hess_3.1 = f32[1,512,2048]{2,1,0:T(8,128)} custom-call(bf16[512,128]{1,0:T(8,128)(2,1)S(1)} %get-tuple-element.33.flip_ref, bf16[128,512]{1,0:T(8,128)(2,1)S(1)} %collective-permute-done.12.h_ref, f32[1,512,2048]{2,1,0:T(8,128)} %hess_2.1.hess_in), custom_call_target="tpu_custom_call", output_to_operand_aliasing={{}: (2, {})} | custom-call | flops 67108864 | bytes 1048576 | tf_op jit(solution)/shard_map/hess_3/pallas_call | solution.py:248
  (7 shorter events, 0.1 us)
Async XLA Ops:
  0.6 4.4 %collective-permute-start.2 = (bf16[256,896]{1,0:T(8,128)(2,1)}, bf16[256,896]{1,0:T(8,128)(2,1)S(1)}, u32[]{:S(2)}, u32[]{:S(2)}) collective-permute-start(bf16[256,896]{1,0:T(8,128)(2,1)} %tok_hbm.1), channel_id=1, source_target_pairs={{0,1},{1,0},{2,3},{3,2},{4,5},{5,4},{6,7},{7,6},{8,9},{9,8},{10,11... | collective-permute-start | bytes 1376264 | tf_op jit(solution)/shard_map/ppermute | solution.py:187
  2.4 6.5 %collective-permute-start = (bf16[16,896]{1,0:T(8,128)(2,1)S(1)}, bf16[16,896]{1,0:T(8,128)(2,1)S(1)}, u32[]{:S(2)}, u32[]{:S(2)}) collective-permute-start(bf16[16,896]{1,0:T(8,128)(2,1)S(1)} %get-tuple-element.20), channel_id=1, source_target_pairs={{0,4},{4,0},{8,12},{12,8},{16,20},{20,16},{24,28},{28,24},{1,5},{5... | collective-permute-start | bytes 86024 | tf_op jit(solution)/shard_map/ppermute | solution.py:206
  5.2 6.2 %collective-permute-start.3 = (bf16[16,1792]{1,0:T(8,128)(2,1)S(1)}, bf16[16,1792]{1,0:T(8,128)(2,1)S(1)}, u32[]{:S(2)}, u32[]{:S(2)}) collective-permute-start(bf16[16,1792]{1,0:T(8,128)(2,1)S(1)} %get-tuple-element.23), channel_id=1, source_target_pairs={{0,24},{1,29},{2,26},{3,31},{4,28},{5,25},{6,30},{7,27},{8,16},{9,... | collective-permute-start | bytes 172040 | tf_op jit(solution)/shard_map/ppermute | solution.py:191
  8.9 4.7 %collective-permute-start.4 = (bf16[16,1792]{1,0:T(8,128)(2,1)S(1)}, bf16[16,1792]{1,0:T(8,128)(2,1)S(1)}, u32[]{:S(2)}, u32[]{:S(2)}) collective-permute-start(bf16[16,1792]{1,0:T(8,128)(2,1)S(1)} %get-tuple-element.24), channel_id=1, source_target_pairs={{0,8},{1,13},{2,10},{3,15},{4,12},{5,9},{6,14},{7,11},{8,0},{9,5},... | collective-permute-start | bytes 172040 | tf_op jit(solution)/shard_map/ppermute | solution.py:191
  8.9 10.7 %collective-permute-start.1 = (bf16[16,1792]{1,0:T(8,128)(2,1)S(1)}, bf16[16,1792]{1,0:T(8,128)(2,1)S(1)}, u32[]{:S(2)}, u32[]{:S(2)}) collective-permute-start(bf16[16,1792]{1,0:T(8,128)(2,1)S(1)} %constant_dynamic-update-slice_fusion), channel_id=1, source_target_pairs={{0,2},{1,3},{2,0},{3,1},{4,6},{5,7},{6,4},{7,5},{8,10},{9,11},{10,... | collective-permute-start | bytes 172040 | tf_op jit(solution)/shard_map/ppermute | solution.py:184
  10.5 5.3 %collective-permute-start.6 = (bf16[16,1792]{1,0:T(8,128)(2,1)S(1)}, bf16[16,1792]{1,0:T(8,128)(2,1)S(1)}, u32[]{:S(2)}, u32[]{:S(2)}) collective-permute-start(bf16[16,1792]{1,0:T(8,128)(2,1)S(1)} %get-tuple-element.25), channel_id=1, source_target_pairs={{0,16},{1,21},{2,18},{3,23},{4,20},{5,17},{6,22},{7,19},{8,24},{9,... | collective-permute-start | bytes 172040 | tf_op jit(solution)/shard_map/ppermute | solution.py:191
  13.6 6.4 %collective-permute-start.5 = (bf16[32,1792]{1,0:T(8,128)(2,1)S(1)}, bf16[32,1792]{1,0:T(8,128)(2,1)S(1)}, u32[]{:S(2)}, u32[]{:S(2)}) collective-permute-start(bf16[32,1792]{1,0:T(8,128)(2,1)S(1)} %pad_maximum_fusion.2), channel_id=1, source_target_pairs={{0,2},{1,3},{2,0},{3,1},{4,6},{5,7},{6,4},{7,5},{8,10},{9,11},{10,... | collective-permute-start | bytes 344072 | tf_op jit(solution)/shard_map/ppermute | solution.py:184
  15.8 4.2 %collective-permute-start.7 = (bf16[16,1792]{1,0:T(8,128)(2,1)S(1)}, bf16[16,1792]{1,0:T(8,128)(2,1)S(1)}, u32[]{:S(2)}, u32[]{:S(2)}) collective-permute-start(bf16[16,1792]{1,0:T(8,128)(2,1)S(1)} %collective-permute-done.6), channel_id=1, source_target_pairs={{0,2},{1,3},{2,0},{3,1},{4,6},{5,7},{6,4},{7,5},{8,10},{9,11},{10,... | collective-permute-start | bytes 172040 | tf_op jit(solution)/shard_map/ppermute | solution.py:184
  16.3 3.9 %collective-permute-start.9 = (bf16[64,1792]{1,0:T(8,128)(2,1)S(1)}, bf16[64,1792]{1,0:T(8,128)(2,1)S(1)}, u32[]{:S(2)}, u32[]{:S(2)}) collective-permute-start(bf16[64,1792]{1,0:T(8,128)(2,1)S(1)} %pad_maximum_fusion.1.after_ref.own_ref), channel_id=1, source_target_pairs={{0,1},{1,0},{2,3},{3,2},{4,5},{5,4},{6,7},{7,6},{8,9},{9,8},{10,11... | collective-permute-start | bytes 688136 | tf_op jit(solution)/shard_map/ppermute | solution.py:187
  20.0 1.6 %collective-permute-start.8 = (bf16[64,1792]{1,0:T(8,128)(2,1)S(1)}, bf16[64,1792]{1,0:T(8,128)(2,1)S(1)}, u32[]{:S(2)}, u32[]{:S(2)}) collective-permute-start(bf16[64,1792]{1,0:T(8,128)(2,1)S(1)} %pad_maximum_fusion.far_ref), channel_id=1, source_target_pairs={{0,1},{1,0},{2,3},{3,2},{4,5},{5,4},{6,7},{7,6},{8,9},{9,8},{10,11... | collective-permute-start | bytes 688136 | tf_op jit(solution)/shard_map/ppermute | solution.py:187
  22.2 1.7 %collective-permute-start.10 = (bf16[128,512]{1,0:T(8,128)(2,1)S(1)}, bf16[128,512]{1,0:T(8,128)(2,1)S(1)}, u32[]{:S(2)}, u32[]{:S(2)}) collective-permute-start(bf16[128,512]{1,0:T(8,128)(2,1)S(1)} %far.1.h_ref), channel_id=1, source_target_pairs={{0,1},{1,0},{2,3},{3,2},{4,5},{5,4},{6,7},{7,6},{8,9},{9,8},{10,11... | collective-permute-start | bytes 393224 | tf_op jit(solution)/shard_map/ppermute | solution.py:187
  22.4 5.7 %collective-permute-start.11 = (bf16[128,512]{1,0:T(8,128)(2,1)S(1)}, bf16[128,512]{1,0:T(8,128)(2,1)S(1)}, u32[]{:S(2)}, u32[]{:S(2)}) collective-permute-start(bf16[128,512]{1,0:T(8,128)(2,1)S(1)} %far.1.h_ref), channel_id=1, source_target_pairs={{0,2},{1,3},{2,0},{3,1},{4,6},{5,7},{6,4},{7,5},{8,10},{9,11},{10,... | collective-permute-start | bytes 393224 | tf_op jit(solution)/shard_map/ppermute | solution.py:184
  28.2 1.3 %collective-permute-start.12 = (bf16[128,512]{1,0:T(8,128)(2,1)S(1)}, bf16[128,512]{1,0:T(8,128)(2,1)S(1)}, u32[]{:S(2)}, u32[]{:S(2)}) collective-permute-start(bf16[128,512]{1,0:T(8,128)(2,1)S(1)} %collective-permute-done.11.h_ref), channel_id=1, source_target_pairs={{0,1},{1,0},{2,3},{3,2},{4,5},{5,4},{6,7},{7,6},{8,9},{9,8},{10,11... | collective-permute-start | bytes 393224 | tf_op jit(solution)/shard_map/ppermute | solution.py:187

commit v4 on v3

--- a/solution.py
+++ b/solution.py
@@ -18,7 +18,7 @@
 
 
 DISTANCE = ((6, 2, 4), (7, 3, 5))
-PARTS = ((0,), (1, 2), (3,))
+PARTS = ((1, 2), (3,), (0,))
 ORDER = sum(PARTS, ())
 
 
@@ -138,9 +138,10 @@
         at = pl.ds(pl.multiple_of((e ^ o) * capacity, capacity), capacity)
         copies.append(pltpu.make_async_copy(src, hid_hbm.at[0, at, :], out_sems.at[o]))
         copies[-1].start()
+    slots = h_ref.shape[0]
     flip_ref[...] = h_ref[...].astype(F32).T.astype(BF16)
     copies += write_block(flip_ref, h_ref[...], factor, t, hess_hbm, buf.at[0], sems.at[0])
-    copies += write_block(flip_ref, sib_ref[...], factor, t ^ 1, hess_hbm, buf.at[1], sems.at[1])
+    copies += write_block(flip_ref, sib_ref[pl.ds(pl.multiple_of((1 - (t & 1)) * slots, slots), slots), :], factor, t ^ 1, hess_hbm, buf.at[1], sems.at[1])
     for c in copies:
         c.wait()
 
@@ -220,8 +221,10 @@
     near_w, far_w = call(
         load_kernel, (half_w, half_w), [VMEM] + [HBM] * 2, (VMEM,) * 2, (D((2,)), D((2,))), name="load", moved=weights,
     )(own, gate_w, up_w)
-    far = tie(far, far_w)
-    diag = cores(far)
+    early = 2 * capacity
+    late = tie(far[early:], (far_w, far[:early]))
+    diag = jnp.concatenate([cores(far[:early]), cores(late)])
+    far = jnp.concatenate([far[:early], late])
     x = V((slots, 2 * depth), BF16)
     gate, up = call(
         functools.partial(near_kernel, capacity), (part, part), [VMEM] * 3, (VMEM,) * 2, (x,), name="near",
@@ -236,13 +239,13 @@
     hess_shape = S((1, wide, full), F32)
     block = wide * wide * 4
     far_h = chips(hidden)
-    sib_h = cores(hidden)
+    pair_h = lax.all_gather(hidden, "tp", axis=0, tiled=True, axis_index_groups=[[0, 1], [2, 3]])
     flip, hidden, hess = call(
         functools.partial(hess_near_kernel, factor, capacity),
         (S((wide, slots), BF16), S((1, slots, wide), BF16), hess_shape),
         [VMEM] * 2, (VMEM, ANY, ANY), (V((2, wide, wide), F32), D((2, 4)), D((8,))), name="hess_near",
         flops=4 * slots * wide * wide, moved=2 * block,
-    )(hidden, sib_h)
+    )(hidden, pair_h)
 
     def other(which, h, hess):
         return call(

time: 30.9 us -> 30.8 us (level)
  waiting for transfers between devices: 6.39 us -> 4.05 us
  blocking collectives: 0 us -> 1.98 us
    all_gather x0 -> x1, blocking collectives: none -> 1.98 us  [paired(): lax.all_gather(hidden, 'tp', axis=0, tiled=True, axis_index_groups=[[0, 1...]
    ppermute x4, waiting for transfers between devices: 2.83 us -> 0.86 us  [chips(): return lax.ppermute(x, 'tp', [(i, i ^ 2) for i in range(4)])]
    ppermute x5, waiting for transfers between devices: 0.82 us -> 0.46 us  [cores(): return lax.ppermute(x, 'tp', [(i, i ^ 1) for i in range(4)])]
where the time goes in v4:
time: 30.8 us; the launch traced here: 30.5 us
  starting transfers between devices  13.6 us (44%)
  Pallas kernels  10.1 us (33%)
  waiting for transfers between devices  4.05 us (13%)
  blocking collectives  1.98 us (6%)
  between operations  0.75 us (2%)
    ppermute x4, starting transfers between devices, chips(): return lax.ppermute(x, 'tp', [(i, i ^ 2) for i in range(4)])  5.2 us
    ppermute x3, starting transfers between devices, spread(): return lax.ppermute(x, ('ep', 'tp'), pairs)  4.66 us
    pallas_call x1, Pallas kernels, paired(): call(load_kernel, (half_w, half_w), [VMEM] + [HBM] * 2, (VMEM,) * 2, (D((...  3.2 us
    ppermute x3, waiting for transfers between devices, spread(): return lax.ppermute(x, ('ep', 'tp'), pairs)  2.73 us
    ppermute x1, starting transfers between devices, paired(): side = lax.ppermute(side, 'ep', [(e, e ^ 1) for e in range(8)])  2.59 us
    pallas_call x2, Pallas kernels, other(): call(functools.partial(hess_far_kernel, factor, which), hess_shape, [VMEM...  2.35 us
    all_gather x1, blocking collectives, paired(): lax.all_gather(hidden, 'tp', axis=0, tiled=True, axis_index_groups=[[0, 1...  1.98 us
    pallas_call x1, Pallas kernels, paired(): call(functools.partial(hess_near_kernel, factor, capacity), (S((wide, slo...  1.74 us
  transfers between devices with their start and end apart: 13, of which 6 were waited for; matrix products, arithmetic and copies ran while one was open for 0% of the time, Pallas kernels for 27%

profile of v4, /device:TPU:0, one launch (start us, length us, event | category | flops | bytes accessed | tf_op | source)
XLA Modules:
  0.0 30.5 jit_solution(14470761665651170402)
XLA Ops:
  0.6 0.5 %collective-permute-start = (bf16[256,896]{1,0:T(8,128)(2,1)}, bf16[256,896]{1,0:T(8,128)(2,1)S(1)}, u32[]{:S(2)}, u32[]{:S(2)}) collective-permute-start(bf16[256,896]{1,0:T(8,128)(2,1)} %tok_hbm.1), channel_id=1, source_target_pairs={{0,1},{1,0},{2,3},{3,2},{4,5},{5,4},{6,7},{7,6},{8,9},{9,8},{10,11... | collective-permute-start | bytes 1376264 | tf_op jit(solution)/shard_map/ppermute | solution.py:188
  1.1 1.3 %prepare.1 = (bf16[48,256]{1,0:T(8,128)(2,1)S(1)}, bf16[48,896]{1,0:T(8,128)(2,1)S(1)}, bf16[16,896]{1,0:T(8,128)(2,1)S(1)}, bf16[16,896]{1,0:T(8,128)(2,1)S(1)}) custom-call(s32[8,256]{1,0:T(8,128)} %bitcast.1, bf16[256,896]{1,0:T(8,128)(2,1)} %tok_hbm.1), custom_call_target="tpu_custom_call" | custom-call | flops 36700160 | bytes 458752 | tf_op jit(solution)/shard_map/prepare/pallas_call | solution.py:200
  2.4 2.6 %collective-permute-start.6 = (bf16[16,896]{1,0:T(8,128)(2,1)S(1)}, bf16[16,896]{1,0:T(8,128)(2,1)S(1)}, u32[]{:S(2)}, u32[]{:S(2)}) collective-permute-start(bf16[16,896]{1,0:T(8,128)(2,1)S(1)} %get-tuple-element.25), channel_id=1, source_target_pairs={{0,4},{4,0},{8,12},{12,8},{16,20},{20,16},{24,28},{28,24},{1,5},{5... | collective-permute-start | bytes 86024 | tf_op jit(solution)/shard_map/ppermute | solution.py:207
  5.0 0.0 collective-permute-done.sib_ref
  5.0 0.2 select.1
  5.2 3.7 %collective-permute-start.1 = (bf16[16,1792]{1,0:T(8,128)(2,1)S(1)}, bf16[16,1792]{1,0:T(8,128)(2,1)S(1)}, u32[]{:S(2)}, u32[]{:S(2)}) collective-permute-start(bf16[16,1792]{1,0:T(8,128)(2,1)S(1)} %get-tuple-element.21), channel_id=1, source_target_pairs={{0,24},{1,29},{2,26},{3,31},{4,28},{5,25},{6,30},{7,27},{8,16},{9,... | collective-permute-start | bytes 172040 | tf_op jit(solution)/shard_map/ppermute | solution.py:192
  8.9 0.0 collective-permute-start.2
  8.9 0.0 collective-permute-done.6
  8.9 1.6 %collective-permute-start.7 = (bf16[16,1792]{1,0:T(8,128)(2,1)S(1)}, bf16[16,1792]{1,0:T(8,128)(2,1)S(1)}, u32[]{:S(2)}, u32[]{:S(2)}) collective-permute-start(bf16[16,1792]{1,0:T(8,128)(2,1)S(1)} %constant_dynamic-update-slice_fusion), channel_id=1, source_target_pairs={{0,2},{1,3},{2,0},{3,1},{4,6},{5,7},{6,4},{7,5},{8,10},{9,11},{10,... | collective-permute-start | bytes 172040 | tf_op jit(solution)/shard_map/ppermute | solution.py:185
  10.5 1.0 %collective-permute-start.4 = (bf16[16,1792]{1,0:T(8,128)(2,1)S(1)}, bf16[16,1792]{1,0:T(8,128)(2,1)S(1)}, u32[]{:S(2)}, u32[]{:S(2)}) collective-permute-start(bf16[16,1792]{1,0:T(8,128)(2,1)S(1)} %get-tuple-element.23), channel_id=1, source_target_pairs={{0,16},{1,21},{2,18},{3,23},{4,20},{5,17},{6,22},{7,19},{8,24},{9,... | collective-permute-start | bytes 172040 | tf_op jit(solution)/shard_map/ppermute | solution.py:192
  11.5 0.0 collective-permute-done.1
  11.5 2.1 %collective-permute-done.2 = bf16[16,1792]{1,0:T(8,128)(2,1)S(1)} collective-permute-done((bf16[16,1792]{1,0:T(8,128)(2,1)S(1)}, bf16[16,1792]{1,0:T(8,128)(2,1)S(1)}, u32[]{:S(2)}, u32[]{:S(2)}) %collective-permute-start.2) | collective-permute-done | bytes 57376 | tf_op jit(solution)/shard_map/ppermute | solution.py:192
  13.6 1.6 %collective-permute-start.3 = (bf16[32,1792]{1,0:T(8,128)(2,1)S(1)}, bf16[32,1792]{1,0:T(8,128)(2,1)S(1)}, u32[]{:S(2)}, u32[]{:S(2)}) collective-permute-start(bf16[32,1792]{1,0:T(8,128)(2,1)S(1)} %pad_maximum_fusion.2), channel_id=1, source_target_pairs={{0,2},{1,3},{2,0},{3,1},{4,6},{5,7},{6,4},{7,5},{8,10},{9,11},{10,... | collective-permute-start | bytes 344072 | tf_op jit(solution)/shard_map/ppermute | solution.py:185
  15.1 0.6 %collective-permute-done.4 = bf16[16,1792]{1,0:T(8,128)(2,1)S(1)} collective-permute-done((bf16[16,1792]{1,0:T(8,128)(2,1)S(1)}, bf16[16,1792]{1,0:T(8,128)(2,1)S(1)}, u32[]{:S(2)}, u32[]{:S(2)}) %collective-permute-start.4) | collective-permute-done | bytes 57376 | tf_op jit(solution)/shard_map/ppermute | solution.py:192
  15.8 0.5 %collective-permute-start.5 = (bf16[16,1792]{1,0:T(8,128)(2,1)S(1)}, bf16[16,1792]{1,0:T(8,128)(2,1)S(1)}, u32[]{:S(2)}, u32[]{:S(2)}) collective-permute-start(bf16[16,1792]{1,0:T(8,128)(2,1)S(1)} %collective-permute-done.4), channel_id=1, source_target_pairs={{0,2},{1,3},{2,0},{3,1},{4,6},{5,7},{6,4},{7,5},{8,10},{9,11},{10,... | collective-permute-start | bytes 172040 | tf_op jit(solution)/shard_map/ppermute | solution.py:185
  16.3 0.1 collective-permute-start.10
  16.4 3.2 %load.1 = (bf16[2,1792,512]{2,1,0:T(8,128)(2,1)S(1)}, bf16[2,1792,512]{2,1,0:T(8,128)(2,1)S(1)}) custom-call(bf16[64,1792]{1,0:T(8,128)(2,1)S(1)} %pad_maximum_fusion.after_ref.own_ref, bf16[1,3584,512]{2,1,0:T(8,128)(2,1)} %gate_hbm.1, bf16[1,3584,512]{2,1,0:T(8,128)(2,1)} %up_hbm.1), custom_call_target="tpu_custom_call" | custom-call | bytes 7340032 | tf_op jit(solution)/shard_map/load/pallas_call | solution.py:221
  19.6 0.0 collective-permute-done.7
  19.6 0.3 %collective-permute-done.5 = bf16[16,1792]{1,0:T(8,128)(2,1)S(1)} collective-permute-done((bf16[16,1792]{1,0:T(8,128)(2,1)S(1)}, bf16[16,1792]{1,0:T(8,128)(2,1)S(1)}, u32[]{:S(2)}, u32[]{:S(2)}) %collective-permute-start.5) | collective-permute-done | bytes 57376 | tf_op jit(solution)/shard_map/ppermute | solution.py:185
  20.0 0.2 collective-permute-start.9
  20.2 0.3 %collective-permute-start.8 = (bf16[32,1792]{1,0:T(8,128)(2,1)S(1)}, bf16[32,1792]{1,0:T(8,128)(2,1)S(1)}, u32[]{:S(2)}, u32[]{:S(2)}) collective-permute-start(bf16[32,1792]{1,0:T(8,128)(2,1)S(1)} %collective-permute-done.3), channel_id=1, source_target_pairs={{0,1},{1,0},{2,3},{3,2},{4,5},{5,4},{6,7},{7,6},{8,9},{9,8},{10,11... | collective-permute-start | bytes 344072 | tf_op jit(solution)/shard_map/ppermute | solution.py:188
  20.6 0.0 collective-permute-done.10.sib_ref
  20.6 0.7 %near.1 = (f32[128,512]{1,0:T(8,128)S(1)}, f32[128,512]{1,0:T(8,128)S(1)}) custom-call(bf16[64,1792]{1,0:T(8,128)(2,1)S(1)} %pad_maximum_fusion.after_ref.own_ref, bf16[64,1792]{1,0:T(8,128)(2,1)S(1)} %collective-permute-done.10.sib_ref, bf16[2,1792,512]{2,1,0:T(8,128)(2,1)S(1)} %get-tuple-element.29.w_ref), custom_call_target="tpu_custom_call" | custom-call | flops 469762048 | bytes 3670016 | tf_op jit(solution)/shard_map/near/pallas_call | solution.py:229
  21.2 0.3 collective-permute-done.8
  21.6 0.7 %far.1.h_ref = bf16[128,512]{1,0:T(8,128)(2,1)S(1)} custom-call(bf16[64,1792]{1,0:T(8,128)(2,1)S(1)} %constant_dynamic-update-slice_fusion.2.far_ref, bf16[64,1792]{1,0:T(8,128)(2,1)S(1)} %pad_maximum_fusion.1.diag_ref, bf16[2,1792,512]{2,1,0:T(8,128)(2,1)S(1)} %get-tuple-element.26.w_ref, f32[128,512]{1,0:T(8,128)S(1)} %get-tuple-element.30.g_ref, ...), custom_call_target="tpu_custom_call" | custom-call | flops 469762048 | bytes 3670016 | tf_op jit(solution)/shard_map/far/pallas_call | solution.py:233
  22.2 1.6 %collective-permute-start.11 = (bf16[128,512]{1,0:T(8,128)(2,1)S(1)}, bf16[128,512]{1,0:T(8,128)(2,1)S(1)}, u32[]{:S(2)}, u32[]{:S(2)}) collective-permute-start(bf16[128,512]{1,0:T(8,128)(2,1)S(1)} %far.1.h_ref), channel_id=1, source_target_pairs={{0,2},{1,3},{2,0},{3,1},{4,6},{5,7},{6,4},{7,5},{8,10},{9,11},{10,... | collective-permute-start | bytes 393224 | tf_op jit(solution)/shard_map/ppermute | solution.py:185
  23.8 2.0 %all_gather.3.sib_ref = bf16[256,512]{1,0:T(8,128)(2,1)S(1)} all-gather(bf16[128,512]{1,0:T(8,128)(2,1)S(1)} %far.1.h_ref), channel_id=1, replica_groups={{0,1},{2,3},{4,5},{6,7},{8,9},{10,11},{12,13},{14,15},{16,17},{18,19},{..., dimensions={0}, use_global_device_ids=true | all-gather | bytes 393216 | tf_op jit(solution)/shard_map/all_gather | solution.py:242
  25.8 1.7 %hess_near.1 = (bf16[512,128]{1,0:T(8,128)(2,1)S(1)}, bf16[1,128,512]{2,1,0:T(8,128)(2,1)}, f32[1,512,2048]{2,1,0:T(8,128)}) custom-call(bf16[128,512]{1,0:T(8,128)(2,1)S(1)} %far.1.h_ref, bf16[256,512]{1,0:T(8,128)(2,1)S(1)} %all_gather.3.sib_ref), custom_call_target="tpu_custom_call" | custom-call | flops 134217728 | bytes 2097152 | tf_op jit(solution)/shard_map/hess_near/pallas_call | solution.py:243
  27.5 0.5 %collective-permute-done.11.h_ref = bf16[128,512]{1,0:T(8,128)(2,1)S(1)} collective-permute-done((bf16[128,512]{1,0:T(8,128)(2,1)S(1)}, bf16[128,512]{1,0:T(8,128)(2,1)S(1)}, u32[]{:S(2)}, u32[]{:S(2)}) %collective-permute-start.11) | collective-permute-done | bytes 131104 | tf_op jit(solution)/shard_map/ppermute | solution.py:185
  28.0 1.2 %hess_2.1.hess_in = f32[1,512,2048]{2,1,0:T(8,128)} custom-call(bf16[512,128]{1,0:T(8,128)(2,1)S(1)} %get-tuple-element.33.flip_ref, bf16[128,512]{1,0:T(8,128)(2,1)S(1)} %collective-permute-done.11.h_ref, f32[1,512,2048]{2,1,0:T(8,128)} %get-tuple-element.35.hess_in), custom_call_target="tpu_custom_call", output_to_operand_aliasing={{}: (2, {})} | custom-call | flops 67108864 | bytes 1048576 | tf_op jit(solution)/shard_map/hess_2/pallas_call | solution.py:251
  29.2 0.2 collective-permute-done.12.h_ref
  29.4 1.2 %hess_3.1 = f32[1,512,2048]{2,1,0:T(8,128)} custom-call(bf16[512,128]{1,0:T(8,128)(2,1)S(1)} %get-tuple-element.33.flip_ref, bf16[128,512]{1,0:T(8,128)(2,1)S(1)} %collective-permute-done.12.h_ref, f32[1,512,2048]{2,1,0:T(8,128)} %hess_2.1.hess_in), custom_call_target="tpu_custom_call", output_to_operand_aliasing={{}: (2, {})} | custom-call | flops 67108864 | bytes 1048576 | tf_op jit(solution)/shard_map/hess_3/pallas_call | solution.py:251
  (11 shorter events, 0.1 us)
Async XLA Ops:
  0.6 4.4 %collective-permute-start = (bf16[256,896]{1,0:T(8,128)(2,1)}, bf16[256,896]{1,0:T(8,128)(2,1)S(1)}, u32[]{:S(2)}, u32[]{:S(2)}) collective-permute-start(bf16[256,896]{1,0:T(8,128)(2,1)} %tok_hbm.1), channel_id=1, source_target_pairs={{0,1},{1,0},{2,3},{3,2},{4,5},{5,4},{6,7},{7,6},{8,9},{9,8},{10,11... | collective-permute-start | bytes 1376264 | tf_op jit(solution)/shard_map/ppermute | solution.py:188
  2.4 6.5 %collective-permute-start.6 = (bf16[16,896]{1,0:T(8,128)(2,1)S(1)}, bf16[16,896]{1,0:T(8,128)(2,1)S(1)}, u32[]{:S(2)}, u32[]{:S(2)}) collective-permute-start(bf16[16,896]{1,0:T(8,128)(2,1)S(1)} %get-tuple-element.25), channel_id=1, source_target_pairs={{0,4},{4,0},{8,12},{12,8},{16,20},{20,16},{24,28},{28,24},{1,5},{5... | collective-permute-start | bytes 86024 | tf_op jit(solution)/shard_map/ppermute | solution.py:207
  5.2 6.2 %collective-permute-start.1 = (bf16[16,1792]{1,0:T(8,128)(2,1)S(1)}, bf16[16,1792]{1,0:T(8,128)(2,1)S(1)}, u32[]{:S(2)}, u32[]{:S(2)}) collective-permute-start(bf16[16,1792]{1,0:T(8,128)(2,1)S(1)} %get-tuple-element.21), channel_id=1, source_target_pairs={{0,24},{1,29},{2,26},{3,31},{4,28},{5,25},{6,30},{7,27},{8,16},{9,... | collective-permute-start | bytes 172040 | tf_op jit(solution)/shard_map/ppermute | solution.py:192
  8.9 4.7 %collective-permute-start.2 = (bf16[16,1792]{1,0:T(8,128)(2,1)S(1)}, bf16[16,1792]{1,0:T(8,128)(2,1)S(1)}, u32[]{:S(2)}, u32[]{:S(2)}) collective-permute-start(bf16[16,1792]{1,0:T(8,128)(2,1)S(1)} %get-tuple-element.22), channel_id=1, source_target_pairs={{0,8},{1,13},{2,10},{3,15},{4,12},{5,9},{6,14},{7,11},{8,0},{9,5},... | collective-permute-start | bytes 172040 | tf_op jit(solution)/shard_map/ppermute | solution.py:192
  8.9 10.7 %collective-permute-start.7 = (bf16[16,1792]{1,0:T(8,128)(2,1)S(1)}, bf16[16,1792]{1,0:T(8,128)(2,1)S(1)}, u32[]{:S(2)}, u32[]{:S(2)}) collective-permute-start(bf16[16,1792]{1,0:T(8,128)(2,1)S(1)} %constant_dynamic-update-slice_fusion), channel_id=1, source_target_pairs={{0,2},{1,3},{2,0},{3,1},{4,6},{5,7},{6,4},{7,5},{8,10},{9,11},{10,... | collective-permute-start | bytes 172040 | tf_op jit(solution)/shard_map/ppermute | solution.py:185
  10.5 5.3 %collective-permute-start.4 = (bf16[16,1792]{1,0:T(8,128)(2,1)S(1)}, bf16[16,1792]{1,0:T(8,128)(2,1)S(1)}, u32[]{:S(2)}, u32[]{:S(2)}) collective-permute-start(bf16[16,1792]{1,0:T(8,128)(2,1)S(1)} %get-tuple-element.23), channel_id=1, source_target_pairs={{0,16},{1,21},{2,18},{3,23},{4,20},{5,17},{6,22},{7,19},{8,24},{9,... | collective-permute-start | bytes 172040 | tf_op jit(solution)/shard_map/ppermute | solution.py:192
  13.6 6.4 %collective-permute-start.3 = (bf16[32,1792]{1,0:T(8,128)(2,1)S(1)}, bf16[32,1792]{1,0:T(8,128)(2,1)S(1)}, u32[]{:S(2)}, u32[]{:S(2)}) collective-permute-start(bf16[32,1792]{1,0:T(8,128)(2,1)S(1)} %pad_maximum_fusion.2), channel_id=1, source_target_pairs={{0,2},{1,3},{2,0},{3,1},{4,6},{5,7},{6,4},{7,5},{8,10},{9,11},{10,... | collective-permute-start | bytes 344072 | tf_op jit(solution)/shard_map/ppermute | solution.py:185
  15.8 4.2 %collective-permute-start.5 = (bf16[16,1792]{1,0:T(8,128)(2,1)S(1)}, bf16[16,1792]{1,0:T(8,128)(2,1)S(1)}, u32[]{:S(2)}, u32[]{:S(2)}) collective-permute-start(bf16[16,1792]{1,0:T(8,128)(2,1)S(1)} %collective-permute-done.4), channel_id=1, source_target_pairs={{0,2},{1,3},{2,0},{3,1},{4,6},{5,7},{6,4},{7,5},{8,10},{9,11},{10,... | collective-permute-start | bytes 172040 | tf_op jit(solution)/shard_map/ppermute | solution.py:185
  16.3 4.3 %collective-permute-start.10 = (bf16[64,1792]{1,0:T(8,128)(2,1)S(1)}, bf16[64,1792]{1,0:T(8,128)(2,1)S(1)}, u32[]{:S(2)}, u32[]{:S(2)}) collective-permute-start(bf16[64,1792]{1,0:T(8,128)(2,1)S(1)} %pad_maximum_fusion.after_ref.own_ref), channel_id=1, source_target_pairs={{0,1},{1,0},{2,3},{3,2},{4,5},{5,4},{6,7},{7,6},{8,9},{9,8},{10,11... | collective-permute-start | bytes 688136 | tf_op jit(solution)/shard_map/ppermute | solution.py:188
  20.0 1.6 %collective-permute-start.9 = (bf16[32,1792]{1,0:T(8,128)(2,1)S(1)}, bf16[32,1792]{1,0:T(8,128)(2,1)S(1)}, u32[]{:S(2)}, u32[]{:S(2)}) collective-permute-start(bf16[32,1792]{1,0:T(8,128)(2,1)S(1)} %pad_maximum_fusion.3), channel_id=1, source_target_pairs={{0,1},{1,0},{2,3},{3,2},{4,5},{5,4},{6,7},{7,6},{8,9},{9,8},{10,11... | collective-permute-start | bytes 344072 | tf_op jit(solution)/shard_map/ppermute | solution.py:188
  20.2 1.3 %collective-permute-start.8 = (bf16[32,1792]{1,0:T(8,128)(2,1)S(1)}, bf16[32,1792]{1,0:T(8,128)(2,1)S(1)}, u32[]{:S(2)}, u32[]{:S(2)}) collective-permute-start(bf16[32,1792]{1,0:T(8,128)(2,1)S(1)} %collective-permute-done.3), channel_id=1, source_target_pairs={{0,1},{1,0},{2,3},{3,2},{4,5},{5,4},{6,7},{7,6},{8,9},{9,8},{10,11... | collective-permute-start | bytes 344072 | tf_op jit(solution)/shard_map/ppermute | solution.py:188
  22.2 5.8 %collective-permute-start.11 = (bf16[128,512]{1,0:T(8,128)(2,1)S(1)}, bf16[128,512]{1,0:T(8,128)(2,1)S(1)}, u32[]{:S(2)}, u32[]{:S(2)}) collective-permute-start(bf16[128,512]{1,0:T(8,128)(2,1)S(1)} %far.1.h_ref), channel_id=1, source_target_pairs={{0,2},{1,3},{2,0},{3,1},{4,6},{5,7},{6,4},{7,5},{8,10},{9,11},{10,... | collective-permute-start | bytes 393224 | tf_op jit(solution)/shard_map/ppermute | solution.py:185
  28.0 1.3 %collective-permute-start.12 = (bf16[128,512]{1,0:T(8,128)(2,1)S(1)}, bf16[128,512]{1,0:T(8,128)(2,1)S(1)}, u32[]{:S(2)}, u32[]{:S(2)}) collective-permute-start(bf16[128,512]{1,0:T(8,128)(2,1)S(1)} %collective-permute-done.11.h_ref), channel_id=1, source_target_pairs={{0,1},{1,0},{2,3},{3,2},{4,5},{5,4},{6,7},{7,6},{8,9},{9,8},{10,11... | collective-permute-start | bytes 393224 | tf_op jit(solution)/shard_map/ppermute | solution.py:188

commit v5 on v4

--- a/solution.py
+++ b/solution.py
@@ -17,8 +17,8 @@
 LIMIT = 40 * 1024 * 1024
 
 
-DISTANCE = ((6, 2, 4), (7, 3, 5))
-PARTS = ((1, 2), (3,), (0,))
+DISTANCE = ((4, 5, 2), (7, 6, 3))
+PARTS = ((1, 2), (0,), (3,))
 ORDER = sum(PARTS, ())
 
 
@@ -187,8 +187,8 @@
     def cores(x):
         return lax.ppermute(x, "tp", [(i, i ^ 1) for i in range(4)])
 
-    def spread(k, x):
-        pairs = [(e * 4 + t, (e ^ DISTANCE[t & 1][k]) * 4 + t) for e in range(8) for t in range(4)]
+    def spread(k, x, other_chip=0):
+        pairs = [(e * 4 + t, (e ^ DISTANCE[t & 1][k]) * 4 + (t ^ other_chip)) for e in range(8) for t in range(4)]
         return lax.ppermute(x, ("ep", "tp"), pairs)
 
     sib_tokens = cores(tokens)
@@ -215,14 +215,14 @@
     part = S((slots, wide), F32)
     work = 4 * slots * depth * 2 * wide
     parts = [jnp.concatenate([got[k] for k in part]) for part in PARTS]
-    far = jnp.concatenate([chips(part) for part in parts])
+    far = jnp.concatenate([chips(part) for part in parts[:-1]] + [spread(k - 1, out[k - 1], 2) for k in PARTS[-1]])
     own = jnp.concatenate(parts)
     sib = cores(own)
     near_w, far_w = call(
         load_kernel, (half_w, half_w), [VMEM] + [HBM] * 2, (VMEM,) * 2, (D((2,)), D((2,))), name="load", moved=weights,
     )(own, gate_w, up_w)
     early = 2 * capacity
-    late = tie(far[early:], (far_w, far[:early]))
+    late = tie(far[early:], far_w)
     diag = jnp.concatenate([cores(far[:early]), cores(late)])
     far = jnp.concatenate([far[:early], late])
     x = V((slots, 2 * depth), BF16)

time: 30.8 us -> 29.9 us (0.971)
  waiting for transfers between devices: 4.05 us -> 3.54 us
    ppermute x4 -> x3, starting transfers between devices: 5.2 us -> 4.43 us  [chips(): return lax.ppermute(x, 'tp', [(i, i ^ 2) for i in range(4)])]
    ppermute x3 -> x4, waiting for transfers between devices: 2.73 us -> 2.01 us  [spread(): return lax.ppermute(x, ('ep', 'tp'), pairs)]
    ppermute x3 -> x4, starting transfers between devices: 4.66 us -> 5.08 us  [spread(): return lax.ppermute(x, ('ep', 'tp'), pairs)]
    ppermute x5, waiting for transfers between devices: 0.46 us -> 0.79 us  [cores(): return lax.ppermute(x, 'tp', [(i, i ^ 1) for i in range(4)])]
    ppermute x4 -> x3, waiting for transfers between devices: 0.86 us -> 0.73 us  [chips(): return lax.ppermute(x, 'tp', [(i, i ^ 2) for i in range(4)])]
  transfers between devices with their start and end apart: 13 -> 13, of which waited for: 6 -> 6; matrix products, arithmetic and copies ran while one was open for 0% -> 0% of each run, Pallas kernels for 27% -> 28%
where the time goes in v5:
time: 29.9 us; the launch traced here: 29.7 us
  starting transfers between devices  13.3 us (44%)
  Pallas kernels  10.1 us (34%)
  waiting for transfers between devices  3.54 us (12%)
  blocking collectives  1.98 us (7%)
  between operations  0.75 us (3%)
    ppermute x4, starting transfers between devices, spread(): return lax.ppermute(x, ('ep', 'tp'), pairs)  5.08 us
    ppermute x3, starting transfers between devices, chips(): return lax.ppermute(x, 'tp', [(i, i ^ 2) for i in range(4)])  4.43 us
    pallas_call x1, Pallas kernels, paired(): call(load_kernel, (half_w, half_w), [VMEM] + [HBM] * 2, (VMEM,) * 2, (D((...  3.2 us
    ppermute x1, starting transfers between devices, paired(): side = lax.ppermute(side, 'ep', [(e, e ^ 1) for e in range(8)])  2.59 us
    pallas_call x2, Pallas kernels, other(): call(functools.partial(hess_far_kernel, factor, which), hess_shape, [VMEM...  2.35 us
    ppermute x4, waiting for transfers between devices, spread(): return lax.ppermute(x, ('ep', 'tp'), pairs)  2.01 us
    all_gather x1, blocking collectives, paired(): lax.all_gather(hidden, 'tp', axis=0, tiled=True, axis_index_groups=[[0, 1...  1.98 us
    pallas_call x1, Pallas kernels, paired(): call(functools.partial(hess_near_kernel, factor, capacity), (S((wide, slo...  1.74 us
  transfers between devices with their start and end apart: 13, of which 6 were waited for; matrix products, arithmetic and copies ran while one was open for 0% of the time, Pallas kernels for 28%

profile of v5, /device:TPU:0, one launch (start us, length us, event | category | flops | bytes accessed | tf_op | source)
XLA Modules:
  0.0 29.7 jit_solution(8517188679750524863)
XLA Ops:
  0.6 0.5 %collective-permute-start = (bf16[256,896]{1,0:T(8,128)(2,1)}, bf16[256,896]{1,0:T(8,128)(2,1)S(1)}, u32[]{:S(2)}, u32[]{:S(2)}) collective-permute-start(bf16[256,896]{1,0:T(8,128)(2,1)} %tok_hbm.1), channel_id=1, source_target_pairs={{0,1},{1,0},{2,3},{3,2},{4,5},{5,4},{6,7},{7,6},{8,9},{9,8},{10,11... | collective-permute-start | bytes 1376264 | tf_op jit(solution)/shard_map/ppermute | solution.py:188
  1.1 1.3 %prepare.1 = (bf16[48,256]{1,0:T(8,128)(2,1)S(1)}, bf16[48,896]{1,0:T(8,128)(2,1)S(1)}, bf16[16,896]{1,0:T(8,128)(2,1)S(1)}, bf16[16,896]{1,0:T(8,128)(2,1)S(1)}) custom-call(s32[8,256]{1,0:T(8,128)} %bitcast.1, bf16[256,896]{1,0:T(8,128)(2,1)} %tok_hbm.1), custom_call_target="tpu_custom_call" | custom-call | flops 36700160 | bytes 458752 | tf_op jit(solution)/shard_map/prepare/pallas_call | solution.py:200
  2.4 2.6 %collective-permute-start.4 = (bf16[16,896]{1,0:T(8,128)(2,1)S(1)}, bf16[16,896]{1,0:T(8,128)(2,1)S(1)}, u32[]{:S(2)}, u32[]{:S(2)}) collective-permute-start(bf16[16,896]{1,0:T(8,128)(2,1)S(1)} %get-tuple-element.24), channel_id=1, source_target_pairs={{0,4},{4,0},{8,12},{12,8},{16,20},{20,16},{24,28},{28,24},{1,5},{5... | collective-permute-start | bytes 86024 | tf_op jit(solution)/shard_map/ppermute | solution.py:207
  5.0 0.0 collective-permute-done.sib_ref
  5.0 0.2 select.1
  5.2 2.7 %collective-permute-start.1 = (bf16[16,1792]{1,0:T(8,128)(2,1)S(1)}, bf16[16,1792]{1,0:T(8,128)(2,1)S(1)}, u32[]{:S(2)}, u32[]{:S(2)}) collective-permute-start(bf16[16,1792]{1,0:T(8,128)(2,1)S(1)} %get-tuple-element.21), channel_id=1, source_target_pairs={{0,16},{1,29},{2,18},{3,31},{4,20},{5,25},{6,22},{7,27},{8,24},{9,... | collective-permute-start | bytes 172040 | tf_op jit(solution)/shard_map/ppermute | solution.py:192
  7.9 0.4 %collective-permute-start.2 = (bf16[16,1792]{1,0:T(8,128)(2,1)S(1)}, bf16[16,1792]{1,0:T(8,128)(2,1)S(1)}, u32[]{:S(2)}, u32[]{:S(2)}) collective-permute-start(bf16[16,1792]{1,0:T(8,128)(2,1)S(1)} %get-tuple-element.22), channel_id=1, source_target_pairs={{0,20},{1,25},{2,22},{3,27},{4,16},{5,29},{6,18},{7,31},{8,28},{9,... | collective-permute-start | bytes 172040 | tf_op jit(solution)/shard_map/ppermute | solution.py:192
  8.3 0.0 collective-permute-done.4
  8.3 1.5 %collective-permute-start.5 = (bf16[16,1792]{1,0:T(8,128)(2,1)S(1)}, bf16[16,1792]{1,0:T(8,128)(2,1)S(1)}, u32[]{:S(2)}, u32[]{:S(2)}) collective-permute-start(bf16[16,1792]{1,0:T(8,128)(2,1)S(1)} %constant_dynamic-update-slice_fusion), channel_id=1, source_target_pairs={{0,2},{1,3},{2,0},{3,1},{4,6},{5,7},{6,4},{7,5},{8,10},{9,11},{10,... | collective-permute-start | bytes 172040 | tf_op jit(solution)/shard_map/ppermute | solution.py:185
  9.9 1.6 %collective-permute-start.7 = (bf16[16,1792]{1,0:T(8,128)(2,1)S(1)}, bf16[16,1792]{1,0:T(8,128)(2,1)S(1)}, u32[]{:S(2)}, u32[]{:S(2)}) collective-permute-start(bf16[16,1792]{1,0:T(8,128)(2,1)S(1)} %get-tuple-element.25), channel_id=1, source_target_pairs={{0,8},{1,13},{2,10},{3,15},{4,12},{5,9},{6,14},{7,11},{8,0},{9,5},... | collective-permute-start | bytes 172040 | tf_op jit(solution)/shard_map/ppermute | solution.py:192
  11.5 0.4 %collective-permute-start.6 = (bf16[16,1792]{1,0:T(8,128)(2,1)S(1)}, bf16[16,1792]{1,0:T(8,128)(2,1)S(1)}, u32[]{:S(2)}, u32[]{:S(2)}) collective-permute-start(bf16[16,1792]{1,0:T(8,128)(2,1)S(1)} %get-tuple-element.25), channel_id=1, source_target_pairs={{0,10},{1,15},{2,8},{3,13},{4,14},{5,11},{6,12},{7,9},{8,2},{9,7},... | collective-permute-start | bytes 172040 | tf_op jit(solution)/shard_map/ppermute | solution.py:192
  11.9 0.0 collective-permute-done.1
  11.9 2.0 %collective-permute-done.2 = bf16[16,1792]{1,0:T(8,128)(2,1)S(1)} collective-permute-done((bf16[16,1792]{1,0:T(8,128)(2,1)S(1)}, bf16[16,1792]{1,0:T(8,128)(2,1)S(1)}, u32[]{:S(2)}, u32[]{:S(2)}) %collective-permute-start.2) | collective-permute-done | bytes 57376 | tf_op jit(solution)/shard_map/ppermute | solution.py:192
  13.9 1.6 %collective-permute-start.3 = (bf16[32,1792]{1,0:T(8,128)(2,1)S(1)}, bf16[32,1792]{1,0:T(8,128)(2,1)S(1)}, u32[]{:S(2)}, u32[]{:S(2)}) collective-permute-start(bf16[32,1792]{1,0:T(8,128)(2,1)S(1)} %pad_maximum_fusion.2), channel_id=1, source_target_pairs={{0,2},{1,3},{2,0},{3,1},{4,6},{5,7},{6,4},{7,5},{8,10},{9,11},{10,... | collective-permute-start | bytes 344072 | tf_op jit(solution)/shard_map/ppermute | solution.py:185
  15.5 0.0 collective-permute-done.7
  15.6 0.1 collective-permute-start.10
  15.6 3.2 %load.1 = (bf16[2,1792,512]{2,1,0:T(8,128)(2,1)S(1)}, bf16[2,1792,512]{2,1,0:T(8,128)(2,1)S(1)}) custom-call(bf16[64,1792]{1,0:T(8,128)(2,1)S(1)} %pad_maximum_fusion.after_ref.own_ref, bf16[1,3584,512]{2,1,0:T(8,128)(2,1)} %gate_hbm.1, bf16[1,3584,512]{2,1,0:T(8,128)(2,1)} %up_hbm.1), custom_call_target="tpu_custom_call" | custom-call | bytes 7340032 | tf_op jit(solution)/shard_map/load/pallas_call | solution.py:221
  18.8 0.0 collective-permute-done.5
  18.9 0.6 %collective-permute-start.9 = (bf16[32,1792]{1,0:T(8,128)(2,1)S(1)}, bf16[32,1792]{1,0:T(8,128)(2,1)S(1)}, u32[]{:S(2)}, u32[]{:S(2)}) collective-permute-start(bf16[32,1792]{1,0:T(8,128)(2,1)S(1)} %pad_maximum_fusion.3), channel_id=1, source_target_pairs={{0,1},{1,0},{2,3},{3,2},{4,5},{5,4},{6,7},{7,6},{8,9},{9,8},{10,11... | collective-permute-start | bytes 344072 | tf_op jit(solution)/shard_map/ppermute | solution.py:188
  19.4 0.1 collective-permute-done.3
  19.5 0.0 collective-permute-start.8
  19.6 0.7 %near.1 = (f32[128,512]{1,0:T(8,128)S(1)}, f32[128,512]{1,0:T(8,128)S(1)}) custom-call(bf16[64,1792]{1,0:T(8,128)(2,1)S(1)} %pad_maximum_fusion.after_ref.own_ref, bf16[64,1792]{1,0:T(8,128)(2,1)S(1)} %collective-permute-done.10.sib_ref, bf16[2,1792,512]{2,1,0:T(8,128)(2,1)S(1)} %get-tuple-element.29.w_ref), custom_call_target="tpu_custom_call" | custom-call | flops 469762048 | bytes 3670016 | tf_op jit(solution)/shard_map/near/pallas_call | solution.py:229
  20.2 0.2 collective-permute-done.9
  20.4 0.4 %collective-permute-done.8 = bf16[32,1792]{1,0:T(8,128)(2,1)S(1)} collective-permute-done((bf16[32,1792]{1,0:T(8,128)(2,1)S(1)}, bf16[32,1792]{1,0:T(8,128)(2,1)S(1)}, u32[]{:S(2)}, u32[]{:S(2)}) %collective-permute-start.8) | collective-permute-done | bytes 114720 | tf_op jit(solution)/shard_map/ppermute | solution.py:188
  20.9 0.7 %far.1.h_ref = bf16[128,512]{1,0:T(8,128)(2,1)S(1)} custom-call(bf16[64,1792]{1,0:T(8,128)(2,1)S(1)} %constant_dynamic-update-slice_fusion.2.far_ref, bf16[64,1792]{1,0:T(8,128)(2,1)S(1)} %pad_maximum_fusion.1.diag_ref, bf16[2,1792,512]{2,1,0:T(8,128)(2,1)S(1)} %get-tuple-element.26.w_ref, f32[128,512]{1,0:T(8,128)S(1)} %get-tuple-element.30.g_ref, ...), custom_call_target="tpu_custom_call" | custom-call | flops 469762048 | bytes 3670016 | tf_op jit(solution)/shard_map/far/pallas_call | solution.py:233
  21.5 1.2 %collective-permute-start.11 = (bf16[128,512]{1,0:T(8,128)(2,1)S(1)}, bf16[128,512]{1,0:T(8,128)(2,1)S(1)}, u32[]{:S(2)}, u32[]{:S(2)}) collective-permute-start(bf16[128,512]{1,0:T(8,128)(2,1)S(1)} %far.1.h_ref), channel_id=1, source_target_pairs={{0,2},{1,3},{2,0},{3,1},{4,6},{5,7},{6,4},{7,5},{8,10},{9,11},{10,... | collective-permute-start | bytes 393224 | tf_op jit(solution)/shard_map/ppermute | solution.py:185
  22.8 2.0 %all_gather.3.sib_ref = bf16[256,512]{1,0:T(8,128)(2,1)S(1)} all-gather(bf16[128,512]{1,0:T(8,128)(2,1)S(1)} %far.1.h_ref), channel_id=1, replica_groups={{0,1},{2,3},{4,5},{6,7},{8,9},{10,11},{12,13},{14,15},{16,17},{18,19},{..., dimensions={0}, use_global_device_ids=true | all-gather | bytes 393216 | tf_op jit(solution)/shard_map/all_gather | solution.py:242
  24.8 1.7 %hess_near.1 = (bf16[512,128]{1,0:T(8,128)(2,1)S(1)}, bf16[1,128,512]{2,1,0:T(8,128)(2,1)}, f32[1,512,2048]{2,1,0:T(8,128)}) custom-call(bf16[128,512]{1,0:T(8,128)(2,1)S(1)} %far.1.h_ref, bf16[256,512]{1,0:T(8,128)(2,1)S(1)} %all_gather.3.sib_ref), custom_call_target="tpu_custom_call" | custom-call | flops 134217728 | bytes 2097152 | tf_op jit(solution)/shard_map/hess_near/pallas_call | solution.py:243
  26.5 0.6 %collective-permute-done.11.h_ref = bf16[128,512]{1,0:T(8,128)(2,1)S(1)} collective-permute-done((bf16[128,512]{1,0:T(8,128)(2,1)S(1)}, bf16[128,512]{1,0:T(8,128)(2,1)S(1)}, u32[]{:S(2)}, u32[]{:S(2)}) %collective-permute-start.11) | collective-permute-done | bytes 131104 | tf_op jit(solution)/shard_map/ppermute | solution.py:185
  27.2 1.2 %hess_2.1.hess_in = f32[1,512,2048]{2,1,0:T(8,128)} custom-call(bf16[512,128]{1,0:T(8,128)(2,1)S(1)} %get-tuple-element.33.flip_ref, bf16[128,512]{1,0:T(8,128)(2,1)S(1)} %collective-permute-done.11.h_ref, f32[1,512,2048]{2,1,0:T(8,128)} %get-tuple-element.35.hess_in), custom_call_target="tpu_custom_call", output_to_operand_aliasing={{}: (2, {})} | custom-call | flops 67108864 | bytes 1048576 | tf_op jit(solution)/shard_map/hess_2/pallas_call | solution.py:251
  28.3 0.2 collective-permute-done.12.h_ref
  28.5 1.2 %hess_3.1 = f32[1,512,2048]{2,1,0:T(8,128)} custom-call(bf16[512,128]{1,0:T(8,128)(2,1)S(1)} %get-tuple-element.33.flip_ref, bf16[128,512]{1,0:T(8,128)(2,1)S(1)} %collective-permute-done.12.h_ref, f32[1,512,2048]{2,1,0:T(8,128)} %hess_2.1.hess_in), custom_call_target="tpu_custom_call", output_to_operand_aliasing={{}: (2, {})} | custom-call | flops 67108864 | bytes 1048576 | tf_op jit(solution)/shard_map/hess_3/pallas_call | solution.py:251
  (11 shorter events, 0.1 us)
Async XLA Ops:
  0.6 4.4 %collective-permute-start = (bf16[256,896]{1,0:T(8,128)(2,1)}, bf16[256,896]{1,0:T(8,128)(2,1)S(1)}, u32[]{:S(2)}, u32[]{:S(2)}) collective-permute-start(bf16[256,896]{1,0:T(8,128)(2,1)} %tok_hbm.1), channel_id=1, source_target_pairs={{0,1},{1,0},{2,3},{3,2},{4,5},{5,4},{6,7},{7,6},{8,9},{9,8},{10,11... | collective-permute-start | bytes 1376264 | tf_op jit(solution)/shard_map/ppermute | solution.py:188
  2.4 5.9 %collective-permute-start.4 = (bf16[16,896]{1,0:T(8,128)(2,1)S(1)}, bf16[16,896]{1,0:T(8,128)(2,1)S(1)}, u32[]{:S(2)}, u32[]{:S(2)}) collective-permute-start(bf16[16,896]{1,0:T(8,128)(2,1)S(1)} %get-tuple-element.24), channel_id=1, source_target_pairs={{0,4},{4,0},{8,12},{12,8},{16,20},{20,16},{24,28},{28,24},{1,5},{5... | collective-permute-start | bytes 86024 | tf_op jit(solution)/shard_map/ppermute | solution.py:207
  5.2 6.7 %collective-permute-start.1 = (bf16[16,1792]{1,0:T(8,128)(2,1)S(1)}, bf16[16,1792]{1,0:T(8,128)(2,1)S(1)}, u32[]{:S(2)}, u32[]{:S(2)}) collective-permute-start(bf16[16,1792]{1,0:T(8,128)(2,1)S(1)} %get-tuple-element.21), channel_id=1, source_target_pairs={{0,16},{1,29},{2,18},{3,31},{4,20},{5,25},{6,22},{7,27},{8,24},{9,... | collective-permute-start | bytes 172040 | tf_op jit(solution)/shard_map/ppermute | solution.py:192
  7.9 6.0 %collective-permute-start.2 = (bf16[16,1792]{1,0:T(8,128)(2,1)S(1)}, bf16[16,1792]{1,0:T(8,128)(2,1)S(1)}, u32[]{:S(2)}, u32[]{:S(2)}) collective-permute-start(bf16[16,1792]{1,0:T(8,128)(2,1)S(1)} %get-tuple-element.22), channel_id=1, source_target_pairs={{0,20},{1,25},{2,22},{3,27},{4,16},{5,29},{6,18},{7,31},{8,28},{9,... | collective-permute-start | bytes 172040 | tf_op jit(solution)/shard_map/ppermute | solution.py:192
  8.3 10.5 %collective-permute-start.5 = (bf16[16,1792]{1,0:T(8,128)(2,1)S(1)}, bf16[16,1792]{1,0:T(8,128)(2,1)S(1)}, u32[]{:S(2)}, u32[]{:S(2)}) collective-permute-start(bf16[16,1792]{1,0:T(8,128)(2,1)S(1)} %constant_dynamic-update-slice_fusion), channel_id=1, source_target_pairs={{0,2},{1,3},{2,0},{3,1},{4,6},{5,7},{6,4},{7,5},{8,10},{9,11},{10,... | collective-permute-start | bytes 172040 | tf_op jit(solution)/shard_map/ppermute | solution.py:185
  9.9 5.7 %collective-permute-start.7 = (bf16[16,1792]{1,0:T(8,128)(2,1)S(1)}, bf16[16,1792]{1,0:T(8,128)(2,1)S(1)}, u32[]{:S(2)}, u32[]{:S(2)}) collective-permute-start(bf16[16,1792]{1,0:T(8,128)(2,1)S(1)} %get-tuple-element.25), channel_id=1, source_target_pairs={{0,8},{1,13},{2,10},{3,15},{4,12},{5,9},{6,14},{7,11},{8,0},{9,5},... | collective-permute-start | bytes 172040 | tf_op jit(solution)/shard_map/ppermute | solution.py:192
  11.5 7.4 %collective-permute-start.6 = (bf16[16,1792]{1,0:T(8,128)(2,1)S(1)}, bf16[16,1792]{1,0:T(8,128)(2,1)S(1)}, u32[]{:S(2)}, u32[]{:S(2)}) collective-permute-start(bf16[16,1792]{1,0:T(8,128)(2,1)S(1)} %get-tuple-element.25), channel_id=1, source_target_pairs={{0,10},{1,15},{2,8},{3,13},{4,14},{5,11},{6,12},{7,9},{8,2},{9,7},... | collective-permute-start | bytes 172040 | tf_op jit(solution)/shard_map/ppermute | solution.py:192
  13.9 5.6 %collective-permute-start.3 = (bf16[32,1792]{1,0:T(8,128)(2,1)S(1)}, bf16[32,1792]{1,0:T(8,128)(2,1)S(1)}, u32[]{:S(2)}, u32[]{:S(2)}) collective-permute-start(bf16[32,1792]{1,0:T(8,128)(2,1)S(1)} %pad_maximum_fusion.2), channel_id=1, source_target_pairs={{0,2},{1,3},{2,0},{3,1},{4,6},{5,7},{6,4},{7,5},{8,10},{9,11},{10,... | collective-permute-start | bytes 344072 | tf_op jit(solution)/shard_map/ppermute | solution.py:185
  15.6 4.0 %collective-permute-start.10 = (bf16[64,1792]{1,0:T(8,128)(2,1)S(1)}, bf16[64,1792]{1,0:T(8,128)(2,1)S(1)}, u32[]{:S(2)}, u32[]{:S(2)}) collective-permute-start(bf16[64,1792]{1,0:T(8,128)(2,1)S(1)} %pad_maximum_fusion.after_ref.own_ref), channel_id=1, source_target_pairs={{0,1},{1,0},{2,3},{3,2},{4,5},{5,4},{6,7},{7,6},{8,9},{9,8},{10,11... | collective-permute-start | bytes 688136 | tf_op jit(solution)/shard_map/ppermute | solution.py:188
  18.9 1.5 %collective-permute-start.9 = (bf16[32,1792]{1,0:T(8,128)(2,1)S(1)}, bf16[32,1792]{1,0:T(8,128)(2,1)S(1)}, u32[]{:S(2)}, u32[]{:S(2)}) collective-permute-start(bf16[32,1792]{1,0:T(8,128)(2,1)S(1)} %pad_maximum_fusion.3), channel_id=1, source_target_pairs={{0,1},{1,0},{2,3},{3,2},{4,5},{5,4},{6,7},{7,6},{8,9},{9,8},{10,11... | collective-permute-start | bytes 344072 | tf_op jit(solution)/shard_map/ppermute | solution.py:188
  19.5 1.3 %collective-permute-start.8 = (bf16[32,1792]{1,0:T(8,128)(2,1)S(1)}, bf16[32,1792]{1,0:T(8,128)(2,1)S(1)}, u32[]{:S(2)}, u32[]{:S(2)}) collective-permute-start(bf16[32,1792]{1,0:T(8,128)(2,1)S(1)} %collective-permute-done.3), channel_id=1, source_target_pairs={{0,1},{1,0},{2,3},{3,2},{4,5},{5,4},{6,7},{7,6},{8,9},{9,8},{10,11... | collective-permute-start | bytes 344072 | tf_op jit(solution)/shard_map/ppermute | solution.py:188
  21.5 5.6 %collective-permute-start.11 = (bf16[128,512]{1,0:T(8,128)(2,1)S(1)}, bf16[128,512]{1,0:T(8,128)(2,1)S(1)}, u32[]{:S(2)}, u32[]{:S(2)}) collective-permute-start(bf16[128,512]{1,0:T(8,128)(2,1)S(1)} %far.1.h_ref), channel_id=1, source_target_pairs={{0,2},{1,3},{2,0},{3,1},{4,6},{5,7},{6,4},{7,5},{8,10},{9,11},{10,... | collective-permute-start | bytes 393224 | tf_op jit(solution)/shard_map/ppermute | solution.py:185
  27.1 1.3 %collective-permute-start.12 = (bf16[128,512]{1,0:T(8,128)(2,1)S(1)}, bf16[128,512]{1,0:T(8,128)(2,1)S(1)}, u32[]{:S(2)}, u32[]{:S(2)}) collective-permute-start(bf16[128,512]{1,0:T(8,128)(2,1)S(1)} %collective-permute-done.11.h_ref), channel_id=1, source_target_pairs={{0,1},{1,0},{2,3},{3,2},{4,5},{5,4},{6,7},{7,6},{8,9},{9,8},{10,11... | collective-permute-start | bytes 393224 | tf_op jit(solution)/shard_map/ppermute | solution.py:188

commit v6 on v5

--- a/solution.py
+++ b/solution.py
@@ -18,6 +18,7 @@
 
 
 DISTANCE = ((4, 5, 2), (7, 6, 3))
+EARLY_ROWS = 512
 PARTS = ((1, 2), (0,), (3,))
 ORDER = sum(PARTS, ())
 
@@ -30,17 +31,21 @@
     return lax.dot_general(a, b, (((1,), (0,)), ((), ())), preferred_element_type=F32)
 
 
-def weight_copies(gate_hbm, up_hbm, w_ref, sems, chip):
-    depth = w_ref.shape[1]
-    at = pl.ds(pl.multiple_of(((lax.axis_index("tp") >> 1) ^ chip) * depth, depth), depth)
-    return [pltpu.make_async_copy(w.at[0, at, :], w_ref.at[i], sems.at[i]) for i, w in enumerate((gate_hbm, up_hbm))]
-
-
-def prepare_kernel(capacity, ids_hbm, tok_hbm, pick_ref, mine_ref, stay_ref, side_ref, ids_ref, tok_ref, sems):
+def weight_copies(gate_hbm, up_hbm, w_ref, sems, chip, first=0):
+    rows = w_ref.shape[1]
+    depth = gate_hbm.shape[1] // 2
+    at = pl.ds(pl.multiple_of(((lax.axis_index("tp") >> 1) ^ chip) * depth + first, 16), rows)
+    return [
+        pltpu.make_async_copy(w.at[0, at, :], w_ref.at[i], sems.at[i])
+        for i, w in enumerate((gate_hbm, up_hbm))
+    ]
+
+
+def prepare_kernel(capacity, ids_hbm, tok_hbm, gate_hbm, up_hbm, pick_ref, mine_ref, stay_ref, side_ref, w_ref, ids_ref, tok_ref, sems, w_sems):
     get = [
         pltpu.make_async_copy(ids_hbm, ids_ref, sems.at[0]),
         pltpu.make_async_copy(tok_hbm, tok_ref, sems.at[1]),
-    ]
+    ] + weight_copies(gate_hbm, up_hbm, w_ref, w_sems, 0)
     for g in get:
         g.start()
     rows = ids_ref.shape[1]
@@ -67,6 +72,8 @@
     stay_ref[...] = taken[:capacity]
     side_ref[...] = taken[capacity : 2 * capacity]
     mine_ref[...] = taken[2 * capacity :]
+    get[2].wait()
+    get[3].wait()
 
 
 def select_kernel(capacity, pick_ref, mine_ref, sib_ref, *outs):
@@ -82,7 +89,7 @@
 
 
 def load_kernel(after_ref, gate_hbm, up_hbm, near_ref, far_ref, near_sems, far_sems):
-    get = weight_copies(gate_hbm, up_hbm, near_ref, near_sems, 0) + weight_copies(gate_hbm, up_hbm, far_ref, far_sems, 1)
+    get = weight_copies(gate_hbm, up_hbm, near_ref, near_sems, 0, EARLY_ROWS) + weight_copies(gate_hbm, up_hbm, far_ref, far_sems, 1)
     for g in get:
         g.start()
     for g in get:
@@ -103,10 +110,11 @@
                 x_ref[pl.ds(pl.multiple_of(distance(c, k - 1) * capacity, capacity), capacity), :] = block
 
 
-def near_kernel(capacity, own_ref, sib_ref, w_ref, g_ref, u_ref, x_ref):
+def near_kernel(capacity, own_ref, sib_ref, early_ref, w_ref, g_ref, u_ref, x_ref):
     assemble(capacity, own_ref, sib_ref, x_ref)
-    g_ref[...] = dot(x_ref[...], w_ref[0])
-    u_ref[...] = dot(x_ref[...], w_ref[1])
+    cut = early_ref.shape[1]
+    for i, out in enumerate((g_ref, u_ref)):
+        out[...] = dot(x_ref[:, :cut], early_ref[i]) + dot(x_ref[:, cut:], w_ref[i])
 
 
 def far_kernel(capacity, far_ref, diag_ref, w_ref, g_ref, u_ref, h_ref, x_ref):
@@ -197,13 +205,16 @@
         pltpu.with_memory_space_constraint(a, pltpu.HBM) for a in (expert_ids.T, tokens, gate_weight, up_weight)
     )
     single = S((capacity, depth), BF16)
-    pick, mine, stay, side = call(
+    half_w = V((2, 2 * depth, wide), BF16)
+    early_w = V((2, EARLY_ROWS, wide), BF16)
+    rest_w = V((2, 2 * depth - EARLY_ROWS, wide), BF16)
+    pick, mine, stay, side, early_w = call(
         functools.partial(prepare_kernel, capacity),
-        (S((3 * capacity, tok_rows), BF16), S((3 * capacity, depth), BF16), single, single),
-        [HBM] * 2, (VMEM,) * 4,
-        (V(ids.shape, jnp.int32), V(tokens.shape, BF16), D((2,))), name="prepare",
+        (S((3 * capacity, tok_rows), BF16), S((3 * capacity, depth), BF16), single, single, early_w),
+        [HBM] * 4, (VMEM,) * 5,
+        (V(ids.shape, jnp.int32), V(tokens.shape, BF16), D((2,)), D((2,))), name="prepare",
         flops=10 * capacity * tok_rows * depth, moved=tokens.size * 2,
-    )(ids, toks)
+    )(ids, toks, gate_w, up_w)
     side = lax.ppermute(side, "ep", [(e, e ^ 1) for e in range(8)])
     out = call(
         functools.partial(select_kernel, capacity),
@@ -211,7 +222,6 @@
         flops=6 * capacity * tok_rows * depth,
     )(pick, mine, sib_tokens)
     got = [jnp.concatenate([stay, side], axis=1)] + [spread(k, out[k]) for k in range(3)]
-    half_w = V((2, 2 * depth, wide), BF16)
     part = S((slots, wide), F32)
     work = 4 * slots * depth * 2 * wide
     parts = [jnp.concatenate([got[k] for k in part]) for part in PARTS]
@@ -219,17 +229,17 @@
     own = jnp.concatenate(parts)
     sib = cores(own)
     near_w, far_w = call(
-        load_kernel, (half_w, half_w), [VMEM] + [HBM] * 2, (VMEM,) * 2, (D((2,)), D((2,))), name="load", moved=weights,
-    )(own, gate_w, up_w)
+        load_kernel, (rest_w, half_w), [VMEM] + [HBM] * 2, (VMEM,) * 2, (D((2,)), D((2,))), name="load", moved=weights,
+    )(jnp.concatenate(parts[:2]), gate_w, up_w)
     early = 2 * capacity
     late = tie(far[early:], far_w)
     diag = jnp.concatenate([cores(far[:early]), cores(late)])
     far = jnp.concatenate([far[:early], late])
     x = V((slots, 2 * depth), BF16)
     gate, up = call(
-        functools.partial(near_kernel, capacity), (part, part), [VMEM] * 3, (VMEM,) * 2, (x,), name="near",
+        functools.partial(near_kernel, capacity), (part, part), [VMEM] * 4, (VMEM,) * 2, (x,), name="near",
         flops=work, moved=weights // 2,
-    )(own, tie(sib, far), near_w)
+    )(own, tie(sib, far), early_w, near_w)
     hidden = call(
         functools.partial(far_kernel, capacity), S((slots, wide), BF16), [VMEM] * 5, VMEM, (x,), name="far",
         flops=work, moved=weights // 2,

time: 29.9 us -> 29.9 us (level)
    pallas_call x2, Pallas kernels: 3.85 us -> 3.55 us  [the longest x1 2.9 us: paired(): call(load_kernel, (rest_w, half_w), [VMEM] + [HBM] * 2, (VMEM,) * 2, (D((...]
  transfers between devices with their start and end apart: 13 -> 13, of which waited for: 6 -> 6; matrix products, arithmetic and copies ran while one was open for 0% -> 0% of each run, Pallas kernels for 28% -> 27%
where the time goes in v6:
time: 29.9 us; the launch traced here: 29.7 us
  starting transfers between devices  13.2 us (44%)
  Pallas kernels  9.88 us (33%)
  waiting for transfers between devices  3.73 us (12%)
  blocking collectives  1.98 us (7%)
  between operations  0.76 us (3%)
    ppermute x4, starting transfers between devices, spread(): return lax.ppermute(x, ('ep', 'tp'), pairs)  4.97 us
    ppermute x3, starting transfers between devices, chips(): return lax.ppermute(x, 'tp', [(i, i ^ 2) for i in range(4)])  4.51 us
    pallas_call x1, Pallas kernels, paired(): call(load_kernel, (rest_w, half_w), [VMEM] + [HBM] * 2, (VMEM,) * 2, (D((...  2.9 us
    ppermute x1, starting transfers between devices, paired(): side = lax.ppermute(side, 'ep', [(e, e ^ 1) for e in range(8)])  2.59 us
    pallas_call x2, Pallas kernels, other(): call(functools.partial(hess_far_kernel, factor, which), hess_shape, [VMEM...  2.35 us
    ppermute x4, waiting for transfers between devices, spread(): return lax.ppermute(x, ('ep', 'tp'), pairs)  2.12 us
    all_gather x1, blocking collectives, paired(): lax.all_gather(hidden, 'tp', axis=0, tiled=True, axis_index_groups=[[0, 1...  1.98 us
    pallas_call x1, Pallas kernels, paired(): call(functools.partial(hess_near_kernel, factor, capacity), (S((wide, slo...  1.74 us
  transfers between devices with their start and end apart: 13, of which 6 were waited for; matrix products, arithmetic and copies ran while one was open for 0% of the time, Pallas kernels for 27%

profile of v6, /device:TPU:0, one launch (start us, length us, event | category | flops | bytes accessed | tf_op | source)
XLA Modules:
  0.0 29.7 jit_solution(1206602198886233374)
XLA Ops:
  0.6 0.5 %collective-permute-start = (bf16[256,896]{1,0:T(8,128)(2,1)}, bf16[256,896]{1,0:T(8,128)(2,1)S(1)}, u32[]{:S(2)}, u32[]{:S(2)}) collective-permute-start(bf16[256,896]{1,0:T(8,128)(2,1)} %tok_hbm.1), channel_id=1, source_target_pairs={{0,1},{1,0},{2,3},{3,2},{4,5},{5,4},{6,7},{7,6},{8,9},{9,8},{10,11... | collective-permute-start | bytes 1376264 | tf_op jit(solution)/shard_map/ppermute | solution.py:196
  1.1 1.4 %prepare.1 = (bf16[48,256]{1,0:T(8,128)(2,1)S(1)}, bf16[48,896]{1,0:T(8,128)(2,1)S(1)}, bf16[16,896]{1,0:T(8,128)(2,1)S(1)}, bf16[16,896]{1,0:T(8,128)(2,1)S(1)}, bf16[2,512,512]{2,1,0:T(8,128)(2,1)S(1)}) custom-call(s32[8,256]{1,0:T(8,128)} %bitcast.1, bf16[256,896]{1,0:T(8,128)(2,1)} %tok_hbm.1, bf16[1,3584,512]{2,1,0:T(8,128)(2,1)} %gate_hbm.3, ...), custom_call_target="tpu_custom_call" | custom-call | flops 36700160 | bytes 458752 | tf_op jit(solution)/shard_map/prepare/pallas_call | solution.py:211
  2.5 2.6 %collective-permute-start.4 = (bf16[16,896]{1,0:T(8,128)(2,1)S(1)}, bf16[16,896]{1,0:T(8,128)(2,1)S(1)}, u32[]{:S(2)}, u32[]{:S(2)}) collective-permute-start(bf16[16,896]{1,0:T(8,128)(2,1)S(1)} %get-tuple-element.25), channel_id=1, source_target_pairs={{0,4},{4,0},{8,12},{12,8},{16,20},{20,16},{24,28},{28,24},{1,5},{5... | collective-permute-start | bytes 86024 | tf_op jit(solution)/shard_map/ppermute | solution.py:218
  5.1 0.0 collective-permute-done.sib_ref
  5.1 0.2 select.1
  5.4 2.7 %collective-permute-start.1 = (bf16[16,1792]{1,0:T(8,128)(2,1)S(1)}, bf16[16,1792]{1,0:T(8,128)(2,1)S(1)}, u32[]{:S(2)}, u32[]{:S(2)}) collective-permute-start(bf16[16,1792]{1,0:T(8,128)(2,1)S(1)} %get-tuple-element.22), channel_id=1, source_target_pairs={{0,16},{1,29},{2,18},{3,31},{4,20},{5,25},{6,22},{7,27},{8,24},{9,... | collective-permute-start | bytes 172040 | tf_op jit(solution)/shard_map/ppermute | solution.py:200
  8.0 0.3 %collective-permute-start.2 = (bf16[16,1792]{1,0:T(8,128)(2,1)S(1)}, bf16[16,1792]{1,0:T(8,128)(2,1)S(1)}, u32[]{:S(2)}, u32[]{:S(2)}) collective-permute-start(bf16[16,1792]{1,0:T(8,128)(2,1)S(1)} %get-tuple-element.23), channel_id=1, source_target_pairs={{0,20},{1,25},{2,22},{3,27},{4,16},{5,29},{6,18},{7,31},{8,28},{9,... | collective-permute-start | bytes 172040 | tf_op jit(solution)/shard_map/ppermute | solution.py:200
  8.3 0.0 collective-permute-done.4
  8.3 1.5 %collective-permute-start.5 = (bf16[16,1792]{1,0:T(8,128)(2,1)S(1)}, bf16[16,1792]{1,0:T(8,128)(2,1)S(1)}, u32[]{:S(2)}, u32[]{:S(2)}) collective-permute-start(bf16[16,1792]{1,0:T(8,128)(2,1)S(1)} %constant_dynamic-update-slice_fusion), channel_id=1, source_target_pairs={{0,2},{1,3},{2,0},{3,1},{4,6},{5,7},{6,4},{7,5},{8,10},{9,11},{10,... | collective-permute-start | bytes 172040 | tf_op jit(solution)/shard_map/ppermute | solution.py:193
  9.9 1.6 %collective-permute-start.9 = (bf16[16,1792]{1,0:T(8,128)(2,1)S(1)}, bf16[16,1792]{1,0:T(8,128)(2,1)S(1)}, u32[]{:S(2)}, u32[]{:S(2)}) collective-permute-start(bf16[16,1792]{1,0:T(8,128)(2,1)S(1)} %get-tuple-element.26), channel_id=1, source_target_pairs={{0,8},{1,13},{2,10},{3,15},{4,12},{5,9},{6,14},{7,11},{8,0},{9,5},... | collective-permute-start | bytes 172040 | tf_op jit(solution)/shard_map/ppermute | solution.py:200
  11.5 0.4 %collective-permute-start.6 = (bf16[16,1792]{1,0:T(8,128)(2,1)S(1)}, bf16[16,1792]{1,0:T(8,128)(2,1)S(1)}, u32[]{:S(2)}, u32[]{:S(2)}) collective-permute-start(bf16[16,1792]{1,0:T(8,128)(2,1)S(1)} %get-tuple-element.26), channel_id=1, source_target_pairs={{0,10},{1,15},{2,8},{3,13},{4,14},{5,11},{6,12},{7,9},{8,2},{9,7},... | collective-permute-start | bytes 172040 | tf_op jit(solution)/shard_map/ppermute | solution.py:200
  11.9 0.2 collective-permute-done.1
  12.0 2.0 %collective-permute-done.2 = bf16[16,1792]{1,0:T(8,128)(2,1)S(1)} collective-permute-done((bf16[16,1792]{1,0:T(8,128)(2,1)S(1)}, bf16[16,1792]{1,0:T(8,128)(2,1)S(1)}, u32[]{:S(2)}, u32[]{:S(2)}) %collective-permute-start.2) | collective-permute-done | bytes 57376 | tf_op jit(solution)/shard_map/ppermute | solution.py:200
  14.0 1.6 %collective-permute-start.3 = (bf16[32,1792]{1,0:T(8,128)(2,1)S(1)}, bf16[32,1792]{1,0:T(8,128)(2,1)S(1)}, u32[]{:S(2)}, u32[]{:S(2)}) collective-permute-start(bf16[32,1792]{1,0:T(8,128)(2,1)S(1)} %pad_maximum_fusion.3), channel_id=1, source_target_pairs={{0,2},{1,3},{2,0},{3,1},{4,6},{5,7},{6,4},{7,5},{8,10},{9,11},{10,... | collective-permute-start | bytes 344072 | tf_op jit(solution)/shard_map/ppermute | solution.py:193
  15.7 0.1 collective-permute-start.10
  15.8 2.9 %load.1 = (bf16[2,1280,512]{2,1,0:T(8,128)(2,1)S(1)}, bf16[2,1792,512]{2,1,0:T(8,128)(2,1)S(1)}) custom-call(bf16[48,1792]{1,0:T(8,128)(2,1)S(1)} %pad_maximum_fusion.2.after_ref, bf16[1,3584,512]{2,1,0:T(8,128)(2,1)} %gate_hbm.3, bf16[1,3584,512]{2,1,0:T(8,128)(2,1)} %up_hbm.3), custom_call_target="tpu_custom_call" | custom-call | bytes 7340032 | tf_op jit(solution)/shard_map/load/pallas_call | solution.py:231
  18.7 0.0 collective-permute-done.6
  18.7 0.6 %collective-permute-start.8 = (bf16[32,1792]{1,0:T(8,128)(2,1)S(1)}, bf16[32,1792]{1,0:T(8,128)(2,1)S(1)}, u32[]{:S(2)}, u32[]{:S(2)}) collective-permute-start(bf16[32,1792]{1,0:T(8,128)(2,1)S(1)} %pad_maximum_fusion.4), channel_id=1, source_target_pairs={{0,1},{1,0},{2,3},{3,2},{4,5},{5,4},{6,7},{7,6},{8,9},{9,8},{10,11... | collective-permute-start | bytes 344072 | tf_op jit(solution)/shard_map/ppermute | solution.py:196
  19.3 0.2 collective-permute-done.3
  19.5 0.0 collective-permute-start.7
  19.6 0.0 collective-permute-done.10.sib_ref
  19.6 0.6 %near.1 = (f32[128,512]{1,0:T(8,128)S(1)}, f32[128,512]{1,0:T(8,128)S(1)}) custom-call(bf16[64,1792]{1,0:T(8,128)(2,1)S(1)} %pad_maximum_fusion.1.own_ref, bf16[64,1792]{1,0:T(8,128)(2,1)S(1)} %collective-permute-done.10.sib_ref, bf16[2,512,512]{2,1,0:T(8,128)(2,1)S(1)} %get-tuple-element.30.early_ref, bf16[2,1280,512]{2,1,0:T(8,128)(2,1)S(1)} %get-tuple-element.31.w_ref), custom_call_target="tpu_custom_call" | custom-call | flops 469762048 | bytes 3670016 | tf_op jit(solution)/shard_map/near/pallas_call | solution.py:239
  20.2 0.0 collective-permute-done.8
  20.2 0.6 %collective-permute-done.7 = bf16[32,1792]{1,0:T(8,128)(2,1)S(1)} collective-permute-done((bf16[32,1792]{1,0:T(8,128)(2,1)S(1)}, bf16[32,1792]{1,0:T(8,128)(2,1)S(1)}, u32[]{:S(2)}, u32[]{:S(2)}) %collective-permute-start.7) | collective-permute-done | bytes 114720 | tf_op jit(solution)/shard_map/ppermute | solution.py:196
  20.9 0.7 %far.1.h_ref = bf16[128,512]{1,0:T(8,128)(2,1)S(1)} custom-call(bf16[64,1792]{1,0:T(8,128)(2,1)S(1)} %constant_dynamic-update-slice_fusion.2.far_ref, bf16[64,1792]{1,0:T(8,128)(2,1)S(1)} %pad_maximum_fusion.diag_ref, bf16[2,1792,512]{2,1,0:T(8,128)(2,1)S(1)} %get-tuple-element.27.w_ref, f32[128,512]{1,0:T(8,128)S(1)} %get-tuple-element.32.g_ref, ...), custom_call_target="tpu_custom_call" | custom-call | flops 469762048 | bytes 3670016 | tf_op jit(solution)/shard_map/far/pallas_call | solution.py:243
  21.5 1.3 %collective-permute-start.11 = (bf16[128,512]{1,0:T(8,128)(2,1)S(1)}, bf16[128,512]{1,0:T(8,128)(2,1)S(1)}, u32[]{:S(2)}, u32[]{:S(2)}) collective-permute-start(bf16[128,512]{1,0:T(8,128)(2,1)S(1)} %far.1.h_ref), channel_id=1, source_target_pairs={{0,2},{1,3},{2,0},{3,1},{4,6},{5,7},{6,4},{7,5},{8,10},{9,11},{10,... | collective-permute-start | bytes 393224 | tf_op jit(solution)/shard_map/ppermute | solution.py:193
  22.9 2.0 %all_gather.3.sib_ref = bf16[256,512]{1,0:T(8,128)(2,1)S(1)} all-gather(bf16[128,512]{1,0:T(8,128)(2,1)S(1)} %far.1.h_ref), channel_id=1, replica_groups={{0,1},{2,3},{4,5},{6,7},{8,9},{10,11},{12,13},{14,15},{16,17},{18,19},{..., dimensions={0}, use_global_device_ids=true | all-gather | bytes 393216 | tf_op jit(solution)/shard_map/all_gather | solution.py:252
  24.8 1.7 %hess_near.1 = (bf16[512,128]{1,0:T(8,128)(2,1)S(1)}, bf16[1,128,512]{2,1,0:T(8,128)(2,1)}, f32[1,512,2048]{2,1,0:T(8,128)}) custom-call(bf16[128,512]{1,0:T(8,128)(2,1)S(1)} %far.1.h_ref, bf16[256,512]{1,0:T(8,128)(2,1)S(1)} %all_gather.3.sib_ref), custom_call_target="tpu_custom_call" | custom-call | flops 134217728 | bytes 2097152 | tf_op jit(solution)/shard_map/hess_near/pallas_call | solution.py:253
  26.6 0.6 %collective-permute-done.11.h_ref = bf16[128,512]{1,0:T(8,128)(2,1)S(1)} collective-permute-done((bf16[128,512]{1,0:T(8,128)(2,1)S(1)}, bf16[128,512]{1,0:T(8,128)(2,1)S(1)}, u32[]{:S(2)}, u32[]{:S(2)}) %collective-permute-start.11) | collective-permute-done | bytes 131104 | tf_op jit(solution)/shard_map/ppermute | solution.py:193
  27.2 1.2 %hess_2.1.hess_in = f32[1,512,2048]{2,1,0:T(8,128)} custom-call(bf16[512,128]{1,0:T(8,128)(2,1)S(1)} %get-tuple-element.35.flip_ref, bf16[128,512]{1,0:T(8,128)(2,1)S(1)} %collective-permute-done.11.h_ref, f32[1,512,2048]{2,1,0:T(8,128)} %get-tuple-element.37.hess_in), custom_call_target="tpu_custom_call", output_to_operand_aliasing={{}: (2, {})} | custom-call | flops 67108864 | bytes 1048576 | tf_op jit(solution)/shard_map/hess_2/pallas_call | solution.py:261
  28.3 0.2 collective-permute-done.12.h_ref
  28.5 1.2 %hess_3.1 = f32[1,512,2048]{2,1,0:T(8,128)} custom-call(bf16[512,128]{1,0:T(8,128)(2,1)S(1)} %get-tuple-element.35.flip_ref, bf16[128,512]{1,0:T(8,128)(2,1)S(1)} %collective-permute-done.12.h_ref, f32[1,512,2048]{2,1,0:T(8,128)} %hess_2.1.hess_in), custom_call_target="tpu_custom_call", output_to_operand_aliasing={{}: (2, {})} | custom-call | flops 67108864 | bytes 1048576 | tf_op jit(solution)/shard_map/hess_3/pallas_call | solution.py:261
  (12 shorter events, 0.1 us)
Async XLA Ops:
  0.6 4.5 %collective-permute-start = (bf16[256,896]{1,0:T(8,128)(2,1)}, bf16[256,896]{1,0:T(8,128)(2,1)S(1)}, u32[]{:S(2)}, u32[]{:S(2)}) collective-permute-start(bf16[256,896]{1,0:T(8,128)(2,1)} %tok_hbm.1), channel_id=1, source_target_pairs={{0,1},{1,0},{2,3},{3,2},{4,5},{5,4},{6,7},{7,6},{8,9},{9,8},{10,11... | collective-permute-start | bytes 1376264 | tf_op jit(solution)/shard_map/ppermute | solution.py:196
  2.5 5.8 %collective-permute-start.4 = (bf16[16,896]{1,0:T(8,128)(2,1)S(1)}, bf16[16,896]{1,0:T(8,128)(2,1)S(1)}, u32[]{:S(2)}, u32[]{:S(2)}) collective-permute-start(bf16[16,896]{1,0:T(8,128)(2,1)S(1)} %get-tuple-element.25), channel_id=1, source_target_pairs={{0,4},{4,0},{8,12},{12,8},{16,20},{20,16},{24,28},{28,24},{1,5},{5... | collective-permute-start | bytes 86024 | tf_op jit(solution)/shard_map/ppermute | solution.py:218
  5.4 6.7 %collective-permute-start.1 = (bf16[16,1792]{1,0:T(8,128)(2,1)S(1)}, bf16[16,1792]{1,0:T(8,128)(2,1)S(1)}, u32[]{:S(2)}, u32[]{:S(2)}) collective-permute-start(bf16[16,1792]{1,0:T(8,128)(2,1)S(1)} %get-tuple-element.22), channel_id=1, source_target_pairs={{0,16},{1,29},{2,18},{3,31},{4,20},{5,25},{6,22},{7,27},{8,24},{9,... | collective-permute-start | bytes 172040 | tf_op jit(solution)/shard_map/ppermute | solution.py:200
  8.0 6.0 %collective-permute-start.2 = (bf16[16,1792]{1,0:T(8,128)(2,1)S(1)}, bf16[16,1792]{1,0:T(8,128)(2,1)S(1)}, u32[]{:S(2)}, u32[]{:S(2)}) collective-permute-start(bf16[16,1792]{1,0:T(8,128)(2,1)S(1)} %get-tuple-element.23), channel_id=1, source_target_pairs={{0,20},{1,25},{2,22},{3,27},{4,16},{5,29},{6,18},{7,31},{8,28},{9,... | collective-permute-start | bytes 172040 | tf_op jit(solution)/shard_map/ppermute | solution.py:200
  8.3 10.4 %collective-permute-start.5 = (bf16[16,1792]{1,0:T(8,128)(2,1)S(1)}, bf16[16,1792]{1,0:T(8,128)(2,1)S(1)}, u32[]{:S(2)}, u32[]{:S(2)}) collective-permute-start(bf16[16,1792]{1,0:T(8,128)(2,1)S(1)} %constant_dynamic-update-slice_fusion), channel_id=1, source_target_pairs={{0,2},{1,3},{2,0},{3,1},{4,6},{5,7},{6,4},{7,5},{8,10},{9,11},{10,... | collective-permute-start | bytes 172040 | tf_op jit(solution)/shard_map/ppermute | solution.py:193
  9.9 5.8 %collective-permute-start.9 = (bf16[16,1792]{1,0:T(8,128)(2,1)S(1)}, bf16[16,1792]{1,0:T(8,128)(2,1)S(1)}, u32[]{:S(2)}, u32[]{:S(2)}) collective-permute-start(bf16[16,1792]{1,0:T(8,128)(2,1)S(1)} %get-tuple-element.26), channel_id=1, source_target_pairs={{0,8},{1,13},{2,10},{3,15},{4,12},{5,9},{6,14},{7,11},{8,0},{9,5},... | collective-permute-start | bytes 172040 | tf_op jit(solution)/shard_map/ppermute | solution.py:200
  11.5 7.2 %collective-permute-start.6 = (bf16[16,1792]{1,0:T(8,128)(2,1)S(1)}, bf16[16,1792]{1,0:T(8,128)(2,1)S(1)}, u32[]{:S(2)}, u32[]{:S(2)}) collective-permute-start(bf16[16,1792]{1,0:T(8,128)(2,1)S(1)} %get-tuple-element.26), channel_id=1, source_target_pairs={{0,10},{1,15},{2,8},{3,13},{4,14},{5,11},{6,12},{7,9},{8,2},{9,7},... | collective-permute-start | bytes 172040 | tf_op jit(solution)/shard_map/ppermute | solution.py:200
  14.0 5.5 %collective-permute-start.3 = (bf16[32,1792]{1,0:T(8,128)(2,1)S(1)}, bf16[32,1792]{1,0:T(8,128)(2,1)S(1)}, u32[]{:S(2)}, u32[]{:S(2)}) collective-permute-start(bf16[32,1792]{1,0:T(8,128)(2,1)S(1)} %pad_maximum_fusion.3), channel_id=1, source_target_pairs={{0,2},{1,3},{2,0},{3,1},{4,6},{5,7},{6,4},{7,5},{8,10},{9,11},{10,... | collective-permute-start | bytes 344072 | tf_op jit(solution)/shard_map/ppermute | solution.py:193
  15.7 3.9 %collective-permute-start.10 = (bf16[64,1792]{1,0:T(8,128)(2,1)S(1)}, bf16[64,1792]{1,0:T(8,128)(2,1)S(1)}, u32[]{:S(2)}, u32[]{:S(2)}) collective-permute-start(bf16[64,1792]{1,0:T(8,128)(2,1)S(1)} %pad_maximum_fusion.1.own_ref), channel_id=1, source_target_pairs={{0,1},{1,0},{2,3},{3,2},{4,5},{5,4},{6,7},{7,6},{8,9},{9,8},{10,11... | collective-permute-start | bytes 688136 | tf_op jit(solution)/shard_map/ppermute | solution.py:196
  18.7 1.5 %collective-permute-start.8 = (bf16[32,1792]{1,0:T(8,128)(2,1)S(1)}, bf16[32,1792]{1,0:T(8,128)(2,1)S(1)}, u32[]{:S(2)}, u32[]{:S(2)}) collective-permute-start(bf16[32,1792]{1,0:T(8,128)(2,1)S(1)} %pad_maximum_fusion.4), channel_id=1, source_target_pairs={{0,1},{1,0},{2,3},{3,2},{4,5},{5,4},{6,7},{7,6},{8,9},{9,8},{10,11... | collective-permute-start | bytes 344072 | tf_op jit(solution)/shard_map/ppermute | solution.py:196
  19.5 1.3 %collective-permute-start.7 = (bf16[32,1792]{1,0:T(8,128)(2,1)S(1)}, bf16[32,1792]{1,0:T(8,128)(2,1)S(1)}, u32[]{:S(2)}, u32[]{:S(2)}) collective-permute-start(bf16[32,1792]{1,0:T(8,128)(2,1)S(1)} %collective-permute-done.3), channel_id=1, source_target_pairs={{0,1},{1,0},{2,3},{3,2},{4,5},{5,4},{6,7},{7,6},{8,9},{9,8},{10,11... | collective-permute-start | bytes 344072 | tf_op jit(solution)/shard_map/ppermute | solution.py:196
  21.5 5.6 %collective-permute-start.11 = (bf16[128,512]{1,0:T(8,128)(2,1)S(1)}, bf16[128,512]{1,0:T(8,128)(2,1)S(1)}, u32[]{:S(2)}, u32[]{:S(2)}) collective-permute-start(bf16[128,512]{1,0:T(8,128)(2,1)S(1)} %far.1.h_ref), channel_id=1, source_target_pairs={{0,2},{1,3},{2,0},{3,1},{4,6},{5,7},{6,4},{7,5},{8,10},{9,11},{10,... | collective-permute-start | bytes 393224 | tf_op jit(solution)/shard_map/ppermute | solution.py:193
  27.2 1.3 %collective-permute-start.12 = (bf16[128,512]{1,0:T(8,128)(2,1)S(1)}, bf16[128,512]{1,0:T(8,128)(2,1)S(1)}, u32[]{:S(2)}, u32[]{:S(2)}) collective-permute-start(bf16[128,512]{1,0:T(8,128)(2,1)S(1)} %collective-permute-done.11.h_ref), channel_id=1, source_target_pairs={{0,1},{1,0},{2,3},{3,2},{4,5},{5,4},{6,7},{7,6},{8,9},{9,8},{10,11... | collective-permute-start | bytes 393224 | tf_op jit(solution)/shard_map/ppermute | solution.py:196

commit v7 on v6

--- a/solution.py
+++ b/solution.py
@@ -17,8 +17,8 @@
 LIMIT = 40 * 1024 * 1024
 
 
-DISTANCE = ((4, 5, 2), (7, 6, 3))
-EARLY_ROWS = 512
+DISTANCE = ((5, 6, 2), (4, 7, 3))
+EARLY_ROWS = 384
 PARTS = ((1, 2), (0,), (3,))
 ORDER = sum(PARTS, ())
 

time: 29.9 us -> 29.8 us (level)
  waiting for transfers between devices: 3.73 us -> 2.63 us
  starting transfers between devices: 13.2 us -> 14.2 us
    ppermute x4, starting transfers between devices: 4.97 us -> 6.06 us  [spread(): return lax.ppermute(x, ('ep', 'tp'), pairs)]
    ppermute x4, waiting for transfers between devices: 2.12 us -> 1.21 us  [spread(): return lax.ppermute(x, ('ep', 'tp'), pairs)]
  transfers between devices with their start and end apart: 13 -> 13, of which waited for: 6 -> 5; matrix products, arithmetic and copies ran while one was open for 0% -> 0% of each run, Pallas kernels for 27% -> 27%
where the time goes in v7:
time: 29.8 us; the launch traced here: 29.6 us
  starting transfers between devices  14.2 us (48%)
  Pallas kernels  9.93 us (33%)
  waiting for transfers between devices  2.63 us (9%)
  blocking collectives  1.98 us (7%)
  between operations  0.76 us (3%)
    ppermute x4, starting transfers between devices, spread(): return lax.ppermute(x, ('ep', 'tp'), pairs)  6.06 us
    ppermute x3, starting transfers between devices, chips(): return lax.ppermute(x, 'tp', [(i, i ^ 2) for i in range(4)])  4.28 us
    pallas_call x1, Pallas kernels, paired(): call(load_kernel, (rest_w, half_w), [VMEM] + [HBM] * 2, (VMEM,) * 2, (D((...  2.98 us
    ppermute x1, starting transfers between devices, paired(): side = lax.ppermute(side, 'ep', [(e, e ^ 1) for e in range(8)])  2.59 us
    pallas_call x2, Pallas kernels, other(): call(functools.partial(hess_far_kernel, factor, which), hess_shape, [VMEM...  2.35 us
    all_gather x1, blocking collectives, paired(): lax.all_gather(hidden, 'tp', axis=0, tiled=True, axis_index_groups=[[0, 1...  1.98 us
    pallas_call x1, Pallas kernels, paired(): call(functools.partial(hess_near_kernel, factor, capacity), (S((wide, slo...  1.74 us
    pallas_call x1, Pallas kernels, paired(): call(functools.partial(prepare_kernel, capacity), (S((3 * capacity, tok_r...  1.3 us
  transfers between devices with their start and end apart: 13, of which 5 were waited for; matrix products, arithmetic and copies ran while one was open for 0% of the time, Pallas kernels for 27%

profile of v7, /device:TPU:0, one launch (start us, length us, event | category | flops | bytes accessed | tf_op | source)
XLA Modules:
  0.0 29.6 jit_solution(3627225543634003479)
XLA Ops:
  0.6 0.5 %collective-permute-start = (bf16[256,896]{1,0:T(8,128)(2,1)}, bf16[256,896]{1,0:T(8,128)(2,1)S(1)}, u32[]{:S(2)}, u32[]{:S(2)}) collective-permute-start(bf16[256,896]{1,0:T(8,128)(2,1)} %tok_hbm.1), channel_id=1, source_target_pairs={{0,1},{1,0},{2,3},{3,2},{4,5},{5,4},{6,7},{7,6},{8,9},{9,8},{10,11... | collective-permute-start | bytes 1376264 | tf_op jit(solution)/shard_map/ppermute | solution.py:196
  1.1 1.3 %prepare.1 = (bf16[48,256]{1,0:T(8,128)(2,1)S(1)}, bf16[48,896]{1,0:T(8,128)(2,1)S(1)}, bf16[16,896]{1,0:T(8,128)(2,1)S(1)}, bf16[16,896]{1,0:T(8,128)(2,1)S(1)}, bf16[2,384,512]{2,1,0:T(8,128)(2,1)S(1)}) custom-call(s32[8,256]{1,0:T(8,128)} %bitcast.1, bf16[256,896]{1,0:T(8,128)(2,1)} %tok_hbm.1, bf16[1,3584,512]{2,1,0:T(8,128)(2,1)} %gate_hbm.3, ...), custom_call_target="tpu_custom_call" | custom-call | flops 36700160 | bytes 458752 | tf_op jit(solution)/shard_map/prepare/pallas_call | solution.py:211
  2.5 2.6 %collective-permute-start.4 = (bf16[16,896]{1,0:T(8,128)(2,1)S(1)}, bf16[16,896]{1,0:T(8,128)(2,1)S(1)}, u32[]{:S(2)}, u32[]{:S(2)}) collective-permute-start(bf16[16,896]{1,0:T(8,128)(2,1)S(1)} %get-tuple-element.25), channel_id=1, source_target_pairs={{0,4},{4,0},{8,12},{12,8},{16,20},{20,16},{24,28},{28,24},{1,5},{5... | collective-permute-start | bytes 86024 | tf_op jit(solution)/shard_map/ppermute | solution.py:218
  5.1 0.0 collective-permute-done.sib_ref
  5.1 0.2 select.1
  5.3 2.7 %collective-permute-start.1 = (bf16[16,1792]{1,0:T(8,128)(2,1)S(1)}, bf16[16,1792]{1,0:T(8,128)(2,1)S(1)}, u32[]{:S(2)}, u32[]{:S(2)}) collective-permute-start(bf16[16,1792]{1,0:T(8,128)(2,1)S(1)} %get-tuple-element.22), channel_id=1, source_target_pairs={{0,20},{1,17},{2,22},{3,19},{4,16},{5,21},{6,18},{7,23},{8,28},{9,... | collective-permute-start | bytes 172040 | tf_op jit(solution)/shard_map/ppermute | solution.py:200
  8.0 1.3 %collective-permute-start.2 = (bf16[16,1792]{1,0:T(8,128)(2,1)S(1)}, bf16[16,1792]{1,0:T(8,128)(2,1)S(1)}, u32[]{:S(2)}, u32[]{:S(2)}) collective-permute-start(bf16[16,1792]{1,0:T(8,128)(2,1)S(1)} %get-tuple-element.23), channel_id=1, source_target_pairs={{0,24},{1,29},{2,26},{3,31},{4,28},{5,25},{6,30},{7,27},{8,16},{9,... | collective-permute-start | bytes 172040 | tf_op jit(solution)/shard_map/ppermute | solution.py:200
  9.3 0.0 collective-permute-done.4
  9.3 1.5 %collective-permute-start.5 = (bf16[16,1792]{1,0:T(8,128)(2,1)S(1)}, bf16[16,1792]{1,0:T(8,128)(2,1)S(1)}, u32[]{:S(2)}, u32[]{:S(2)}) collective-permute-start(bf16[16,1792]{1,0:T(8,128)(2,1)S(1)} %constant_dynamic-update-slice_fusion), channel_id=1, source_target_pairs={{0,2},{1,3},{2,0},{3,1},{4,6},{5,7},{6,4},{7,5},{8,10},{9,11},{10,... | collective-permute-start | bytes 172040 | tf_op jit(solution)/shard_map/ppermute | solution.py:193
  10.9 0.2 collective-permute-start.9
  11.1 1.8 %collective-permute-start.6 = (bf16[16,1792]{1,0:T(8,128)(2,1)S(1)}, bf16[16,1792]{1,0:T(8,128)(2,1)S(1)}, u32[]{:S(2)}, u32[]{:S(2)}) collective-permute-start(bf16[16,1792]{1,0:T(8,128)(2,1)S(1)} %get-tuple-element.26), channel_id=1, source_target_pairs={{0,10},{1,15},{2,8},{3,13},{4,14},{5,11},{6,12},{7,9},{8,2},{9,7},... | collective-permute-start | bytes 172040 | tf_op jit(solution)/shard_map/ppermute | solution.py:200
  12.9 0.0 collective-permute-done.1
  12.9 1.2 %collective-permute-done.2 = bf16[16,1792]{1,0:T(8,128)(2,1)S(1)} collective-permute-done((bf16[16,1792]{1,0:T(8,128)(2,1)S(1)}, bf16[16,1792]{1,0:T(8,128)(2,1)S(1)}, u32[]{:S(2)}, u32[]{:S(2)}) %collective-permute-start.2) | collective-permute-done | bytes 57376 | tf_op jit(solution)/shard_map/ppermute | solution.py:200
  14.1 1.6 %collective-permute-start.3 = (bf16[32,1792]{1,0:T(8,128)(2,1)S(1)}, bf16[32,1792]{1,0:T(8,128)(2,1)S(1)}, u32[]{:S(2)}, u32[]{:S(2)}) collective-permute-start(bf16[32,1792]{1,0:T(8,128)(2,1)S(1)} %pad_maximum_fusion.3), channel_id=1, source_target_pairs={{0,2},{1,3},{2,0},{3,1},{4,6},{5,7},{6,4},{7,5},{8,10},{9,11},{10,... | collective-permute-start | bytes 344072 | tf_op jit(solution)/shard_map/ppermute | solution.py:193
  15.7 0.1 collective-permute-start.10
  15.8 3.0 %load.1 = (bf16[2,1408,512]{2,1,0:T(8,128)(2,1)S(1)}, bf16[2,1792,512]{2,1,0:T(8,128)(2,1)S(1)}) custom-call(bf16[48,1792]{1,0:T(8,128)(2,1)S(1)} %pad_maximum_fusion.2.after_ref, bf16[1,3584,512]{2,1,0:T(8,128)(2,1)} %gate_hbm.3, bf16[1,3584,512]{2,1,0:T(8,128)(2,1)} %up_hbm.3), custom_call_target="tpu_custom_call" | custom-call | bytes 7340032 | tf_op jit(solution)/shard_map/load/pallas_call | solution.py:231
  18.8 0.0 collective-permute-done.6
  18.8 0.6 %collective-permute-start.8 = (bf16[32,1792]{1,0:T(8,128)(2,1)S(1)}, bf16[32,1792]{1,0:T(8,128)(2,1)S(1)}, u32[]{:S(2)}, u32[]{:S(2)}) collective-permute-start(bf16[32,1792]{1,0:T(8,128)(2,1)S(1)} %pad_maximum_fusion.4), channel_id=1, source_target_pairs={{0,1},{1,0},{2,3},{3,2},{4,5},{5,4},{6,7},{7,6},{8,9},{9,8},{10,11... | collective-permute-start | bytes 344072 | tf_op jit(solution)/shard_map/ppermute | solution.py:196
  19.4 0.0 collective-permute-done.3
  19.4 0.1 collective-permute-start.7
  19.5 0.0 collective-permute-done.10.sib_ref
  19.5 0.7 %near.1 = (f32[128,512]{1,0:T(8,128)S(1)}, f32[128,512]{1,0:T(8,128)S(1)}) custom-call(bf16[64,1792]{1,0:T(8,128)(2,1)S(1)} %pad_maximum_fusion.1.own_ref, bf16[64,1792]{1,0:T(8,128)(2,1)S(1)} %collective-permute-done.10.sib_ref, bf16[2,384,512]{2,1,0:T(8,128)(2,1)S(1)} %get-tuple-element.30.early_ref, bf16[2,1408,512]{2,1,0:T(8,128)(2,1)S(1)} %get-tuple-element.31.w_ref), custom_call_target="tpu_custom_call" | custom-call | flops 469762048 | bytes 3670016 | tf_op jit(solution)/shard_map/near/pallas_call | solution.py:239
  20.2 0.1 collective-permute-done.8
  20.4 0.4 %collective-permute-done.7 = bf16[32,1792]{1,0:T(8,128)(2,1)S(1)} collective-permute-done((bf16[32,1792]{1,0:T(8,128)(2,1)S(1)}, bf16[32,1792]{1,0:T(8,128)(2,1)S(1)}, u32[]{:S(2)}, u32[]{:S(2)}) %collective-permute-start.7) | collective-permute-done | bytes 114720 | tf_op jit(solution)/shard_map/ppermute | solution.py:196
  20.8 0.7 %far.1.h_ref = bf16[128,512]{1,0:T(8,128)(2,1)S(1)} custom-call(bf16[64,1792]{1,0:T(8,128)(2,1)S(1)} %constant_dynamic-update-slice_fusion.2.far_ref, bf16[64,1792]{1,0:T(8,128)(2,1)S(1)} %pad_maximum_fusion.diag_ref, bf16[2,1792,512]{2,1,0:T(8,128)(2,1)S(1)} %get-tuple-element.27.w_ref, f32[128,512]{1,0:T(8,128)S(1)} %get-tuple-element.32.g_ref, ...), custom_call_target="tpu_custom_call" | custom-call | flops 469762048 | bytes 3670016 | tf_op jit(solution)/shard_map/far/pallas_call | solution.py:243
  21.4 1.2 %collective-permute-start.11 = (bf16[128,512]{1,0:T(8,128)(2,1)S(1)}, bf16[128,512]{1,0:T(8,128)(2,1)S(1)}, u32[]{:S(2)}, u32[]{:S(2)}) collective-permute-start(bf16[128,512]{1,0:T(8,128)(2,1)S(1)} %far.1.h_ref), channel_id=1, source_target_pairs={{0,2},{1,3},{2,0},{3,1},{4,6},{5,7},{6,4},{7,5},{8,10},{9,11},{10,... | collective-permute-start | bytes 393224 | tf_op jit(solution)/shard_map/ppermute | solution.py:193
  22.6 2.0 %all_gather.3.sib_ref = bf16[256,512]{1,0:T(8,128)(2,1)S(1)} all-gather(bf16[128,512]{1,0:T(8,128)(2,1)S(1)} %far.1.h_ref), channel_id=1, replica_groups={{0,1},{2,3},{4,5},{6,7},{8,9},{10,11},{12,13},{14,15},{16,17},{18,19},{..., dimensions={0}, use_global_device_ids=true | all-gather | bytes 393216 | tf_op jit(solution)/shard_map/all_gather | solution.py:252
  24.5 1.7 %hess_near.1 = (bf16[512,128]{1,0:T(8,128)(2,1)S(1)}, bf16[1,128,512]{2,1,0:T(8,128)(2,1)}, f32[1,512,2048]{2,1,0:T(8,128)}) custom-call(bf16[128,512]{1,0:T(8,128)(2,1)S(1)} %far.1.h_ref, bf16[256,512]{1,0:T(8,128)(2,1)S(1)} %all_gather.3.sib_ref), custom_call_target="tpu_custom_call" | custom-call | flops 134217728 | bytes 2097152 | tf_op jit(solution)/shard_map/hess_near/pallas_call | solution.py:253
  26.3 0.8 %collective-permute-done.11.h_ref = bf16[128,512]{1,0:T(8,128)(2,1)S(1)} collective-permute-done((bf16[128,512]{1,0:T(8,128)(2,1)S(1)}, bf16[128,512]{1,0:T(8,128)(2,1)S(1)}, u32[]{:S(2)}, u32[]{:S(2)}) %collective-permute-start.11) | collective-permute-done | bytes 131104 | tf_op jit(solution)/shard_map/ppermute | solution.py:193
  27.0 1.2 %hess_2.1.hess_in = f32[1,512,2048]{2,1,0:T(8,128)} custom-call(bf16[512,128]{1,0:T(8,128)(2,1)S(1)} %get-tuple-element.35.flip_ref, bf16[128,512]{1,0:T(8,128)(2,1)S(1)} %collective-permute-done.11.h_ref, f32[1,512,2048]{2,1,0:T(8,128)} %get-tuple-element.37.hess_in), custom_call_target="tpu_custom_call", output_to_operand_aliasing={{}: (2, {})} | custom-call | flops 67108864 | bytes 1048576 | tf_op jit(solution)/shard_map/hess_2/pallas_call | solution.py:261
  28.2 0.2 collective-permute-done.12.h_ref
  28.4 1.2 %hess_3.1 = f32[1,512,2048]{2,1,0:T(8,128)} custom-call(bf16[512,128]{1,0:T(8,128)(2,1)S(1)} %get-tuple-element.35.flip_ref, bf16[128,512]{1,0:T(8,128)(2,1)S(1)} %collective-permute-done.12.h_ref, f32[1,512,2048]{2,1,0:T(8,128)} %hess_2.1.hess_in), custom_call_target="tpu_custom_call", output_to_operand_aliasing={{}: (2, {})} | custom-call | flops 67108864 | bytes 1048576 | tf_op jit(solution)/shard_map/hess_3/pallas_call | solution.py:261
  (12 shorter events, 0.1 us)
Async XLA Ops:
  0.6 4.4 %collective-permute-start = (bf16[256,896]{1,0:T(8,128)(2,1)}, bf16[256,896]{1,0:T(8,128)(2,1)S(1)}, u32[]{:S(2)}, u32[]{:S(2)}) collective-permute-start(bf16[256,896]{1,0:T(8,128)(2,1)} %tok_hbm.1), channel_id=1, source_target_pairs={{0,1},{1,0},{2,3},{3,2},{4,5},{5,4},{6,7},{7,6},{8,9},{9,8},{10,11... | collective-permute-start | bytes 1376264 | tf_op jit(solution)/shard_map/ppermute | solution.py:196
  2.5 6.9 %collective-permute-start.4 = (bf16[16,896]{1,0:T(8,128)(2,1)S(1)}, bf16[16,896]{1,0:T(8,128)(2,1)S(1)}, u32[]{:S(2)}, u32[]{:S(2)}) collective-permute-start(bf16[16,896]{1,0:T(8,128)(2,1)S(1)} %get-tuple-element.25), channel_id=1, source_target_pairs={{0,4},{4,0},{8,12},{12,8},{16,20},{20,16},{24,28},{28,24},{1,5},{5... | collective-permute-start | bytes 86024 | tf_op jit(solution)/shard_map/ppermute | solution.py:218
  5.3 7.6 %collective-permute-start.1 = (bf16[16,1792]{1,0:T(8,128)(2,1)S(1)}, bf16[16,1792]{1,0:T(8,128)(2,1)S(1)}, u32[]{:S(2)}, u32[]{:S(2)}) collective-permute-start(bf16[16,1792]{1,0:T(8,128)(2,1)S(1)} %get-tuple-element.22), channel_id=1, source_target_pairs={{0,20},{1,17},{2,22},{3,19},{4,16},{5,21},{6,18},{7,23},{8,28},{9,... | collective-permute-start | bytes 172040 | tf_op jit(solution)/shard_map/ppermute | solution.py:200
  8.0 6.1 %collective-permute-start.2 = (bf16[16,1792]{1,0:T(8,128)(2,1)S(1)}, bf16[16,1792]{1,0:T(8,128)(2,1)S(1)}, u32[]{:S(2)}, u32[]{:S(2)}) collective-permute-start(bf16[16,1792]{1,0:T(8,128)(2,1)S(1)} %get-tuple-element.23), channel_id=1, source_target_pairs={{0,24},{1,29},{2,26},{3,31},{4,28},{5,25},{6,30},{7,27},{8,16},{9,... | collective-permute-start | bytes 172040 | tf_op jit(solution)/shard_map/ppermute | solution.py:200
  9.3 9.5 %collective-permute-start.5 = (bf16[16,1792]{1,0:T(8,128)(2,1)S(1)}, bf16[16,1792]{1,0:T(8,128)(2,1)S(1)}, u32[]{:S(2)}, u32[]{:S(2)}) collective-permute-start(bf16[16,1792]{1,0:T(8,128)(2,1)S(1)} %constant_dynamic-update-slice_fusion), channel_id=1, source_target_pairs={{0,2},{1,3},{2,0},{3,1},{4,6},{5,7},{6,4},{7,5},{8,10},{9,11},{10,... | collective-permute-start | bytes 172040 | tf_op jit(solution)/shard_map/ppermute | solution.py:193
  10.9 4.8 %collective-permute-start.9 = (bf16[16,1792]{1,0:T(8,128)(2,1)S(1)}, bf16[16,1792]{1,0:T(8,128)(2,1)S(1)}, u32[]{:S(2)}, u32[]{:S(2)}) collective-permute-start(bf16[16,1792]{1,0:T(8,128)(2,1)S(1)} %get-tuple-element.26), channel_id=1, source_target_pairs={{0,8},{1,13},{2,10},{3,15},{4,12},{5,9},{6,14},{7,11},{8,0},{9,5},... | collective-permute-start | bytes 172040 | tf_op jit(solution)/shard_map/ppermute | solution.py:200
  11.1 7.7 %collective-permute-start.6 = (bf16[16,1792]{1,0:T(8,128)(2,1)S(1)}, bf16[16,1792]{1,0:T(8,128)(2,1)S(1)}, u32[]{:S(2)}, u32[]{:S(2)}) collective-permute-start(bf16[16,1792]{1,0:T(8,128)(2,1)S(1)} %get-tuple-element.26), channel_id=1, source_target_pairs={{0,10},{1,15},{2,8},{3,13},{4,14},{5,11},{6,12},{7,9},{8,2},{9,7},... | collective-permute-start | bytes 172040 | tf_op jit(solution)/shard_map/ppermute | solution.py:200
  14.1 5.3 %collective-permute-start.3 = (bf16[32,1792]{1,0:T(8,128)(2,1)S(1)}, bf16[32,1792]{1,0:T(8,128)(2,1)S(1)}, u32[]{:S(2)}, u32[]{:S(2)}) collective-permute-start(bf16[32,1792]{1,0:T(8,128)(2,1)S(1)} %pad_maximum_fusion.3), channel_id=1, source_target_pairs={{0,2},{1,3},{2,0},{3,1},{4,6},{5,7},{6,4},{7,5},{8,10},{9,11},{10,... | collective-permute-start | bytes 344072 | tf_op jit(solution)/shard_map/ppermute | solution.py:193
  15.7 3.8 %collective-permute-start.10 = (bf16[64,1792]{1,0:T(8,128)(2,1)S(1)}, bf16[64,1792]{1,0:T(8,128)(2,1)S(1)}, u32[]{:S(2)}, u32[]{:S(2)}) collective-permute-start(bf16[64,1792]{1,0:T(8,128)(2,1)S(1)} %pad_maximum_fusion.1.own_ref), channel_id=1, source_target_pairs={{0,1},{1,0},{2,3},{3,2},{4,5},{5,4},{6,7},{7,6},{8,9},{9,8},{10,11... | collective-permute-start | bytes 688136 | tf_op jit(solution)/shard_map/ppermute | solution.py:196
  18.8 1.5 %collective-permute-start.8 = (bf16[32,1792]{1,0:T(8,128)(2,1)S(1)}, bf16[32,1792]{1,0:T(8,128)(2,1)S(1)}, u32[]{:S(2)}, u32[]{:S(2)}) collective-permute-start(bf16[32,1792]{1,0:T(8,128)(2,1)S(1)} %pad_maximum_fusion.4), channel_id=1, source_target_pairs={{0,1},{1,0},{2,3},{3,2},{4,5},{5,4},{6,7},{7,6},{8,9},{9,8},{10,11... | collective-permute-start | bytes 344072 | tf_op jit(solution)/shard_map/ppermute | solution.py:196
  19.4 1.3 %collective-permute-start.7 = (bf16[32,1792]{1,0:T(8,128)(2,1)S(1)}, bf16[32,1792]{1,0:T(8,128)(2,1)S(1)}, u32[]{:S(2)}, u32[]{:S(2)}) collective-permute-start(bf16[32,1792]{1,0:T(8,128)(2,1)S(1)} %collective-permute-done.3), channel_id=1, source_target_pairs={{0,1},{1,0},{2,3},{3,2},{4,5},{5,4},{6,7},{7,6},{8,9},{9,8},{10,11... | collective-permute-start | bytes 344072 | tf_op jit(solution)/shard_map/ppermute | solution.py:196
  21.4 5.6 %collective-permute-start.11 = (bf16[128,512]{1,0:T(8,128)(2,1)S(1)}, bf16[128,512]{1,0:T(8,128)(2,1)S(1)}, u32[]{:S(2)}, u32[]{:S(2)}) collective-permute-start(bf16[128,512]{1,0:T(8,128)(2,1)S(1)} %far.1.h_ref), channel_id=1, source_target_pairs={{0,2},{1,3},{2,0},{3,1},{4,6},{5,7},{6,4},{7,5},{8,10},{9,11},{10,... | collective-permute-start | bytes 393224 | tf_op jit(solution)/shard_map/ppermute | solution.py:193
  27.0 1.3 %collective-permute-start.12 = (bf16[128,512]{1,0:T(8,128)(2,1)S(1)}, bf16[128,512]{1,0:T(8,128)(2,1)S(1)}, u32[]{:S(2)}, u32[]{:S(2)}) collective-permute-start(bf16[128,512]{1,0:T(8,128)(2,1)S(1)} %collective-permute-done.11.h_ref), channel_id=1, source_target_pairs={{0,1},{1,0},{2,3},{3,2},{4,5},{5,4},{6,7},{7,6},{8,9},{9,8},{10,11... | collective-permute-start | bytes 393224 | tf_op jit(solution)/shard_map/ppermute | solution.py:196
